TPU v7x, 32 devices: a whole 2x2x4 slice. The times are simulated.
32 devices in a mesh: groups: 2 (over x), outer: 2 (over core), inner: 8 (over z, y).
Axes of the slice: x: 2, y: 2, z: 4, core: 2. Of those that a mesh axis runs over, the one named last changes fastest.
Arguments:
- hidden_states: bfloat16 [768, 3584], P(('groups', 'outer', 'inner')), parts along dimension 0, may hold values from -6 to 6
- expert_ids: int32 [768, 8], P(('groups', 'outer', 'inner')), parts along dimension 0, may hold values from 0 to 31, all different within a row; in each aligned block of 24 rows (0 to 23, 24 to 47, ...) at most 12 rows name the same one
- gate_scores: float32 [768, 8], P(('groups', 'outer', 'inner')), parts along dimension 0, may hold values from -6 to 6
- w_gate: bfloat16 [32, 3584, 1024], P('inner', None, 'outer'), may hold values from -0.09375 to 0.09375
- w_up: bfloat16 [32, 3584, 1024], P('inner', None, 'outer'), may hold values from -0.09375 to 0.09375
- w_down: bfloat16 [32, 1024, 3584], P('inner', 'outer'), may hold values from -0.1875 to 0.1875
Outputs:
- moe_out: bfloat16 [768, 3584], P(('groups', 'outer', 'inner')), parts along dimension 0
There are 2 independent parts, one for each index of `groups`. A program takes and returns all parts, laid end to end along the dimension named above; an argument that names none is the same for every part. Nothing has to cross between parts.
Inputs may be any that keep to these rules, and one draw needn't show every extreme that they name: `expert_ids`: each row names 8 different experts; in each aligned block of 24 rows (the tokens of one device) no expert is named by more than 12 rows, a bound that some block reaches.
All inputs are finite; a program needn't handle non-finite values.
Results may differ from a plain program's by a relative error of at most 0.012.
Values may be sent and summed in bfloat16 or wider, within the bound.
No kernel may reach another device: no remote copies, remote signals or barrier semaphores. Data moves between devices by JAX's collectives and lax.ppermute only.
A program may use at most 128 MiB of HBM per device.

v0:
```python
import jax
import jax.numpy as jnp
from jax import lax
from jax.sharding import PartitionSpec as P

MOST = 12


def slot_index(choices, experts):
    flat = choices.reshape(-1)
    onehot = (flat[:, None] == jnp.arange(experts, dtype=jnp.int32)).astype(jnp.int32)
    ranking = jnp.sum((jnp.cumsum(onehot, axis=0) - onehot) * onehot, axis=1)
    return (flat * MOST + ranking).reshape(choices.shape)


def placement_table(positions, width_all):
    table = positions[..., None] == jnp.arange(width_all, dtype=jnp.int32)
    return jnp.sum(table.astype(jnp.float32), axis=1).astype(jnp.bfloat16)


def on_device(hidden_states, expert_ids, gate_scores, w_gate, w_up, w_down):
    local_experts = w_gate.shape[0]
    inner_size = lax.axis_size("inner")
    experts = local_experts * inner_size
    width_all = experts * MOST
    model_width = hidden_states.shape[1]
    positions = slot_index(expert_ids, experts)
    table = placement_table(positions, width_all)
    outgoing = jnp.einsum(
        "tc,td->cd", table, hidden_states, preferred_element_type=jnp.float32
    ).astype(jnp.bfloat16)
    arrived = lax.all_to_all(outgoing, "inner", split_axis=0, concat_axis=0, tiled=True)
    received = lax.all_gather(arrived[None], "outer", axis=0, tiled=True)
    rows = received.reshape(2, inner_size, local_experts, MOST, model_width)
    gate = jnp.einsum("ailmd,ldf->ailmf", rows, w_gate, preferred_element_type=jnp.float32)
    upper = jnp.einsum("ailmd,ldf->ailmf", rows, w_up, preferred_element_type=jnp.float32)
    hidden = (jax.nn.silu(gate) * upper).astype(jnp.bfloat16)
    partial_value = jnp.einsum(
        "ailmf,lfd->ailmd", hidden, w_down, preferred_element_type=jnp.float32
    ).astype(jnp.bfloat16)
    partial_value = partial_value.reshape(2, width_all, model_width)
    returned = lax.all_to_all(partial_value, "inner", split_axis=1, concat_axis=1, tiled=True)
    summed = lax.psum_scatter(returned, "outer", scatter_dimension=0, tiled=True).astype(
        jnp.float32
    )
    routed = summed[0].astype(jnp.bfloat16)
    picked = routed[positions].astype(jnp.float32)
    sigmoid_vals = jax.nn.sigmoid(gate_scores)
    weights = 2.5 * sigmoid_vals / jnp.sum(sigmoid_vals, axis=1, keepdims=True)
    return jnp.sum(weights[..., None] * picked, axis=1).astype(jnp.bfloat16)


def solution(mesh):
    return jax.shard_map(
        on_device,
        mesh=mesh,
        in_specs=(
            P(("groups", "outer", "inner"), None),
            P(("groups", "outer", "inner"), None),
            P(("groups", "outer", "inner"), None),
            P("inner", None, "outer"),
            P("inner", None, "outer"),
            P("inner", "outer", None),
        ),
        out_specs=P(("groups", "outer", "inner"), None),
        check_vma=False,
    )
```

profile of v0, /device:TPU:0, one launch (start us, length us, event | category | flops | bytes accessed | tf_op | source)
XLA Modules:
  0.0 312.9 jit_solution(15627706954709975343)
XLA Ops:
  6.5 0.0 copy-start
  6.5 0.0 all-gather.2.cloned.1.call-start
  6.5 0.8 copy.38
  7.3 0.1 eq.35
  7.5 0.6 reduce-window.6
  8.0 0.2 slice_reduce_fusion
  8.3 0.1 bitcast_bitcast_fusion
  8.4 0.1 reduce_sum.40
  8.5 0.2 convert_reduce_fusion
  8.7 0.0 copy-done
  8.7 0.9 convolution_convert_fusion
  9.6 69.8 %all_to_all.14 = bf16[8,48,3584]{2,1,0:T(8,128)(2,1)} all-to-all(bf16[8,48,3584]{2,1,0:T(8,128)(2,1)S(1)} %bitcast.66), channel_id=1, replica_groups=mesh['groups'=2,'outer'=2,'inner'=8] {'inner'}, dimensions={0} | all-to-all | bytes 5505024 | tf_op jit(solution)/shard_map/all_to_all | solution.py:32
  79.4 0.0 all-gather.2.cloned.1.call-update
  79.4 0.0 reduce-scatter.2.cloned.1.call-start
  79.5 14.3 %all-gather.2.cloned.1.call-done = bf16[2,384,3584]{2,1,0:T(8,128)(2,1)} async-done(((bf16[1,384,3584]{2,1,0:T(8,128)(2,1)}), bf16[2,384,3584]{2,1,0:T(8,128)(2,1)}) %all-gather.2.cloned.1.call-update) | async-done | bytes 5505040 | tf_op jit(solution)/shard_map/all_gather | solution.py:33
  93.8 22.5 %copy.42 = bf16[2,384,3584]{2,0,1:T(2,128)(2,1)S(1)} copy(bf16[2,384,3584]{2,1,0:T(8,128)(2,1)} %all-gather.2.cloned.1.call-done) | data formatting | bytes 11010048 | tf_op jit(solution)/shard_map/all_gather | solution.py:33
  116.3 7.3 %fusion.2 = f32[4,2,8,12,512]{4,3,2,1,0:T(8,128)S(1)} fusion(bf16[4,3584,512]{2,1,0:T(8,128)(2,1)} %param.10, bf16[2,8,4,12,3584]{4,0,3,2,1:T(2,128)(2,1)S(1)} %bitcast.67), kind=kOutput, calls=%fused_computation.3 | convolution fusion | flops 2818572288 | bytes 21757952 | tf_op jit(solution)/shard_map/ailmd,ldf->ailmf/dot_general | solution.py:36
  123.6 9.4 %fusion.15 = bf16[2,8,4,12,512]{4,3,1,0,2:T(8,128)(2,1)S(1)} fusion(f32[4,2,8,12,512]{4,3,2,1,0:T(8,128)S(1)} %fusion.2, bf16[4,3584,512]{2,1,0:T(8,128)(2,1)} %param.9, bf16[2,8,4,12,3584]{4,0,3,2,1:T(2,128)(2,1)S(1)} %bitcast.68), kind=kOutput, calls=%fused_computation.15 | convolution fusion | flops 2820931584 | bytes 22544384 | tf_op jit(solution)/shard_map/ailmd,ldf->ailmf/dot_general | solution.py:35
  133.0 9.6 %fusion.11 = bf16[2,8,4,12,3584]{4,3,1,0,2:T(8,128)(2,1)S(1)} fusion(bf16[2,8,4,12,512]{4,3,1,0,2:T(8,128)(2,1)S(1)} %fusion.15, bf16[4,512,3584]{2,1,0:T(8,128)(2,1)} %param.11), kind=kOutput, calls=%fused_computation.10 | convolution fusion | flops 2821324800 | bytes 20971520 | tf_op jit(solution)/shard_map/ailmf,lfd->ailmd/dot_general | solution.py:38
  142.6 13.9 %copy.45 = bf16[2,8,4,12,3584]{4,0,3,2,1:T(2,128)(2,1)S(1)} copy(bf16[2,8,4,12,3584]{4,3,1,0,2:T(8,128)(2,1)S(1)} %fusion.11) | data formatting | bytes 11010048 | tf_op jit(solution)/shard_map/convert_element_type | solution.py:40
  156.5 127.3 %all_to_all.15 = bf16[2,384,3584]{2,0,1:T(2,128)(2,1)S(1)} all-to-all(bf16[2,384,3584]{2,0,1:T(2,128)(2,1)S(1)} %bitcast.64), channel_id=1, replica_groups=mesh['groups'=2,'outer'=2,'inner'=8] {'inner'}, dimensions={1} | all-to-all | bytes 11010048 | tf_op jit(solution)/shard_map/all_to_all | solution.py:42
  283.8 2.9 copy.46
  286.7 0.0 copy-start.2
  286.7 0.0 reduce-scatter.2.cloned.1.call-update
  286.7 0.1 reshape.40
  286.8 0.6 copy-done.2
  287.4 0.1 copy.37
  287.5 11.9 %reduce-scatter.2.cloned.1.call-done = bf16[1,384,3584]{2,1,0:T(8,128)(2,1)} async-done(((bf16[2,384,3584]{2,1,0:T(8,128)(2,1)}), bf16[1,384,3584]{2,1,0:T(8,128)(2,1)}) %reduce-scatter.2.cloned.1.call-update) | async-done | bytes 2752528 | tf_op jit(solution)/shard_map/reduce_scatter | solution.py:43
  299.4 0.0 copy-start.1
  299.4 5.0 %gather_fusion = bf16[192,3584]{1,0:T(8,128)(2,1)S(1)} fusion(bf16[384,3584]{1,0:T(8,128)(2,1)} %bitcast.63, s32[1024]{0:T(1024)S(1)} %pad_clamp_fusion), kind=kCustom, calls=%fused_computation | custom fusion | bytes 2753280 | tf_op jit(solution)/shard_map/gather | solution.py:47
  304.4 1.7 fusion.14
  306.1 0.0 copy-done.1
  (9 shorter events, 0.1 us)
Async XLA Ops:
  6.5 2.1 copy-start
  6.5 87.3 %all-gather.2.cloned.1.call-start = ((), (), s32[]{:S(2)}) async-start(), calls=%async_computation.3 | async-start | bytes 8257536 | tf_op jit(solution)/shard_map/all_gather | solution.py:33
  79.4 220.0 %reduce-scatter.2.cloned.1.call-start = ((), (), s32[]{:S(2)}) async-start(), calls=%async_computation.4 | async-start | bytes 8257536 | tf_op jit(solution)/shard_map/reduce_scatter | solution.py:43
  286.7 0.7 copy-start.2
  299.4 6.7 %copy-start.1 = (bf16[24,3584]{1,0:T(8,128)(2,1)S(1)}, bf16[24,3584]{1,0:T(8,128)(2,1)}, u32[]{:S(2)}) copy-start(bf16[24,3584]{1,0:T(8,128)(2,1)} %param.6) | copy-start | bytes 516100
Sparse Core Ops, SparseCore 0:
  79.6 14.2 all-gather.1
  286.8 12.5 reduce-scatter.1
where the time goes:
time: 313 us
  blocking collectives  197 us (63%)
  local copies, waits for them, and re-layouts  46.1 us (15%)
  matrix products  27.2 us (9%)
  waiting for transfers between devices  26.3 us (8%)
  between operations  13.5 us (4%)
    all_to_all x1, blocking collectives, on_device(): lax.all_to_all(partial_value, 'inner', split_axis=1, concat_axis=1, tiled...  127 us
    all_to_all x1, blocking collectives, on_device(): lax.all_to_all(outgoing, 'inner', split_axis=0, concat_axis=0, tiled=True)  69.8 us
    all_gather x1, local copies, waits for them, and re-layouts, on_device(): received = lax.all_gather(arrived[None], 'outer', axis=0, tiled=True)  22.5 us
    all_gather x1, waiting for transfers between devices, on_device(): received = lax.all_gather(arrived[None], 'outer', axis=0, tiled=True)  14.3 us
    convert_element_type x1, local copies, waits for them, and re-layouts, on_device(): partial_value = jnp.einsum('ailmf,lfd->ailmd', hidden, w_down, preferred_...  13.9 us
    reduce_scatter x1, waiting for transfers between devices, on_device(): lax.psum_scatter(returned, 'outer', scatter_dimension=0, tiled=True)  11.9 us
    dot_general x1, matrix products, on_device(): jnp.einsum('ailmf,lfd->ailmd', hidden, w_down, preferred_element_type=jnp...  9.6 us
    dot_general x1, matrix products, on_device(): jnp.einsum('ailmd,ldf->ailmf', rows, w_gate, preferred_element_type=jnp.f...  9.41 us
  transfers between devices with their start and end apart: 2, of which 2 were waited for; matrix products, arithmetic and copies ran while one was open for 0% of the time, Pallas kernels for 0%

commit v1 on v0

v1 whole, which is shorter than its diff:
```python
import functools

import jax
import jax.numpy as jnp
from jax import lax
from jax.experimental import pallas as pl
from jax.experimental.pallas import tpu as pltpu
from jax.sharding import PartitionSpec as P

LANES = 128
SPLIT = 2
VMEM_LIMIT = 60 * 1024 * 1024


def routing_columns(expert_ids, gate_scores, experts):
    sigmoid_vals = jax.nn.sigmoid(gate_scores)
    weights = 2.5 * sigmoid_vals / jnp.sum(sigmoid_vals, axis=1, keepdims=True)
    named = expert_ids[..., None] == jnp.arange(experts, dtype=jnp.int32)
    dense = jnp.sum(jnp.where(named, weights[..., None], 0.0), axis=1)
    high = lax.reduce_precision(dense, 8, 7)
    both = jnp.concatenate([high, dense - high], axis=1).astype(jnp.bfloat16)
    return jnp.pad(both, ((0, 0), (0, LANES - 2 * experts)))


def up_kernel(experts, local_experts, index_ref, rows_ref, gate_w_ref, up_w_ref, out_ref):
    model_width = gate_w_ref.shape[1]
    x = rows_ref[:, :model_width]
    gate = jnp.dot(x, gate_w_ref[0], preferred_element_type=jnp.float32)
    upper = jnp.dot(x, up_w_ref[0], preferred_element_type=jnp.float32)
    expert = index_ref[0] * local_experts + pl.program_id(0)
    columns = rows_ref[:, model_width:].astype(jnp.float32)
    lane = lax.broadcasted_iota(jnp.int32, columns.shape, 1)
    mine = (lane == expert) | (lane == expert + experts)
    weight = jnp.sum(jnp.where(mine, columns, 0.0), axis=1, keepdims=True)
    hidden = gate / (1.0 + jnp.exp(-gate)) * upper * weight
    out_ref[...] = hidden.astype(jnp.bfloat16)


def down_kernel(hidden_ref, down_w_ref, out_ref):
    block = down_w_ref[...]
    block = block.reshape(block.shape[0] * block.shape[1], block.shape[2])
    out_ref[...] = jnp.dot(
        hidden_ref[...], block, preferred_element_type=jnp.float32
    ).astype(jnp.bfloat16)


def expert_rows(rows, w_gate, w_up, w_down, inner_index, experts):
    local_experts, model_width, width = w_gate.shape
    count = rows.shape[0]
    part = width // SPLIT
    hidden = pl.pallas_call(
        functools.partial(up_kernel, experts, local_experts),
        grid=(local_experts, SPLIT),
        in_specs=[
            pl.BlockSpec(memory_space=pltpu.SMEM),
            pl.BlockSpec((count, rows.shape[1]), lambda l, s: (0, 0)),
            pl.BlockSpec((1, model_width, part), lambda l, s: (l, 0, s)),
            pl.BlockSpec((1, model_width, part), lambda l, s: (l, 0, s)),
        ],
        out_specs=pl.BlockSpec((count, part), lambda l, s: (0, l * SPLIT + s)),
        out_shape=jax.ShapeDtypeStruct((count, local_experts * width), jnp.bfloat16),
        compiler_params=pltpu.CompilerParams(vmem_limit_bytes=VMEM_LIMIT),
        name="gate_up",
    )(inner_index, rows, w_gate, w_up)
    tile = 512
    return pl.pallas_call(
        down_kernel,
        grid=(model_width // tile,),
        in_specs=[
            pl.BlockSpec(hidden.shape, lambda n: (0, 0)),
            pl.BlockSpec((local_experts, width, tile), lambda n: (0, 0, n)),
        ],
        out_specs=pl.BlockSpec((count, tile), lambda n: (0, n)),
        out_shape=jax.ShapeDtypeStruct((count, model_width), jnp.bfloat16),
        compiler_params=pltpu.CompilerParams(vmem_limit_bytes=VMEM_LIMIT),
        name="down",
    )(hidden, w_down)


def swap_core(value):
    return lax.ppermute(value, "outer", [(0, 1), (1, 0)])


def swap_inner(value, bit):
    return lax.ppermute(value, "inner", [(i, i ^ bit) for i in range(8)])


def add(a, b):
    return (a.astype(jnp.float32) + b.astype(jnp.float32)).astype(jnp.bfloat16)


def on_device(hidden_states, expert_ids, gate_scores, w_gate, w_up, w_down):
    local_experts = w_gate.shape[0]
    inner_size = lax.axis_size("inner")
    experts = local_experts * inner_size
    count = hidden_states.shape[0]
    inner_index = lax.axis_index("inner").astype(jnp.int32).reshape(1)
    own = jnp.concatenate(
        [hidden_states, routing_columns(expert_ids, gate_scores, experts)], axis=1
    )
    compute = functools.partial(
        expert_rows, w_gate=w_gate, w_up=w_up, w_down=w_down, inner_index=inner_index,
        experts=experts,
    )
    if inner_size != 8 or lax.axis_size("outer") != 2:
        everyone = lax.all_gather(own, ("outer", "inner"), axis=0, tiled=True)
        return lax.psum_scatter(
            compute(everyone), ("outer", "inner"), scatter_dimension=0, tiled=True
        )

    column = [own] + [swap_inner(own, bit) for bit in (2, 4, 6)]
    partner = [swap_inner(block, 1) for block in column]
    near, far = jnp.concatenate(column), jnp.concatenate(partner)
    everyone = jnp.concatenate([near, swap_core(near), far, swap_core(far)])
    outs = compute(everyone)
    group = 4 * count
    near_sum, near_other, far_sum, far_other = (
        outs[i * group : (i + 1) * group] for i in range(4)
    )
    far_sum = add(far_sum, swap_core(far_other))
    near_sum = add(near_sum, swap_core(near_other))
    total = None
    for step in (3, 2, 1, 0):
        part = slice(step * count, (step + 1) * count)
        arrived = swap_inner(far_sum[part], 1)
        if step:
            term = swap_inner(add(near_sum[part], arrived), 2 * step).astype(jnp.float32)
        else:
            term = near_sum[part].astype(jnp.float32) + arrived.astype(jnp.float32)
        total = term if total is None else total + term
    return total.astype(jnp.bfloat16)


def solution(mesh):
    return jax.shard_map(
        on_device,
        mesh=mesh,
        in_specs=(
            P(("groups", "outer", "inner"), None),
            P(("groups", "outer", "inner"), None),
            P(("groups", "outer", "inner"), None),
            P("inner", None, "outer"),
            P("inner", None, "outer"),
            P("inner", "outer", None),
        ),
        out_specs=P(("groups", "outer", "inner"), None),
        check_vma=False,
    )
```

time: 313 us -> 112 us (0.36)
  blocking collectives: 197 us -> 0 us
  local copies, waits for them, and re-layouts: 46.1 us -> 5.24 us
  Pallas kernels: 0 us -> 30.5 us
  matrix products: 27.2 us -> 0 us
  waiting for transfers between devices: 26.3 us -> 49.9 us
  starting transfers between devices: 0.04 us -> 20.5 us
  between operations: 13.5 us -> 0.13 us
    all_to_all x2 -> x0, blocking collectives: 197 us -> none  [the longest x1 127 us: on_device(): lax.all_to_all(partial_value, 'inner', split_axis=1, concat_axis=1, tiled...]
    ppermute x0 -> x18, waiting for transfers between devices: none -> 49.9 us  [the longest x14 45.3 us: swap_inner(): return lax.ppermute(value, 'inner', [(i, i ^ bit) for i in range(8)])]
    pallas_call x0 -> x2, Pallas kernels: none -> 30.5 us  [the longest x1 18.5 us: expert_rows(): pl.pallas_call(functools.partial(up_kernel, experts, local_experts), grid...]
    dot_general x4 -> x0, matrix products: 27.2 us -> none  [the longest x1 9.6 us: on_device(): jnp.einsum('ailmf,lfd->ailmd', hidden, w_down, preferred_element_type=jnp...]
    all_gather x1 -> x0, local copies, waits for them, and re-layouts: 22.5 us -> none  [on_device(): received = lax.all_gather(arrived[None], 'outer', axis=0, tiled=True)]
    ppermute x0 -> x18, starting transfers between devices: none -> 20.5 us  [the longest x14 19.8 us: swap_inner(): return lax.ppermute(value, 'inner', [(i, i ^ bit) for i in range(8)])]
    all_gather x1 -> x0, waiting for transfers between devices: 14.3 us -> none  [on_device(): received = lax.all_gather(arrived[None], 'outer', axis=0, tiled=True)]
    convert_element_type x1 -> x0, local copies, waits for them, and re-layouts: 13.9 us -> none  [on_device(): partial_value = jnp.einsum('ailmf,lfd->ailmd', hidden, w_down, preferred_...]
  transfers between devices with their start and end apart: 2 -> 18, of which waited for: 2 -> 13; matrix products, arithmetic and copies ran while one was open for 0% -> 2% of each run, Pallas kernels for 0% -> 0%
where the time goes in v1:
time: 112 us
  waiting for transfers between devices  49.9 us (45%)
  Pallas kernels  30.5 us (27%)
  starting transfers between devices  20.5 us (18%)
  other arithmetic  5.59 us (5%)
  local copies, waits for them, and re-layouts  5.24 us (5%)
    ppermute x14, waiting for transfers between devices, swap_inner(): return lax.ppermute(value, 'inner', [(i, i ^ bit) for i in range(8)])  45.3 us
    ppermute x14, starting transfers between devices, swap_inner(): return lax.ppermute(value, 'inner', [(i, i ^ bit) for i in range(8)])  19.8 us
    pallas_call x1, Pallas kernels, expert_rows(): pl.pallas_call(functools.partial(up_kernel, experts, local_experts), grid...  18.5 us
    pallas_call x1, Pallas kernels, expert_rows(): pl.pallas_call(down_kernel, grid=(model_width // tile,), in_specs=[pl.Blo...  12.1 us
    ppermute x4, waiting for transfers between devices, swap_core(): return lax.ppermute(value, 'outer', [(0, 1), (1, 0)])  4.59 us
    unnamed x13, local copies, waits for them, and re-layouts  3.49 us
  transfers between devices with their start and end apart: 18, of which 13 were waited for; matrix products, arithmetic and copies ran while one was open for 2% of the time, Pallas kernels for 0%

profile of v1, /device:TPU:0, one launch (start us, length us, event | category | flops | bytes accessed | tf_op | source)
XLA Modules:
  0.0 111.9 jit_solution(2938079243319357116)
XLA Ops:
  0.0 0.7 fusion.4
  0.7 0.7 multiply_divide_fusion
  1.4 0.1 copy.10
  1.5 0.8 copy.9
  2.3 0.1 select_reduce_fusion
  2.4 0.1 fusion.3
  2.5 1.6 %pad_maximum_fusion.2 = (bf16[24,3712]{1,0:T(8,128)(2,1)}, bf16[384,3712]{1,0:T(8,128)(2,1)S(1)}) fusion(bf16[24,128]{1,0:T(8,128)(2,1)S(1)} %fusion.3, bf16[24,3584]{1,0:T(8,128)(2,1)} %param.6), kind=kLoop, calls=%fused_computation.8 | loop fusion | flops 356351 | bytes 534528 | tf_op jit(solution)/shard_map/concatenate | solution.py:98
  4.1 3.0 %collective-permute-start = (bf16[24,3712]{1,0:T(8,128)(2,1)}, bf16[24,3712]{1,0:T(8,128)(2,1)S(1)}, u32[]{:S(2)}, u32[]{:S(2)}) collective-permute-start(bf16[24,3712]{1,0:T(8,128)(2,1)} %get-tuple-element.16), channel_id=1, source_target_pairs={{0,2},{1,3},{2,0},{3,1},{4,6},{5,7},{6,4},{7,5},{8,10},{9,11},{10,... | collective-permute-start | bytes 534536 | tf_op jit(solution)/shard_map/ppermute | solution.py:85
  7.1 2.6 %collective-permute-start.1 = (bf16[24,3712]{1,0:T(8,128)(2,1)}, bf16[24,3712]{1,0:T(8,128)(2,1)S(1)}, u32[]{:S(2)}, u32[]{:S(2)}) collective-permute-start(bf16[24,3712]{1,0:T(8,128)(2,1)} %get-tuple-element.16), channel_id=1, source_target_pairs={{0,4},{1,5},{2,6},{3,7},{4,0},{5,1},{6,2},{7,3},{8,12},{9,13},{10,... | collective-permute-start | bytes 534536 | tf_op jit(solution)/shard_map/ppermute | solution.py:85
  9.7 1.7 %collective-permute-start.4 = (bf16[24,3712]{1,0:T(8,128)(2,1)}, bf16[24,3712]{1,0:T(8,128)(2,1)S(1)}, u32[]{:S(2)}, u32[]{:S(2)}) collective-permute-start(bf16[24,3712]{1,0:T(8,128)(2,1)} %get-tuple-element.16), channel_id=1, source_target_pairs={{0,1},{1,0},{2,3},{3,2},{4,5},{5,4},{6,7},{7,6},{8,9},{9,8},{10,11... | collective-permute-start | bytes 534536 | tf_op jit(solution)/shard_map/ppermute | solution.py:85
  11.4 3.3 %collective-permute-done = bf16[24,3712]{1,0:T(8,128)(2,1)S(1)} collective-permute-done((bf16[24,3712]{1,0:T(8,128)(2,1)}, bf16[24,3712]{1,0:T(8,128)(2,1)S(1)}, u32[]{:S(2)}, u32[]{:S(2)}) %collective-permute-start) | collective-permute-done | bytes 178208 | tf_op jit(solution)/shard_map/ppermute | solution.py:85
  14.7 8.6 %collective-permute-done.1 = bf16[24,3712]{1,0:T(8,128)(2,1)S(1)} collective-permute-done((bf16[24,3712]{1,0:T(8,128)(2,1)}, bf16[24,3712]{1,0:T(8,128)(2,1)S(1)}, u32[]{:S(2)}, u32[]{:S(2)}) %collective-permute-start.1) | collective-permute-done | bytes 178208 | tf_op jit(solution)/shard_map/ppermute | solution.py:85
  23.3 1.1 pad_maximum_fusion
  24.4 0.1 collective-permute-start.3
  24.4 1.6 %collective-permute-start.5 = (bf16[24,3712]{1,0:T(8,128)(2,1)S(1)}, bf16[24,3712]{1,0:T(8,128)(2,1)S(1)}, u32[]{:S(2)}, u32[]{:S(2)}) collective-permute-start(bf16[24,3712]{1,0:T(8,128)(2,1)S(1)} %collective-permute-done), channel_id=1, source_target_pairs={{0,1},{1,0},{2,3},{3,2},{4,5},{5,4},{6,7},{7,6},{8,9},{9,8},{10,11... | collective-permute-start | bytes 534536 | tf_op jit(solution)/shard_map/ppermute | solution.py:85
  26.0 0.5 collective-permute-start.6
  26.5 1.6 %collective-permute-start.7 = (bf16[24,3712]{1,0:T(8,128)(2,1)}, bf16[24,3712]{1,0:T(8,128)(2,1)S(1)}, u32[]{:S(2)}, u32[]{:S(2)}) collective-permute-start(bf16[24,3712]{1,0:T(8,128)(2,1)} %collective-permute-done.2), channel_id=1, source_target_pairs={{0,1},{1,0},{2,3},{3,2},{4,5},{5,4},{6,7},{7,6},{8,9},{9,8},{10,11... | collective-permute-start | bytes 534536 | tf_op jit(solution)/shard_map/ppermute | solution.py:85
  28.1 1.0 constant_dynamic-update-slice_fusion.6
  29.1 2.7 %collective-permute-done.5 = bf16[24,3712]{1,0:T(8,128)(2,1)S(1)} collective-permute-done((bf16[24,3712]{1,0:T(8,128)(2,1)S(1)}, bf16[24,3712]{1,0:T(8,128)(2,1)S(1)}, u32[]{:S(2)}, u32[]{:S(2)}) %collective-permute-start.5) | collective-permute-done | bytes 178208 | tf_op jit(solution)/shard_map/ppermute | solution.py:85
  31.8 3.8 %collective-permute-done.6 = bf16[24,3712]{1,0:T(8,128)(2,1)S(1)} collective-permute-done((bf16[24,3712]{1,0:T(8,128)(2,1)S(1)}, bf16[24,3712]{1,0:T(8,128)(2,1)S(1)}, u32[]{:S(2)}, u32[]{:S(2)}) %collective-permute-start.6) | collective-permute-done | bytes 178208 | tf_op jit(solution)/shard_map/ppermute | solution.py:85
  35.6 3.4 %collective-permute-done.7 = bf16[24,3712]{1,0:T(8,128)(2,1)S(1)} collective-permute-done((bf16[24,3712]{1,0:T(8,128)(2,1)}, bf16[24,3712]{1,0:T(8,128)(2,1)S(1)}, u32[]{:S(2)}, u32[]{:S(2)}) %collective-permute-start.7) | collective-permute-done | bytes 178208 | tf_op jit(solution)/shard_map/ppermute | solution.py:85
  39.1 0.1 collective-permute-start.8
  39.1 0.1 constant_dynamic-update-slice_fusion.5
  39.3 2.0 %collective-permute-done.8 = bf16[96,3712]{1,0:T(8,128)(2,1)S(1)} collective-permute-done((bf16[96,3712]{1,0:T(8,128)(2,1)S(1)}, bf16[96,3712]{1,0:T(8,128)(2,1)S(1)}, u32[]{:S(2)}, u32[]{:S(2)}) %collective-permute-start.8) | collective-permute-done | bytes 712736 | tf_op jit(solution)/shard_map/ppermute | solution.py:81
  41.3 0.1 constant_dynamic-update-slice_fusion.rows_ref
  41.4 1.6 %copy-done.1 = bf16[384,3712]{1,0:T(8,128)(2,1)} copy-done((bf16[384,3712]{1,0:T(8,128)(2,1)}, bf16[384,3712]{1,0:T(8,128)(2,1)S(1)}, u32[]{:S(2)}) %copy-start.1) | copy-done | bytes 2850840
  42.9 18.5 %gate_up.1.hidden_ref = bf16[384,2048]{1,0:T(8,128)(2,1)} custom-call(s32[1]{0:T(128)} %bitcast.index_ref, bf16[384,3712]{1,0:T(8,128)(2,1)} %copy-done.1, bf16[4,3584,512]{2,1,0:T(8,128)(2,1)} %gate_w_ref.1, bf16[4,3584,512]{2,1,0:T(8,128)(2,1)} %up_w_ref.1), custom_call_target="tpu_custom_call" | custom-call | tf_op jit(solution)/shard_map/gate_up/pallas_call | solution.py:51
  61.4 12.1 %down.1 = bf16[384,3584]{1,0:T(8,128)(2,1)} custom-call(bf16[384,2048]{1,0:T(8,128)(2,1)} %gate_up.1.hidden_ref, bf16[4,512,3584]{2,1,0:T(8,128)(2,1)} %down_w_ref.1), custom_call_target="tpu_custom_call" | custom-call | tf_op jit(solution)/shard_map/down/pallas_call | solution.py:66
  73.5 1.5 %fusion.5 = (bf16[96,3584]{1,0:T(8,128)(2,1)S(1)}, bf16[96,3584]{1,0:T(8,128)(2,1)S(1)}) fusion(bf16[384,3584]{1,0:T(8,128)(2,1)} %down.1), kind=kLoop, calls=%fused_computation.31 | loop fusion | bytes 2752512 | tf_op jit(solution)/shard_map/slice | solution.py:118
  75.0 0.2 collective-permute-start.10
  75.2 0.4 collective-permute-start.9
  75.6 1.6 %collective-permute-done.10 = bf16[96,3584]{1,0:T(8,128)(2,1)S(1)} collective-permute-done((bf16[96,3584]{1,0:T(8,128)(2,1)S(1)}, bf16[96,3584]{1,0:T(8,128)(2,1)S(1)}, u32[]{:S(2)}, u32[]{:S(2)}) %collective-permute-start.10) | collective-permute-done | bytes 688160 | tf_op jit(solution)/shard_map/ppermute | solution.py:81
  77.2 1.0 collective-permute-done.9
  78.2 0.3 add_convert_fusion.1
  78.6 1.6 %collective-permute-start.11 = (bf16[24,3584]{1,0:T(8,128)(2,1)S(1)}, bf16[24,3584]{1,0:T(8,128)(2,1)S(1)}, u32[]{:S(2)}, u32[]{:S(2)}) collective-permute-start(bf16[24,3584]{1,0:T(8,128)(2,1)S(1)} %get-tuple-element.12), channel_id=1, source_target_pairs={{0,1},{1,0},{2,3},{3,2},{4,5},{5,4},{6,7},{7,6},{8,9},{9,8},{10,11... | collective-permute-start | bytes 516104 | tf_op jit(solution)/shard_map/ppermute | solution.py:85
  80.2 0.5 collective-permute-start.13
  80.7 1.5 %collective-permute-start.15 = (bf16[24,3584]{1,0:T(8,128)(2,1)S(1)}, bf16[24,3584]{1,0:T(8,128)(2,1)S(1)}, u32[]{:S(2)}, u32[]{:S(2)}) collective-permute-start(bf16[24,3584]{1,0:T(8,128)(2,1)S(1)} %get-tuple-element.14), channel_id=1, source_target_pairs={{0,1},{1,0},{2,3},{3,2},{4,5},{5,4},{6,7},{7,6},{8,9},{9,8},{10,11... | collective-permute-start | bytes 516104 | tf_op jit(solution)/shard_map/ppermute | solution.py:85
  82.2 0.5 collective-permute-start.17
  82.7 3.2 %collective-permute-done.11 = bf16[24,3584]{1,0:T(8,128)(2,1)S(1)} collective-permute-done((bf16[24,3584]{1,0:T(8,128)(2,1)S(1)}, bf16[24,3584]{1,0:T(8,128)(2,1)S(1)}, u32[]{:S(2)}, u32[]{:S(2)}) %collective-permute-start.11) | collective-permute-done | bytes 172064 | tf_op jit(solution)/shard_map/ppermute | solution.py:85
  85.9 3.7 %collective-permute-done.13 = bf16[24,3584]{1,0:T(8,128)(2,1)S(1)} collective-permute-done((bf16[24,3584]{1,0:T(8,128)(2,1)S(1)}, bf16[24,3584]{1,0:T(8,128)(2,1)S(1)}, u32[]{:S(2)}, u32[]{:S(2)}) %collective-permute-start.13) | collective-permute-done | bytes 172064 | tf_op jit(solution)/shard_map/ppermute | solution.py:85
  89.6 3.7 %collective-permute-done.15 = bf16[24,3584]{1,0:T(8,128)(2,1)S(1)} collective-permute-done((bf16[24,3584]{1,0:T(8,128)(2,1)S(1)}, bf16[24,3584]{1,0:T(8,128)(2,1)S(1)}, u32[]{:S(2)}, u32[]{:S(2)}) %collective-permute-start.15) | collective-permute-done | bytes 172064 | tf_op jit(solution)/shard_map/ppermute | solution.py:85
  93.3 0.1 add_convert_fusion.5
  93.4 2.5 %collective-permute-start.12 = (bf16[24,3584]{1,0:T(8,128)(2,1)S(1)}, bf16[24,3584]{1,0:T(8,128)(2,1)S(1)}, u32[]{:S(2)}, u32[]{:S(2)}) collective-permute-start(bf16[24,3584]{1,0:T(8,128)(2,1)S(1)} %get-tuple-element.9), channel_id=1, source_target_pairs={{0,6},{1,7},{2,4},{3,5},{4,2},{5,3},{6,0},{7,1},{8,14},{9,15},{10,... | collective-permute-start | bytes 516104 | tf_op jit(solution)/shard_map/ppermute | solution.py:85
  95.9 2.1 %collective-permute-start.14 = (bf16[24,3584]{1,0:T(8,128)(2,1)S(1)}, bf16[24,3584]{1,0:T(8,128)(2,1)S(1)}, u32[]{:S(2)}, u32[]{:S(2)}) collective-permute-start(bf16[24,3584]{1,0:T(8,128)(2,1)S(1)} %get-tuple-element.11), channel_id=1, source_target_pairs={{0,4},{1,5},{2,6},{3,7},{4,0},{5,1},{6,2},{7,3},{8,12},{9,13},{10,... | collective-permute-start | bytes 516104 | tf_op jit(solution)/shard_map/ppermute | solution.py:85
  98.0 0.1 collective-permute-start.16
  98.1 4.2 %collective-permute-done.12 = bf16[24,3584]{1,0:T(8,128)(2,1)S(1)} collective-permute-done((bf16[24,3584]{1,0:T(8,128)(2,1)S(1)}, bf16[24,3584]{1,0:T(8,128)(2,1)S(1)}, u32[]{:S(2)}, u32[]{:S(2)}) %collective-permute-start.12) | collective-permute-done | bytes 172064 | tf_op jit(solution)/shard_map/ppermute | solution.py:85
  102.3 8.8 %collective-permute-done.14 = bf16[24,3584]{1,0:T(8,128)(2,1)S(1)} collective-permute-done((bf16[24,3584]{1,0:T(8,128)(2,1)S(1)}, bf16[24,3584]{1,0:T(8,128)(2,1)S(1)}, u32[]{:S(2)}, u32[]{:S(2)}) %collective-permute-start.14) | collective-permute-done | bytes 172064 | tf_op jit(solution)/shard_map/ppermute | solution.py:85
  111.1 0.8 add_convert_fusion.2
  (18 shorter events, 0.3 us)
Async XLA Ops:
  4.1 10.6 %collective-permute-start = (bf16[24,3712]{1,0:T(8,128)(2,1)}, bf16[24,3712]{1,0:T(8,128)(2,1)S(1)}, u32[]{:S(2)}, u32[]{:S(2)}) collective-permute-start(bf16[24,3712]{1,0:T(8,128)(2,1)} %get-tuple-element.16), channel_id=1, source_target_pairs={{0,2},{1,3},{2,0},{3,1},{4,6},{5,7},{6,4},{7,5},{8,10},{9,11},{10,... | collective-permute-start | bytes 534536 | tf_op jit(solution)/shard_map/ppermute | solution.py:85
  7.1 16.2 %collective-permute-start.1 = (bf16[24,3712]{1,0:T(8,128)(2,1)}, bf16[24,3712]{1,0:T(8,128)(2,1)S(1)}, u32[]{:S(2)}, u32[]{:S(2)}) collective-permute-start(bf16[24,3712]{1,0:T(8,128)(2,1)} %get-tuple-element.16), channel_id=1, source_target_pairs={{0,4},{1,5},{2,6},{3,7},{4,0},{5,1},{6,2},{7,3},{8,12},{9,13},{10,... | collective-permute-start | bytes 534536 | tf_op jit(solution)/shard_map/ppermute | solution.py:85
  9.7 13.6 %collective-permute-start.2 = (bf16[24,3712]{1,0:T(8,128)(2,1)}, bf16[24,3712]{1,0:T(8,128)(2,1)}, u32[]{:S(2)}, u32[]{:S(2)}) collective-permute-start(bf16[24,3712]{1,0:T(8,128)(2,1)} %get-tuple-element.16), channel_id=1, source_target_pairs={{0,6},{1,7},{2,4},{3,5},{4,2},{5,3},{6,0},{7,1},{8,14},{9,15},{10,... | collective-permute-start | bytes 534536 | tf_op jit(solution)/shard_map/ppermute | solution.py:85
  9.7 19.4 %collective-permute-start.4 = (bf16[24,3712]{1,0:T(8,128)(2,1)}, bf16[24,3712]{1,0:T(8,128)(2,1)S(1)}, u32[]{:S(2)}, u32[]{:S(2)}) collective-permute-start(bf16[24,3712]{1,0:T(8,128)(2,1)} %get-tuple-element.16), channel_id=1, source_target_pairs={{0,1},{1,0},{2,3},{3,2},{4,5},{5,4},{6,7},{7,6},{8,9},{9,8},{10,11... | collective-permute-start | bytes 534536 | tf_op jit(solution)/shard_map/ppermute | solution.py:85
  24.4 14.8 %collective-permute-start.3 = (bf16[96,3712]{1,0:T(8,128)(2,1)S(1)}, bf16[96,3712]{1,0:T(8,128)(2,1)S(1)}, u32[]{:S(2)}, u32[]{:S(2)}) collective-permute-start(bf16[96,3712]{1,0:T(8,128)(2,1)S(1)} %pad_maximum_fusion), channel_id=1, source_target_pairs={{0,8},{8,0},{1,9},{9,1},{2,10},{10,2},{3,11},{11,3},{4,12},{12,4},... | collective-permute-start | bytes 2138120 | tf_op jit(solution)/shard_map/ppermute | solution.py:81
  24.4 7.4 %collective-permute-start.5 = (bf16[24,3712]{1,0:T(8,128)(2,1)S(1)}, bf16[24,3712]{1,0:T(8,128)(2,1)S(1)}, u32[]{:S(2)}, u32[]{:S(2)}) collective-permute-start(bf16[24,3712]{1,0:T(8,128)(2,1)S(1)} %collective-permute-done), channel_id=1, source_target_pairs={{0,1},{1,0},{2,3},{3,2},{4,5},{5,4},{6,7},{7,6},{8,9},{9,8},{10,11... | collective-permute-start | bytes 534536 | tf_op jit(solution)/shard_map/ppermute | solution.py:85
  26.0 9.6 %collective-permute-start.6 = (bf16[24,3712]{1,0:T(8,128)(2,1)S(1)}, bf16[24,3712]{1,0:T(8,128)(2,1)S(1)}, u32[]{:S(2)}, u32[]{:S(2)}) collective-permute-start(bf16[24,3712]{1,0:T(8,128)(2,1)S(1)} %collective-permute-done.1), channel_id=1, source_target_pairs={{0,1},{1,0},{2,3},{3,2},{4,5},{5,4},{6,7},{7,6},{8,9},{9,8},{10,11... | collective-permute-start | bytes 534536 | tf_op jit(solution)/shard_map/ppermute | solution.py:85
  26.5 12.5 %collective-permute-start.7 = (bf16[24,3712]{1,0:T(8,128)(2,1)}, bf16[24,3712]{1,0:T(8,128)(2,1)S(1)}, u32[]{:S(2)}, u32[]{:S(2)}) collective-permute-start(bf16[24,3712]{1,0:T(8,128)(2,1)} %collective-permute-done.2), channel_id=1, source_target_pairs={{0,1},{1,0},{2,3},{3,2},{4,5},{5,4},{6,7},{7,6},{8,9},{9,8},{10,11... | collective-permute-start | bytes 534536 | tf_op jit(solution)/shard_map/ppermute | solution.py:85
  39.1 2.2 %collective-permute-start.8 = (bf16[96,3712]{1,0:T(8,128)(2,1)S(1)}, bf16[96,3712]{1,0:T(8,128)(2,1)S(1)}, u32[]{:S(2)}, u32[]{:S(2)}) collective-permute-start(bf16[96,3712]{1,0:T(8,128)(2,1)S(1)} %pad_maximum_fusion.1), channel_id=1, source_target_pairs={{0,8},{8,0},{1,9},{9,1},{2,10},{10,2},{3,11},{11,3},{4,12},{12,4},... | collective-permute-start | bytes 2138120 | tf_op jit(solution)/shard_map/ppermute | solution.py:81
  41.4 1.6 %copy-start.1 = (bf16[384,3712]{1,0:T(8,128)(2,1)}, bf16[384,3712]{1,0:T(8,128)(2,1)S(1)}, u32[]{:S(2)}) copy-start(bf16[384,3712]{1,0:T(8,128)(2,1)S(1)} %constant_dynamic-update-slice_fusion.rows_ref) | copy-start | bytes 8552452
  73.5 4.7 %copy-start = (bf16[384,3584]{1,0:T(8,128)(2,1)S(1)}, bf16[384,3584]{1,0:T(8,128)(2,1)}, u32[]{:S(2)}) copy-start(bf16[384,3584]{1,0:T(8,128)(2,1)} %down.1) | copy-start | bytes 8257540
  75.0 2.2 %collective-permute-start.10 = (bf16[96,3584]{1,0:T(8,128)(2,1)S(1)}, bf16[96,3584]{1,0:T(8,128)(2,1)S(1)}, u32[]{:S(2)}, u32[]{:S(2)}) collective-permute-start(bf16[96,3584]{1,0:T(8,128)(2,1)S(1)} %get-tuple-element.8), channel_id=1, source_target_pairs={{0,8},{8,0},{1,9},{9,1},{2,10},{10,2},{3,11},{11,3},{4,12},{12,4},... | collective-permute-start | bytes 2064392 | tf_op jit(solution)/shard_map/ppermute | solution.py:81
  75.2 3.0 %collective-permute-start.9 = (bf16[96,3584]{1,0:T(8,128)(2,1)S(1)}, bf16[96,3584]{1,0:T(8,128)(2,1)S(1)}, u32[]{:S(2)}, u32[]{:S(2)}) collective-permute-start(bf16[96,3584]{1,0:T(8,128)(2,1)S(1)} %get-tuple-element.7), channel_id=1, source_target_pairs={{0,8},{8,0},{1,9},{9,1},{2,10},{10,2},{3,11},{11,3},{4,12},{12,4},... | collective-permute-start | bytes 2064392 | tf_op jit(solution)/shard_map/ppermute | solution.py:81
  78.6 7.3 %collective-permute-start.11 = (bf16[24,3584]{1,0:T(8,128)(2,1)S(1)}, bf16[24,3584]{1,0:T(8,128)(2,1)S(1)}, u32[]{:S(2)}, u32[]{:S(2)}) collective-permute-start(bf16[24,3584]{1,0:T(8,128)(2,1)S(1)} %get-tuple-element.12), channel_id=1, source_target_pairs={{0,1},{1,0},{2,3},{3,2},{4,5},{5,4},{6,7},{7,6},{8,9},{9,8},{10,11... | collective-permute-start | bytes 516104 | tf_op jit(solution)/shard_map/ppermute | solution.py:85
  80.2 9.4 %collective-permute-start.13 = (bf16[24,3584]{1,0:T(8,128)(2,1)S(1)}, bf16[24,3584]{1,0:T(8,128)(2,1)S(1)}, u32[]{:S(2)}, u32[]{:S(2)}) collective-permute-start(bf16[24,3584]{1,0:T(8,128)(2,1)S(1)} %get-tuple-element.15), channel_id=1, source_target_pairs={{0,1},{1,0},{2,3},{3,2},{4,5},{5,4},{6,7},{7,6},{8,9},{9,8},{10,11... | collective-permute-start | bytes 516104 | tf_op jit(solution)/shard_map/ppermute | solution.py:85
  80.7 12.6 %collective-permute-start.15 = (bf16[24,3584]{1,0:T(8,128)(2,1)S(1)}, bf16[24,3584]{1,0:T(8,128)(2,1)S(1)}, u32[]{:S(2)}, u32[]{:S(2)}) collective-permute-start(bf16[24,3584]{1,0:T(8,128)(2,1)S(1)} %get-tuple-element.14), channel_id=1, source_target_pairs={{0,1},{1,0},{2,3},{3,2},{4,5},{5,4},{6,7},{7,6},{8,9},{9,8},{10,11... | collective-permute-start | bytes 516104 | tf_op jit(solution)/shard_map/ppermute | solution.py:85
  82.2 15.9 %collective-permute-start.17 = (bf16[24,3584]{1,0:T(8,128)(2,1)S(1)}, bf16[24,3584]{1,0:T(8,128)(2,1)S(1)}, u32[]{:S(2)}, u32[]{:S(2)}) collective-permute-start(bf16[24,3584]{1,0:T(8,128)(2,1)S(1)} %get-tuple-element.13), channel_id=1, source_target_pairs={{0,1},{1,0},{2,3},{3,2},{4,5},{5,4},{6,7},{7,6},{8,9},{9,8},{10,11... | collective-permute-start | bytes 516104 | tf_op jit(solution)/shard_map/ppermute | solution.py:85
  93.4 8.9 %collective-permute-start.12 = (bf16[24,3584]{1,0:T(8,128)(2,1)S(1)}, bf16[24,3584]{1,0:T(8,128)(2,1)S(1)}, u32[]{:S(2)}, u32[]{:S(2)}) collective-permute-start(bf16[24,3584]{1,0:T(8,128)(2,1)S(1)} %get-tuple-element.9), channel_id=1, source_target_pairs={{0,6},{1,7},{2,4},{3,5},{4,2},{5,3},{6,0},{7,1},{8,14},{9,15},{10,... | collective-permute-start | bytes 516104 | tf_op jit(solution)/shard_map/ppermute | solution.py:85
  95.9 15.2 %collective-permute-start.14 = (bf16[24,3584]{1,0:T(8,128)(2,1)S(1)}, bf16[24,3584]{1,0:T(8,128)(2,1)S(1)}, u32[]{:S(2)}, u32[]{:S(2)}) collective-permute-start(bf16[24,3584]{1,0:T(8,128)(2,1)S(1)} %get-tuple-element.11), channel_id=1, source_target_pairs={{0,4},{1,5},{2,6},{3,7},{4,0},{5,1},{6,2},{7,3},{8,12},{9,13},{10,... | collective-permute-start | bytes 516104 | tf_op jit(solution)/shard_map/ppermute | solution.py:85
  98.0 13.1 %collective-permute-start.16 = (bf16[24,3584]{1,0:T(8,128)(2,1)S(1)}, bf16[24,3584]{1,0:T(8,128)(2,1)S(1)}, u32[]{:S(2)}, u32[]{:S(2)}) collective-permute-start(bf16[24,3584]{1,0:T(8,128)(2,1)S(1)} %get-tuple-element.10), channel_id=1, source_target_pairs={{0,2},{1,3},{2,0},{3,1},{4,6},{5,7},{6,4},{7,5},{8,10},{9,11},{10,... | collective-permute-start | bytes 516104 | tf_op jit(solution)/shard_map/ppermute | solution.py:85

commit v2 on v1

v2 whole, which is shorter than its diff:
```python
import functools

import jax
import jax.numpy as jnp
from jax import lax
from jax.experimental import pallas as pl
from jax.experimental.pallas import tpu as pltpu
from jax.sharding import PartitionSpec as P

LANES = 128
MIB = 1024 * 1024
TILE = 512
VMEM = pl.BlockSpec(memory_space=pltpu.VMEM)
HBM = pl.BlockSpec(memory_space=pltpu.HBM)
SMEM = pl.BlockSpec(memory_space=pltpu.SMEM)


def send_kernel(experts, rows_ref, ids_ref, scores_ref, out_ref):
    sigmoid_vals = jax.nn.sigmoid(scores_ref[...])
    weights = 2.5 * sigmoid_vals / jnp.sum(sigmoid_vals, axis=0, keepdims=True)
    top, count = weights.shape
    expert = lax.broadcasted_iota(jnp.int32, (experts, count), 0)
    dense = jnp.zeros((experts, count), jnp.float32)
    for k in range(top):
        dense += jnp.where(expert == ids_ref[k : k + 1, :], weights[k : k + 1, :], 0.0)
    high = lax.reduce_precision(dense, 8, 7)
    rest = jnp.zeros((LANES - 2 * experts, count), jnp.float32)
    table = jnp.concatenate([high, dense - high, rest]).astype(jnp.bfloat16)
    same = lax.broadcasted_iota(jnp.int32, (count, count), 0)
    same = same == lax.broadcasted_iota(jnp.int32, (count, count), 1)
    columns = lax.dot_general(
        same.astype(jnp.float32).astype(jnp.bfloat16),
        table,
        (((1,), (1,)), ((), ())),
        preferred_element_type=jnp.float32,
    )
    width = rows_ref.shape[1]
    out_ref[:, :width] = rows_ref[...]
    out_ref[:, width:] = columns.astype(jnp.bfloat16)


def with_routing(rows, expert_ids, gate_scores, experts):
    count, width = rows.shape
    return pl.pallas_call(
        functools.partial(send_kernel, experts),
        in_specs=[VMEM] * 3,
        out_specs=VMEM,
        out_shape=jax.ShapeDtypeStruct((count, width + LANES), jnp.bfloat16),
        compiler_params=pltpu.CompilerParams(vmem_limit_bytes=4 * MIB),
        name="with_routing",
    )(rows, expert_ids.T, gate_scores.T)


def weight_of(columns, expert, experts):
    lane = lax.broadcasted_iota(jnp.int32, columns.shape, 1)
    mine = (lane == expert) | (lane == expert + experts)
    return jnp.sum(jnp.where(mine, columns, 0.0), axis=1, keepdims=True)


def hidden_of(x, gate_w, up_w, weight):
    gate = jnp.dot(x, gate_w, preferred_element_type=jnp.float32)
    upper = jnp.dot(x, up_w, preferred_element_type=jnp.float32)
    return (gate / (1.0 + jnp.exp(-gate)) * upper * weight).astype(jnp.bfloat16)


def stream_up_kernel(experts, local_experts, index_ref, rows_ref, gate_w_ref, up_w_ref, out_ref):
    model_width = gate_w_ref.shape[1]
    expert = index_ref[0] * local_experts + pl.program_id(0)
    weight = weight_of(rows_ref[:, model_width:].astype(jnp.float32), expert, experts)
    out_ref[...] = hidden_of(rows_ref[:, :model_width], gate_w_ref[0], up_w_ref[0], weight)


def stream_down_kernel(hidden_ref, down_w_ref, out_ref):
    block = down_w_ref[...]
    block = block.reshape(block.shape[0] * block.shape[1], block.shape[2])
    out_ref[...] = jnp.dot(
        hidden_ref[...], block, preferred_element_type=jnp.float32
    ).astype(jnp.bfloat16)


def stream_rows(rows, w_gate, w_up, w_down, inner_index, experts):
    local_experts, model_width, width = w_gate.shape
    count, part = rows.shape[0], width // 2
    hidden = pl.pallas_call(
        functools.partial(stream_up_kernel, experts, local_experts),
        grid=(local_experts, 2),
        in_specs=[
            pl.BlockSpec(memory_space=pltpu.SMEM),
            pl.BlockSpec((count, rows.shape[1]), lambda l, s: (0, 0)),
            pl.BlockSpec((1, model_width, part), lambda l, s: (l, 0, s)),
            pl.BlockSpec((1, model_width, part), lambda l, s: (l, 0, s)),
        ],
        out_specs=pl.BlockSpec((count, part), lambda l, s: (0, l * 2 + s)),
        out_shape=jax.ShapeDtypeStruct((count, local_experts * width), jnp.bfloat16),
        compiler_params=pltpu.CompilerParams(vmem_limit_bytes=60 * MIB),
        name="stream_gate_up",
    )(inner_index, rows, w_gate, w_up)
    return pl.pallas_call(
        stream_down_kernel,
        grid=(model_width // TILE,),
        in_specs=[
            pl.BlockSpec(hidden.shape, lambda n: (0, 0)),
            pl.BlockSpec((local_experts, width, TILE), lambda n: (0, 0, n)),
        ],
        out_specs=pl.BlockSpec((count, TILE), lambda n: (0, n)),
        out_shape=jax.ShapeDtypeStruct((count, model_width), jnp.bfloat16),
        compiler_params=pltpu.CompilerParams(vmem_limit_bytes=60 * MIB),
        name="stream_down",
    )(hidden, w_down)


def load_kernel(source_ref, copy_ref, sem):
    copy = pltpu.make_async_copy(source_ref, copy_ref, sem)
    copy.start()
    copy.wait()


def load(weights):
    size = weights.size * weights.dtype.itemsize
    return pl.pallas_call(
        load_kernel,
        in_specs=[pl.BlockSpec(memory_space=pltpu.HBM)],
        out_specs=VMEM,
        out_shape=pltpu.VMEM(weights.shape, weights.dtype),
        scratch_shapes=[pltpu.SemaphoreType.DMA],
        compiler_params=pltpu.CompilerParams(vmem_limit_bytes=MIB),
        cost_estimate=pl.CostEstimate(flops=0, bytes_accessed=2 * size, transcendentals=0),
        name="load",
    )(weights)


def assemble(row_refs, x_ref):
    rows = jnp.concatenate([ref[...].astype(jnp.float32) for ref in row_refs])
    width = x_ref.shape[1]
    x_ref[...] = rows[:, :width].astype(jnp.bfloat16)
    return rows[:, width:]


def near_kernel(experts, blocks, index_ref, *refs):
    rows, (gate_w, up_source, out, up_w, x, gates, sems) = refs[:blocks], refs[blocks:]
    local_experts, _, width = gate_w.shape
    copies = [
        pltpu.make_async_copy(up_source.at[l], up_w.at[l], sems.at[l])
        for l in range(local_experts)
    ]
    for copy in copies:
        copy.start()
    columns = assemble(rows, x)
    for l in range(local_experts):
        part = slice(l * width, (l + 1) * width)
        gates[:, part] = jnp.dot(x[...], gate_w[l], preferred_element_type=jnp.float32)
    for l in range(local_experts):
        part = slice(l * width, (l + 1) * width)
        weight = weight_of(columns, index_ref[0] * local_experts + l, experts)
        copies[l].wait()
        gate = gates[:, part]
        upper = jnp.dot(x[...], up_w[l], preferred_element_type=jnp.float32)
        out[:, part] = (gate / (1.0 + jnp.exp(-gate)) * upper * weight).astype(jnp.bfloat16)


def near_rows(blocks, w_gate, w_up, inner_index, experts):
    local_experts, model_width, width = w_gate.shape
    count = sum(block.shape[0] for block in blocks)
    return pl.pallas_call(
        functools.partial(near_kernel, experts, len(blocks)),
        in_specs=[SMEM] + [VMEM] * (len(blocks) + 1) + [HBM],
        out_specs=[VMEM] * 2,
        out_shape=[
            jax.ShapeDtypeStruct((count, local_experts * width), jnp.bfloat16),
            pltpu.VMEM(w_up.shape, w_up.dtype),
        ],
        scratch_shapes=[
            pltpu.VMEM((count, model_width), jnp.bfloat16),
            pltpu.VMEM((count, local_experts * width), jnp.float32),
            pltpu.SemaphoreType.DMA((local_experts,)),
        ],
        compiler_params=pltpu.CompilerParams(vmem_limit_bytes=8 * MIB),
        cost_estimate=pl.CostEstimate(
            flops=4 * count * model_width * width * local_experts,
            bytes_accessed=0,
            transcendentals=0,
        ),
        name="near_rows",
    )(inner_index, *blocks, w_gate, w_up)


def fetch(source_ref, first, block_ref, sems):
    copies = []
    for at in range(0, block_ref.shape[2], TILE):
        size = min(TILE, block_ref.shape[2] - at)
        copy = pltpu.make_async_copy(
            source_ref.at[:, :, pl.ds(first + at, size)],
            block_ref.at[:, :, pl.ds(at, size)],
            sems.at[at // TILE],
        )
        copy.start()
        copies.append((at, size, copy))
    return copies


def down_into(copies, hidden_ref, block_ref, near_out, far_out, other_out):
    half = near_out.shape[0]
    for at, size, copy in copies:
        copy.wait()
        block = block_ref[:, :, at : at + size].reshape(-1, size)
        value = jnp.dot(hidden_ref[...], block, preferred_element_type=jnp.float32)
        value = value.astype(jnp.bfloat16)
        near_out[:, at : at + size] = value[:half]
        other_out[:half, at : at + size] = value[half : 2 * half]
        far_out[:, at : at + size] = value[2 * half : 3 * half]
        other_out[half:, at : at + size] = value[3 * half :]


def far_kernel(experts, blocks, index_ref, *refs):
    rows, rest = refs[:blocks], refs[blocks:]
    gate_w, up_w, near, down_w, hidden, near_out, far_out, other_out, x, block, sems = rest
    local_experts, _, width = gate_w.shape
    copies = fetch(down_w, 0, block, sems)
    columns = assemble(rows, x)
    count = near.shape[0]
    hidden[:count] = near[...]
    for l in range(local_experts):
        weight = weight_of(columns, index_ref[0] * local_experts + l, experts)
        hidden[count:, l * width : (l + 1) * width] = hidden_of(
            x[...], gate_w[l], up_w[l], weight
        )
    down_into(copies, hidden, block, near_out, far_out, other_out)


def down_kernel(first, hidden, down_w, near_out, far_out, other_out, block, sems):
    down_into(
        fetch(down_w, first, block, sems), hidden, block, near_out, far_out, other_out
    )


def sums(half, columns):
    return [
        jax.ShapeDtypeStruct((rows, columns), jnp.bfloat16) for rows in (half, half, 2 * half)
    ]


def tiles(local_experts, width, columns):
    return [
        pltpu.VMEM((local_experts, width, columns), jnp.bfloat16),
        pltpu.SemaphoreType.DMA((pl.cdiv(columns, TILE),)),
    ]


def far_rows(blocks, w_gate, w_up, near, w_down, inner_index, experts, cut):
    count, depth = near.shape
    local_experts, width, model_width = w_down.shape
    return pl.pallas_call(
        functools.partial(far_kernel, experts, len(blocks)),
        in_specs=[SMEM] + [VMEM] * (len(blocks) + 3) + [HBM],
        out_specs=[VMEM] * 4,
        out_shape=[jax.ShapeDtypeStruct((2 * count, depth), near.dtype)]
        + sums(count // 2, cut),
        scratch_shapes=[pltpu.VMEM((count, model_width), jnp.bfloat16)]
        + tiles(local_experts, width, cut),
        compiler_params=pltpu.CompilerParams(vmem_limit_bytes=15 * MIB),
        name="far_rows",
    )(inner_index, *blocks, w_gate, w_up, near, w_down)


def down(hidden, w_down, first):
    local_experts, width, model_width = w_down.shape
    columns = model_width - first
    return pl.pallas_call(
        functools.partial(down_kernel, first),
        in_specs=[VMEM, HBM],
        out_specs=[VMEM] * 3,
        out_shape=sums(hidden.shape[0] // 4, columns),
        scratch_shapes=tiles(local_experts, width, columns),
        compiler_params=pltpu.CompilerParams(vmem_limit_bytes=15 * MIB),
        cost_estimate=pl.CostEstimate(
            flops=2 * hidden.size * columns, bytes_accessed=0, transcendentals=0
        ),
        name="down",
    )(hidden, w_down)


def swap_core(value):
    return lax.ppermute(value, "outer", [(0, 1), (1, 0)])


def swap_inner(value, bit):
    return lax.ppermute(value, "inner", [(i, i ^ bit) for i in range(8)])


def tie(*values):
    return lax.optimization_barrier(values)


def wide(value):
    return value.astype(jnp.float32)


def on_device(hidden_states, expert_ids, gate_scores, w_gate, w_up, w_down):
    local_experts, model_width, _ = w_gate.shape
    inner_size = lax.axis_size("inner")
    experts = local_experts * inner_size
    count = hidden_states.shape[0]
    inner_index = lax.axis_index("inner").astype(jnp.int32).reshape(1)
    own = with_routing(hidden_states, expert_ids, gate_scores, experts)
    if inner_size != 8 or lax.axis_size("outer") != 2:
        everyone = lax.all_gather(own, ("outer", "inner"), axis=0, tiled=True)
        outs = stream_rows(everyone, w_gate, w_up, w_down, inner_index, experts)
        return lax.psum_scatter(outs, ("outer", "inner"), scatter_dimension=0, tiled=True)

    w_gate, w_up, w_down = (
        pltpu.with_memory_space_constraint(w, pltpu.HBM) for w in (w_gate, w_up, w_down)
    )
    own, inner_index = tie(own, inner_index)
    z1, y0, z2 = swap_inner(own, 2), swap_inner(own, 1), swap_inner(own, 4)
    w_gate = load(w_gate)
    own, z1, z2, y0, w_gate = tie(own, z1, z2, y0, w_gate)
    z3, y1, y2 = swap_inner(own, 6), swap_inner(z1, 1), swap_inner(z2, 1)
    y3 = swap_inner(z3, 1)
    near = [own, z1, z2, z3]
    near += [swap_core(block) for block in near]
    hidden, w_up = near_rows(near, w_gate, w_up, inner_index, experts)
    hidden, y3 = tie(hidden, y3)
    far = [y0, y1, y2, y3]
    far += [swap_core(block) for block in far]

    cut = (model_width // LANES * 5 // 7) * LANES
    group = 4 * count

    def rows(step):
        return slice(step * count, (step + 1) * count)

    hidden, near_a, far_a, other_a = far_rows(
        far, w_gate, w_up, hidden, w_down, inner_index, experts, cut
    )
    other_a = swap_core(other_a)
    far_a = (wide(far_a) + wide(other_a[group:])).astype(jnp.bfloat16)
    far_a, hidden = tie(far_a, hidden)
    across = swap_inner(far_a, 1)
    near_b, far_b, other_b = down(hidden, w_down, cut)
    other_b = swap_core(other_b)

    both = jnp.stack([near_b, far_b]).reshape(2, 4, count, -1)
    both = wide(both) + wide(other_b.reshape(2, 4, count, -1))
    sent_b = [swap_inner(both[:, step].astype(jnp.bfloat16), 2 * step) for step in (3, 2, 1)]
    across, *sent_b = tie(across, *sent_b)

    total_a = wide(near_a) + wide(other_a[:group]) + wide(across)
    sent_a = [
        swap_inner(total_a[rows(step)].astype(jnp.bfloat16), 2 * step) for step in (3, 2, 1)
    ]
    sum_b = sum((wide(block) for block in sent_b), both[:, 0])
    sum_b = sum_b[0] + wide(swap_inner(sum_b[1].astype(jnp.bfloat16), 1))
    sum_a = sum((wide(block) for block in sent_a), total_a[rows(0)])
    return jnp.concatenate([sum_a, sum_b], axis=1).astype(jnp.bfloat16)


def solution(mesh):
    return jax.shard_map(
        on_device,
        mesh=mesh,
        in_specs=(
            P(("groups", "outer", "inner"), None),
            P(("groups", "outer", "inner"), None),
            P(("groups", "outer", "inner"), None),
            P("inner", None, "outer"),
            P("inner", None, "outer"),
            P("inner", "outer", None),
        ),
        out_specs=P(("groups", "outer", "inner"), None),
        check_vma=False,
    )
```

time: 112 us -> 87.6 us (0.78)
  waiting for transfers between devices: 49.9 us -> 29.9 us
  other arithmetic: 5.59 us -> 1.24 us
  starting transfers between devices: 20.5 us -> 24.1 us
  local copies, waits for them, and re-layouts: 5.24 us -> 2.35 us
    ppermute x14 -> x15, waiting for transfers between devices: 45.3 us -> 25 us  [swap_inner(): return lax.ppermute(value, 'inner', [(i, i ^ bit) for i in range(8)])]
    ppermute x14 -> x15, starting transfers between devices: 19.8 us -> 22.9 us  [swap_inner(): return lax.ppermute(value, 'inner', [(i, i ^ bit) for i in range(8)])]
    concatenate x4 -> x1, other arithmetic: 2.8 us -> 0.68 us  [on_device(): return jnp.concatenate([sum_a, sum_b], axis=1).astype(jnp.bfloat16)]
    slice x2 -> x1, local copies, waits for them, and re-layouts: 1.59 us -> 0.03 us  [on_device(): total_a[rows(step)].astype(jnp.bfloat16)]
    unnamed x13 -> x6, local copies, waits for them, and re-layouts: 3.49 us -> 2.29 us
    convert_element_type x3 -> x1, other arithmetic: 1.25 us -> 0.11 us  [on_device(): far_a = (wide(far_a) + wide(other_a[group:])).astype(jnp.bfloat16)]
    pallas_call x2 -> x5, Pallas kernels: 30.5 us -> 29.6 us  [the longest x1 12.6 us: far_rows(): pl.pallas_call(functools.partial(far_kernel, experts, len(blocks)), in_sp...]
    ppermute x4 -> x10, waiting for transfers between devices: 4.59 us -> 4.86 us  [swap_core(): return lax.ppermute(value, 'outer', [(0, 1), (1, 0)])]
  transfers between devices with their start and end apart: 18 -> 25, of which waited for: 13 -> 12; matrix products, arithmetic and copies ran while one was open for 2% -> 0% of each run, Pallas kernels for 0% -> 15%
where the time goes in v2:
time: 87.6 us; the launch traced here: 87.4 us
  waiting for transfers between devices  29.9 us (34%)
  Pallas kernels  29.6 us (34%)
  starting transfers between devices  24.1 us (28%)
  local copies, waits for them, and re-layouts  2.35 us (3%)
  other arithmetic  1.24 us (1%)
    ppermute x15, waiting for transfers between devices, swap_inner(): return lax.ppermute(value, 'inner', [(i, i ^ bit) for i in range(8)])  25 us
    ppermute x15, starting transfers between devices, swap_inner(): return lax.ppermute(value, 'inner', [(i, i ^ bit) for i in range(8)])  22.9 us
    pallas_call x1, Pallas kernels, far_rows(): pl.pallas_call(functools.partial(far_kernel, experts, len(blocks)), in_sp...  12.6 us
    pallas_call x1, Pallas kernels, near_rows(): pl.pallas_call(functools.partial(near_kernel, experts, len(blocks)), in_s...  8.07 us
    pallas_call x1, Pallas kernels, load(): pl.pallas_call(load_kernel, in_specs=[pl.BlockSpec(memory_space=pltpu.HBM...  5.18 us
    ppermute x10, waiting for transfers between devices, swap_core(): return lax.ppermute(value, 'outer', [(0, 1), (1, 0)])  4.86 us
    pallas_call x1, Pallas kernels, down(): pl.pallas_call(functools.partial(down_kernel, first), in_specs=[VMEM, HBM...  3.57 us
    unnamed x6, local copies, waits for them, and re-layouts  2.29 us
  transfers between devices with their start and end apart: 25, of which 12 were waited for; matrix products, arithmetic and copies ran while one was open for 0% of the time, Pallas kernels for 15%

profile of v2, /device:TPU:0, one launch (start us, length us, event | category | flops | bytes accessed | tf_op | source)
XLA Modules:
  0.0 87.4 jit_solution(2747169411759587485)
XLA Ops:
  0.0 0.9 %copy-done = bf16[24,3584]{1,0:T(8,128)(2,1)S(1)} copy-done((bf16[24,3584]{1,0:T(8,128)(2,1)S(1)}, bf16[24,3584]{1,0:T(8,128)(2,1)}, u32[]{:S(2)}) %copy-start) | copy-done | bytes 172056
  0.9 0.7 copy-done.1
  1.6 0.7 copy-done.2
  2.3 0.2 with_routing.1.refs_0_
  2.5 3.0 %collective-permute-start.2 = (bf16[24,3712]{1,0:T(8,128)(2,1)S(1)}, bf16[24,3712]{1,0:T(8,128)(2,1)S(1)}, u32[]{:S(2)}, u32[]{:S(2)}) collective-permute-start(bf16[24,3712]{1,0:T(8,128)(2,1)S(1)} %with_routing.1.refs_0_), channel_id=1, source_target_pairs={{0,1},{1,0},{2,3},{3,2},{4,5},{5,4},{6,7},{7,6},{8,9},{9,8},{10,11... | collective-permute-start | bytes 534536 | tf_op jit(solution)/shard_map/ppermute | solution.py:287
  5.4 2.6 %collective-permute-start.1 = (bf16[24,3712]{1,0:T(8,128)(2,1)S(1)}, bf16[24,3712]{1,0:T(8,128)(2,1)S(1)}, u32[]{:S(2)}, u32[]{:S(2)}) collective-permute-start(bf16[24,3712]{1,0:T(8,128)(2,1)S(1)} %with_routing.1.refs_0_), channel_id=1, source_target_pairs={{0,4},{1,5},{2,6},{3,7},{4,0},{5,1},{6,2},{7,3},{8,12},{9,13},{10,... | collective-permute-start | bytes 534536 | tf_op jit(solution)/shard_map/ppermute | solution.py:287
  8.0 1.6 %collective-permute-start = (bf16[24,3712]{1,0:T(8,128)(2,1)S(1)}, bf16[24,3712]{1,0:T(8,128)(2,1)S(1)}, u32[]{:S(2)}, u32[]{:S(2)}) collective-permute-start(bf16[24,3712]{1,0:T(8,128)(2,1)S(1)} %with_routing.1.refs_0_), channel_id=1, source_target_pairs={{0,2},{1,3},{2,0},{3,1},{4,6},{5,7},{6,4},{7,5},{8,10},{9,11},{10,... | collective-permute-start | bytes 534536 | tf_op jit(solution)/shard_map/ppermute | solution.py:287
  9.6 5.2 %load.1.refs_8_ = bf16[4,3584,512]{2,1,0:T(8,128)(2,1)S(1)} custom-call(bf16[4,3584,512]{2,1,0:T(8,128)(2,1)} %source_ref.1), custom_call_target="tpu_custom_call" | custom-call | bytes 29360128 | tf_op jit(solution)/shard_map/load/pallas_call | solution.py:120
  14.8 0.0 collective-permute-done.2.refs_0_
  14.8 1.4 %collective-permute-done.1.refs_2_ = bf16[24,3712]{1,0:T(8,128)(2,1)S(1)} collective-permute-done((bf16[24,3712]{1,0:T(8,128)(2,1)S(1)}, bf16[24,3712]{1,0:T(8,128)(2,1)S(1)}, u32[]{:S(2)}, u32[]{:S(2)}) %collective-permute-start.1) | collective-permute-done | bytes 178208 | tf_op jit(solution)/shard_map/ppermute | solution.py:287
  16.2 0.2 collective-permute-done.refs_1_
  16.4 0.0 collective-permute-start.7
  16.4 3.2 %collective-permute-start.5 = (bf16[24,3712]{1,0:T(8,128)(2,1)S(1)}, bf16[24,3712]{1,0:T(8,128)(2,1)S(1)}, u32[]{:S(2)}, u32[]{:S(2)}) collective-permute-start(bf16[24,3712]{1,0:T(8,128)(2,1)S(1)} %with_routing.1.refs_0_), channel_id=1, source_target_pairs={{0,6},{1,7},{2,4},{3,5},{4,2},{5,3},{6,0},{7,1},{8,14},{9,15},{10,... | collective-permute-start | bytes 534536 | tf_op jit(solution)/shard_map/ppermute | solution.py:287
  19.6 0.5 collective-permute-start.3
  20.1 0.0 collective-permute-start.8
  20.1 1.5 %collective-permute-start.4 = (bf16[24,3712]{1,0:T(8,128)(2,1)S(1)}, bf16[24,3712]{1,0:T(8,128)(2,1)S(1)}, u32[]{:S(2)}, u32[]{:S(2)}) collective-permute-start(bf16[24,3712]{1,0:T(8,128)(2,1)S(1)} %collective-permute-done.1.refs_2_), channel_id=1, source_target_pairs={{0,1},{1,0},{2,3},{3,2},{4,5},{5,4},{6,7},{7,6},{8,9},{9,8},{10,11... | collective-permute-start | bytes 534536 | tf_op jit(solution)/shard_map/ppermute | solution.py:287
  21.7 0.2 collective-permute-start.6
  21.9 3.4 %collective-permute-done.5.refs_3_ = bf16[24,3712]{1,0:T(8,128)(2,1)S(1)} collective-permute-done((bf16[24,3712]{1,0:T(8,128)(2,1)S(1)}, bf16[24,3712]{1,0:T(8,128)(2,1)S(1)}, u32[]{:S(2)}, u32[]{:S(2)}) %collective-permute-start.5) | collective-permute-done | bytes 178208 | tf_op jit(solution)/shard_map/ppermute | solution.py:287
  25.2 1.7 %collective-permute-done.3.refs_1_ = bf16[24,3712]{1,0:T(8,128)(2,1)S(1)} collective-permute-done((bf16[24,3712]{1,0:T(8,128)(2,1)S(1)}, bf16[24,3712]{1,0:T(8,128)(2,1)S(1)}, u32[]{:S(2)}, u32[]{:S(2)}) %collective-permute-start.3) | collective-permute-done | bytes 178208 | tf_op jit(solution)/shard_map/ppermute | solution.py:287
  27.0 0.5 collective-permute-start.10
  27.5 2.6 %collective-permute-done.4.refs_2_ = bf16[24,3712]{1,0:T(8,128)(2,1)S(1)} collective-permute-done((bf16[24,3712]{1,0:T(8,128)(2,1)S(1)}, bf16[24,3712]{1,0:T(8,128)(2,1)S(1)}, u32[]{:S(2)}, u32[]{:S(2)}) %collective-permute-start.4) | collective-permute-done | bytes 178208 | tf_op jit(solution)/shard_map/ppermute | solution.py:287
  30.1 0.5 collective-permute-start.13
  30.6 8.1 %near_rows.1 = (bf16[192,2048]{1,0:T(8,128)(2,1)S(1)}, bf16[4,3584,512]{2,1,0:T(8,128)(2,1)S(1)}) custom-call(s32[1]{0:T(128)} %bitcast.2.index_ref, bf16[24,3712]{1,0:T(8,128)(2,1)S(1)} %with_routing.1.refs_0_, bf16[24,3712]{1,0:T(8,128)(2,1)S(1)} %collective-permute-done.refs_1_, bf16[24,3712]{1,0:T(8,128)(2,1)S(1)} %collective-permute-done.1.refs_2_, ...), custom_call_target="tpu_custom_call" | custom-call | flops 5637144576 | tf_op jit(solution)/shard_map/near_rows/pallas_call | solution.py:164
  38.7 0.1 collective-permute-start.14
  38.8 1.4 %collective-permute-done.14.refs_7_ = bf16[24,3712]{1,0:T(8,128)(2,1)S(1)} collective-permute-done((bf16[24,3712]{1,0:T(8,128)(2,1)S(1)}, bf16[24,3712]{1,0:T(8,128)(2,1)S(1)}, u32[]{:S(2)}, u32[]{:S(2)}) %collective-permute-start.14) | collective-permute-done | bytes 178208 | tf_op jit(solution)/shard_map/ppermute | solution.py:283
  40.2 12.6 %far_rows.1 = (bf16[384,2048]{1,0:T(8,128)(2,1)S(1)}, bf16[96,2560]{1,0:T(8,128)(2,1)S(1)}, bf16[96,2560]{1,0:T(8,128)(2,1)S(1)}, bf16[192,2560]{1,0:T(8,128)(2,1)S(1)}) custom-call(s32[1]{0:T(128)} %bitcast.2.index_ref, bf16[24,3712]{1,0:T(8,128)(2,1)S(1)} %collective-permute-done.2.refs_0_, bf16[24,3712]{1,0:T(8,128)(2,1)S(1)} %collective-permute-done.3.refs_1_, ...), custom_call_target="tpu_custom_call" | custom-call | tf_op jit(solution)/shard_map/far_rows/pallas_call | solution.py:252
  52.8 0.2 collective-permute-start.15
  53.0 2.4 %collective-permute-done.15 = bf16[192,2560]{1,0:T(8,128)(2,1)S(1)} collective-permute-done((bf16[192,2560]{1,0:T(8,128)(2,1)S(1)}, bf16[192,2560]{1,0:T(8,128)(2,1)S(1)}, u32[]{:S(2)}, u32[]{:S(2)}) %collective-permute-start.15) | collective-permute-done | bytes 983072 | tf_op jit(solution)/shard_map/ppermute | solution.py:283
  55.4 0.1 add_convert_fusion
  55.5 3.6 %down.1 = (bf16[96,1024]{1,0:T(8,128)(2,1)S(1)}, bf16[96,1024]{1,0:T(8,128)(2,1)S(1)}, bf16[192,1024]{1,0:T(8,128)(2,1)S(1)}) custom-call(bf16[384,2048]{1,0:T(8,128)(2,1)S(1)} %get-tuple-element.45.hidden, bf16[4,512,3584]{2,1,0:T(8,128)(2,1)} %down_w.1), custom_call_target="tpu_custom_call" | custom-call | flops 1610612736 | tf_op jit(solution)/shard_map/down/pallas_call | solution.py:268
  59.1 0.2 collective-permute-start.17
  59.3 0.5 collective-permute-start.16
  59.8 1.0 %collective-permute-done.17 = bf16[192,1024]{1,0:T(8,128)(2,1)S(1)} collective-permute-done((bf16[192,1024]{1,0:T(8,128)(2,1)S(1)}, bf16[192,1024]{1,0:T(8,128)(2,1)S(1)}, u32[]{:S(2)}, u32[]{:S(2)}) %collective-permute-start.17) | collective-permute-done | bytes 393248 | tf_op jit(solution)/shard_map/ppermute | solution.py:283
  60.9 0.1 fusion.10
  61.1 0.1 collective-permute-start.20
  61.2 1.2 %collective-permute-start.19 = (bf16[2,24,1024]{2,1,0:T(8,128)(2,1)S(1)}, bf16[2,24,1024]{2,1,0:T(8,128)(2,1)S(1)}, u32[]{:S(2)}, u32[]{:S(2)}) collective-permute-start(bf16[2,24,1024]{2,1,0:T(8,128)(2,1)S(1)} %get-tuple-element.61), channel_id=1, source_target_pairs={{0,4},{1,5},{2,6},{3,7},{4,0},{5,1},{6,2},{7,3},{8,12},{9,13},{10,... | collective-permute-start | bytes 294920 | tf_op jit(solution)/shard_map/ppermute | solution.py:287
  62.3 3.2 %collective-permute-start.18 = (bf16[2,24,1024]{2,1,0:T(8,128)(2,1)S(1)}, bf16[2,24,1024]{2,1,0:T(8,128)(2,1)S(1)}, u32[]{:S(2)}, u32[]{:S(2)}) collective-permute-start(bf16[2,24,1024]{2,1,0:T(8,128)(2,1)S(1)} %get-tuple-element.62), channel_id=1, source_target_pairs={{0,6},{1,7},{2,4},{3,5},{4,2},{5,3},{6,0},{7,1},{8,14},{9,15},{10,... | collective-permute-start | bytes 294920 | tf_op jit(solution)/shard_map/ppermute | solution.py:287
  65.5 7.3 %collective-permute-done.16 = bf16[96,2560]{1,0:T(8,128)(2,1)S(1)} collective-permute-done((bf16[96,2560]{1,0:T(8,128)(2,1)S(1)}, bf16[96,2560]{1,0:T(8,128)(2,1)S(1)}, u32[]{:S(2)}, u32[]{:S(2)}) %collective-permute-start.16) | collective-permute-done | bytes 491552 | tf_op jit(solution)/shard_map/ppermute | solution.py:287
  72.9 0.6 collective-permute-start.24
  73.5 0.2 fusion.9
  73.7 1.0 %collective-permute-start.21 = (bf16[24,2560]{1,0:T(8,128)(2,1)S(1)}, bf16[24,2560]{1,0:T(8,128)(2,1)S(1)}, u32[]{:S(2)}, u32[]{:S(2)}) collective-permute-start(bf16[24,2560]{1,0:T(8,128)(2,1)S(1)} %get-tuple-element.57), channel_id=1, source_target_pairs={{0,6},{1,7},{2,4},{3,5},{4,2},{5,3},{6,0},{7,1},{8,14},{9,15},{10,... | collective-permute-start | bytes 368648 | tf_op jit(solution)/shard_map/ppermute | solution.py:287
  74.6 0.8 collective-permute-start.23
  75.5 2.7 %collective-permute-start.22 = (bf16[24,2560]{1,0:T(8,128)(2,1)S(1)}, bf16[24,2560]{1,0:T(8,128)(2,1)S(1)}, u32[]{:S(2)}, u32[]{:S(2)}) collective-permute-start(bf16[24,2560]{1,0:T(8,128)(2,1)S(1)} %get-tuple-element.59), channel_id=1, source_target_pairs={{0,4},{1,5},{2,6},{3,7},{4,0},{5,1},{6,2},{7,3},{8,12},{9,13},{10,... | collective-permute-start | bytes 368648 | tf_op jit(solution)/shard_map/ppermute | solution.py:287
  78.2 3.6 %collective-permute-done.21 = bf16[24,2560]{1,0:T(8,128)(2,1)S(1)} collective-permute-done((bf16[24,2560]{1,0:T(8,128)(2,1)S(1)}, bf16[24,2560]{1,0:T(8,128)(2,1)S(1)}, u32[]{:S(2)}, u32[]{:S(2)}) %collective-permute-start.21) | collective-permute-done | bytes 122912 | tf_op jit(solution)/shard_map/ppermute | solution.py:287
  81.8 0.3 collective-permute-done.23
  82.1 4.5 %collective-permute-done.22 = bf16[24,2560]{1,0:T(8,128)(2,1)S(1)} collective-permute-done((bf16[24,2560]{1,0:T(8,128)(2,1)S(1)}, bf16[24,2560]{1,0:T(8,128)(2,1)S(1)}, u32[]{:S(2)}, u32[]{:S(2)}) %collective-permute-start.22) | collective-permute-done | bytes 122912 | tf_op jit(solution)/shard_map/ppermute | solution.py:287
  86.6 0.1 fusion.2
  86.7 0.7 pad_maximum_fusion
  (23 shorter events, 0.2 us)
Async XLA Ops:
  0.0 0.9 %copy-start = (bf16[24,3584]{1,0:T(8,128)(2,1)S(1)}, bf16[24,3584]{1,0:T(8,128)(2,1)}, u32[]{:S(2)}) copy-start(bf16[24,3584]{1,0:T(8,128)(2,1)} %rows_ref.1) | copy-start | bytes 516100
  0.9 0.7 copy-start.1
  1.6 0.7 copy-start.2
  2.5 12.3 %collective-permute-start.2 = (bf16[24,3712]{1,0:T(8,128)(2,1)S(1)}, bf16[24,3712]{1,0:T(8,128)(2,1)S(1)}, u32[]{:S(2)}, u32[]{:S(2)}) collective-permute-start(bf16[24,3712]{1,0:T(8,128)(2,1)S(1)} %with_routing.1.refs_0_), channel_id=1, source_target_pairs={{0,1},{1,0},{2,3},{3,2},{4,5},{5,4},{6,7},{7,6},{8,9},{9,8},{10,11... | collective-permute-start | bytes 534536 | tf_op jit(solution)/shard_map/ppermute | solution.py:287
  5.4 10.8 %collective-permute-start.1 = (bf16[24,3712]{1,0:T(8,128)(2,1)S(1)}, bf16[24,3712]{1,0:T(8,128)(2,1)S(1)}, u32[]{:S(2)}, u32[]{:S(2)}) collective-permute-start(bf16[24,3712]{1,0:T(8,128)(2,1)S(1)} %with_routing.1.refs_0_), channel_id=1, source_target_pairs={{0,4},{1,5},{2,6},{3,7},{4,0},{5,1},{6,2},{7,3},{8,12},{9,13},{10,... | collective-permute-start | bytes 534536 | tf_op jit(solution)/shard_map/ppermute | solution.py:287
  8.0 8.4 %collective-permute-start = (bf16[24,3712]{1,0:T(8,128)(2,1)S(1)}, bf16[24,3712]{1,0:T(8,128)(2,1)S(1)}, u32[]{:S(2)}, u32[]{:S(2)}) collective-permute-start(bf16[24,3712]{1,0:T(8,128)(2,1)S(1)} %with_routing.1.refs_0_), channel_id=1, source_target_pairs={{0,2},{1,3},{2,0},{3,1},{4,6},{5,7},{6,4},{7,5},{8,10},{9,11},{10,... | collective-permute-start | bytes 534536 | tf_op jit(solution)/shard_map/ppermute | solution.py:287
  16.4 5.2 %collective-permute-start.7 = (bf16[24,3712]{1,0:T(8,128)(2,1)S(1)}, bf16[24,3712]{1,0:T(8,128)(2,1)S(1)}, u32[]{:S(2)}, u32[]{:S(2)}) collective-permute-start(bf16[24,3712]{1,0:T(8,128)(2,1)S(1)} %collective-permute-done.refs_1_), channel_id=1, source_target_pairs={{0,8},{8,0},{1,9},{9,1},{2,10},{10,2},{3,11},{11,3},{4,12},{12,4},... | collective-permute-start | bytes 534536 | tf_op jit(solution)/shard_map/ppermute | solution.py:283
  16.4 8.8 %collective-permute-start.5 = (bf16[24,3712]{1,0:T(8,128)(2,1)S(1)}, bf16[24,3712]{1,0:T(8,128)(2,1)S(1)}, u32[]{:S(2)}, u32[]{:S(2)}) collective-permute-start(bf16[24,3712]{1,0:T(8,128)(2,1)S(1)} %with_routing.1.refs_0_), channel_id=1, source_target_pairs={{0,6},{1,7},{2,4},{3,5},{4,2},{5,3},{6,0},{7,1},{8,14},{9,15},{10,... | collective-permute-start | bytes 534536 | tf_op jit(solution)/shard_map/ppermute | solution.py:287
  19.6 7.3 %collective-permute-start.3 = (bf16[24,3712]{1,0:T(8,128)(2,1)S(1)}, bf16[24,3712]{1,0:T(8,128)(2,1)S(1)}, u32[]{:S(2)}, u32[]{:S(2)}) collective-permute-start(bf16[24,3712]{1,0:T(8,128)(2,1)S(1)} %collective-permute-done.refs_1_), channel_id=1, source_target_pairs={{0,1},{1,0},{2,3},{3,2},{4,5},{5,4},{6,7},{7,6},{8,9},{9,8},{10,11... | collective-permute-start | bytes 534536 | tf_op jit(solution)/shard_map/ppermute | solution.py:287
  20.1 6.8 %collective-permute-start.8 = (bf16[24,3712]{1,0:T(8,128)(2,1)S(1)}, bf16[24,3712]{1,0:T(8,128)(2,1)S(1)}, u32[]{:S(2)}, u32[]{:S(2)}) collective-permute-start(bf16[24,3712]{1,0:T(8,128)(2,1)S(1)} %collective-permute-done.1.refs_2_), channel_id=1, source_target_pairs={{0,8},{8,0},{1,9},{9,1},{2,10},{10,2},{3,11},{11,3},{4,12},{12,4},... | collective-permute-start | bytes 534536 | tf_op jit(solution)/shard_map/ppermute | solution.py:283
  20.1 9.9 %collective-permute-start.4 = (bf16[24,3712]{1,0:T(8,128)(2,1)S(1)}, bf16[24,3712]{1,0:T(8,128)(2,1)S(1)}, u32[]{:S(2)}, u32[]{:S(2)}) collective-permute-start(bf16[24,3712]{1,0:T(8,128)(2,1)S(1)} %collective-permute-done.1.refs_2_), channel_id=1, source_target_pairs={{0,1},{1,0},{2,3},{3,2},{4,5},{5,4},{6,7},{7,6},{8,9},{9,8},{10,11... | collective-permute-start | bytes 534536 | tf_op jit(solution)/shard_map/ppermute | solution.py:287
  21.7 8.4 %collective-permute-start.6 = (bf16[24,3712]{1,0:T(8,128)(2,1)S(1)}, bf16[24,3712]{1,0:T(8,128)(2,1)S(1)}, u32[]{:S(2)}, u32[]{:S(2)}) collective-permute-start(bf16[24,3712]{1,0:T(8,128)(2,1)S(1)} %with_routing.1.refs_0_), channel_id=1, source_target_pairs={{0,8},{8,0},{1,9},{9,1},{2,10},{10,2},{3,11},{11,3},{4,12},{12,4},... | collective-permute-start | bytes 534536 | tf_op jit(solution)/shard_map/ppermute | solution.py:283
  25.2 5.3 %collective-permute-start.9 = (bf16[24,3712]{1,0:T(8,128)(2,1)S(1)}, bf16[24,3712]{1,0:T(8,128)(2,1)S(1)}, u32[]{:S(2)}, u32[]{:S(2)}) collective-permute-start(bf16[24,3712]{1,0:T(8,128)(2,1)S(1)} %collective-permute-done.5.refs_3_), channel_id=1, source_target_pairs={{0,8},{8,0},{1,9},{9,1},{2,10},{10,2},{3,11},{11,3},{4,12},{12,4},... | collective-permute-start | bytes 534536 | tf_op jit(solution)/shard_map/ppermute | solution.py:283
  27.0 11.8 %collective-permute-start.11 = (bf16[24,3712]{1,0:T(8,128)(2,1)S(1)}, bf16[24,3712]{1,0:T(8,128)(2,1)S(1)}, u32[]{:S(2)}, u32[]{:S(2)}) collective-permute-start(bf16[24,3712]{1,0:T(8,128)(2,1)S(1)} %collective-permute-done.2.refs_0_), channel_id=1, source_target_pairs={{0,8},{8,0},{1,9},{9,1},{2,10},{10,2},{3,11},{11,3},{4,12},{12,4},... | collective-permute-start | bytes 534536 | tf_op jit(solution)/shard_map/ppermute | solution.py:283
  27.0 11.7 %collective-permute-start.10 = (bf16[24,3712]{1,0:T(8,128)(2,1)S(1)}, bf16[24,3712]{1,0:T(8,128)(2,1)S(1)}, u32[]{:S(2)}, u32[]{:S(2)}) collective-permute-start(bf16[24,3712]{1,0:T(8,128)(2,1)S(1)} %collective-permute-done.5.refs_3_), channel_id=1, source_target_pairs={{0,1},{1,0},{2,3},{3,2},{4,5},{5,4},{6,7},{7,6},{8,9},{9,8},{10,11... | collective-permute-start | bytes 534536 | tf_op jit(solution)/shard_map/ppermute | solution.py:287
  30.1 8.7 %collective-permute-start.12 = (bf16[24,3712]{1,0:T(8,128)(2,1)S(1)}, bf16[24,3712]{1,0:T(8,128)(2,1)S(1)}, u32[]{:S(2)}, u32[]{:S(2)}) collective-permute-start(bf16[24,3712]{1,0:T(8,128)(2,1)S(1)} %collective-permute-done.3.refs_1_), channel_id=1, source_target_pairs={{0,8},{8,0},{1,9},{9,1},{2,10},{10,2},{3,11},{11,3},{4,12},{12,4},... | collective-permute-start | bytes 534536 | tf_op jit(solution)/shard_map/ppermute | solution.py:283
  30.1 8.7 %collective-permute-start.13 = (bf16[24,3712]{1,0:T(8,128)(2,1)S(1)}, bf16[24,3712]{1,0:T(8,128)(2,1)S(1)}, u32[]{:S(2)}, u32[]{:S(2)}) collective-permute-start(bf16[24,3712]{1,0:T(8,128)(2,1)S(1)} %collective-permute-done.4.refs_2_), channel_id=1, source_target_pairs={{0,8},{8,0},{1,9},{9,1},{2,10},{10,2},{3,11},{11,3},{4,12},{12,4},... | collective-permute-start | bytes 534536 | tf_op jit(solution)/shard_map/ppermute | solution.py:283
  38.7 1.5 %collective-permute-start.14 = (bf16[24,3712]{1,0:T(8,128)(2,1)S(1)}, bf16[24,3712]{1,0:T(8,128)(2,1)S(1)}, u32[]{:S(2)}, u32[]{:S(2)}) collective-permute-start(bf16[24,3712]{1,0:T(8,128)(2,1)S(1)} %collective-permute-done.10.refs_3_), channel_id=1, source_target_pairs={{0,8},{8,0},{1,9},{9,1},{2,10},{10,2},{3,11},{11,3},{4,12},{12,4},... | collective-permute-start | bytes 534536 | tf_op jit(solution)/shard_map/ppermute | solution.py:283
  52.8 2.6 %collective-permute-start.15 = (bf16[192,2560]{1,0:T(8,128)(2,1)S(1)}, bf16[192,2560]{1,0:T(8,128)(2,1)S(1)}, u32[]{:S(2)}, u32[]{:S(2)}) collective-permute-start(bf16[192,2560]{1,0:T(8,128)(2,1)S(1)} %get-tuple-element.41), channel_id=1, source_target_pairs={{0,8},{8,0},{1,9},{9,1},{2,10},{10,2},{3,11},{11,3},{4,12},{12,4},... | collective-permute-start | bytes 2949128 | tf_op jit(solution)/shard_map/ppermute | solution.py:283
  59.1 1.8 %collective-permute-start.17 = (bf16[192,1024]{1,0:T(8,128)(2,1)S(1)}, bf16[192,1024]{1,0:T(8,128)(2,1)S(1)}, u32[]{:S(2)}, u32[]{:S(2)}) collective-permute-start(bf16[192,1024]{1,0:T(8,128)(2,1)S(1)} %get-tuple-element.48), channel_id=1, source_target_pairs={{0,8},{8,0},{1,9},{9,1},{2,10},{10,2},{3,11},{11,3},{4,12},{12,4},... | collective-permute-start | bytes 1179656 | tf_op jit(solution)/shard_map/ppermute | solution.py:283
  59.3 13.5 %collective-permute-start.16 = (bf16[96,2560]{1,0:T(8,128)(2,1)S(1)}, bf16[96,2560]{1,0:T(8,128)(2,1)S(1)}, u32[]{:S(2)}, u32[]{:S(2)}) collective-permute-start(bf16[96,2560]{1,0:T(8,128)(2,1)S(1)} %add_convert_fusion), channel_id=1, source_target_pairs={{0,1},{1,0},{2,3},{3,2},{4,5},{5,4},{6,7},{7,6},{8,9},{9,8},{10,11... | collective-permute-start | bytes 1474568 | tf_op jit(solution)/shard_map/ppermute | solution.py:287
  61.1 11.7 %collective-permute-start.20 = (bf16[2,24,1024]{2,1,0:T(8,128)(2,1)S(1)}, bf16[2,24,1024]{2,1,0:T(8,128)(2,1)S(1)}, u32[]{:S(2)}, u32[]{:S(2)}) collective-permute-start(bf16[2,24,1024]{2,1,0:T(8,128)(2,1)S(1)} %get-tuple-element.60), channel_id=1, source_target_pairs={{0,2},{1,3},{2,0},{3,1},{4,6},{5,7},{6,4},{7,5},{8,10},{9,11},{10,... | collective-permute-start | bytes 294920 | tf_op jit(solution)/shard_map/ppermute | solution.py:287
  61.2 11.7 %collective-permute-start.19 = (bf16[2,24,1024]{2,1,0:T(8,128)(2,1)S(1)}, bf16[2,24,1024]{2,1,0:T(8,128)(2,1)S(1)}, u32[]{:S(2)}, u32[]{:S(2)}) collective-permute-start(bf16[2,24,1024]{2,1,0:T(8,128)(2,1)S(1)} %get-tuple-element.61), channel_id=1, source_target_pairs={{0,4},{1,5},{2,6},{3,7},{4,0},{5,1},{6,2},{7,3},{8,12},{9,13},{10,... | collective-permute-start | bytes 294920 | tf_op jit(solution)/shard_map/ppermute | solution.py:287
  62.3 10.5 %collective-permute-start.18 = (bf16[2,24,1024]{2,1,0:T(8,128)(2,1)S(1)}, bf16[2,24,1024]{2,1,0:T(8,128)(2,1)S(1)}, u32[]{:S(2)}, u32[]{:S(2)}) collective-permute-start(bf16[2,24,1024]{2,1,0:T(8,128)(2,1)S(1)} %get-tuple-element.62), channel_id=1, source_target_pairs={{0,6},{1,7},{2,4},{3,5},{4,2},{5,3},{6,0},{7,1},{8,14},{9,15},{10,... | collective-permute-start | bytes 294920 | tf_op jit(solution)/shard_map/ppermute | solution.py:287
  72.9 5.3 %collective-permute-start.24 = (bf16[24,1024]{1,0:T(8,128)(2,1)S(1)}, bf16[24,1024]{1,0:T(8,128)(2,1)S(1)}, u32[]{:S(2)}, u32[]{:S(2)}) collective-permute-start(bf16[24,1024]{1,0:T(8,128)(2,1)S(1)} %fusion.8), channel_id=1, source_target_pairs={{0,1},{1,0},{2,3},{3,2},{4,5},{5,4},{6,7},{7,6},{8,9},{9,8},{10,11... | collective-permute-start | bytes 147464 | tf_op jit(solution)/shard_map/ppermute | solution.py:287
  73.7 8.1 %collective-permute-start.21 = (bf16[24,2560]{1,0:T(8,128)(2,1)S(1)}, bf16[24,2560]{1,0:T(8,128)(2,1)S(1)}, u32[]{:S(2)}, u32[]{:S(2)}) collective-permute-start(bf16[24,2560]{1,0:T(8,128)(2,1)S(1)} %get-tuple-element.57), channel_id=1, source_target_pairs={{0,6},{1,7},{2,4},{3,5},{4,2},{5,3},{6,0},{7,1},{8,14},{9,15},{10,... | collective-permute-start | bytes 368648 | tf_op jit(solution)/shard_map/ppermute | solution.py:287
  74.6 7.5 %collective-permute-start.23 = (bf16[24,2560]{1,0:T(8,128)(2,1)S(1)}, bf16[24,2560]{1,0:T(8,128)(2,1)S(1)}, u32[]{:S(2)}, u32[]{:S(2)}) collective-permute-start(bf16[24,2560]{1,0:T(8,128)(2,1)S(1)} %get-tuple-element.58), channel_id=1, source_target_pairs={{0,2},{1,3},{2,0},{3,1},{4,6},{5,7},{6,4},{7,5},{8,10},{9,11},{10,... | collective-permute-start | bytes 368648 | tf_op jit(solution)/shard_map/ppermute | solution.py:287
  75.5 11.2 %collective-permute-start.22 = (bf16[24,2560]{1,0:T(8,128)(2,1)S(1)}, bf16[24,2560]{1,0:T(8,128)(2,1)S(1)}, u32[]{:S(2)}, u32[]{:S(2)}) collective-permute-start(bf16[24,2560]{1,0:T(8,128)(2,1)S(1)} %get-tuple-element.59), channel_id=1, source_target_pairs={{0,4},{1,5},{2,6},{3,7},{4,0},{5,1},{6,2},{7,3},{8,12},{9,13},{10,... | collective-permute-start | bytes 368648 | tf_op jit(solution)/shard_map/ppermute | solution.py:287

commit v3 on v2

--- a/solution.py
+++ b/solution.py
@@ -10,19 +10,26 @@
 LANES = 128
 MIB = 1024 * 1024
 TILE = 512
+SLOTS = 4
 VMEM = pl.BlockSpec(memory_space=pltpu.VMEM)
 HBM = pl.BlockSpec(memory_space=pltpu.HBM)
 SMEM = pl.BlockSpec(memory_space=pltpu.SMEM)
 
 
-def send_kernel(experts, rows_ref, ids_ref, scores_ref, out_ref):
-    sigmoid_vals = jax.nn.sigmoid(scores_ref[...])
+def send_kernel(experts, rows_hbm, ids_hbm, scores_hbm, out_ref, rows, ids, scores, sems):
+    pairs = ((rows_hbm, rows), (ids_hbm, ids), (scores_hbm, scores))
+    copies = [pltpu.make_async_copy(*pair, sems.at[i]) for i, pair in enumerate(pairs)]
+    for copy in copies:
+        copy.start()
+    copies[1].wait()
+    copies[2].wait()
+    sigmoid_vals = jax.nn.sigmoid(scores[...])
     weights = 2.5 * sigmoid_vals / jnp.sum(sigmoid_vals, axis=0, keepdims=True)
     top, count = weights.shape
     expert = lax.broadcasted_iota(jnp.int32, (experts, count), 0)
     dense = jnp.zeros((experts, count), jnp.float32)
     for k in range(top):
-        dense += jnp.where(expert == ids_ref[k : k + 1, :], weights[k : k + 1, :], 0.0)
+        dense += jnp.where(expert == ids[k : k + 1, :], weights[k : k + 1, :], 0.0)
     high = lax.reduce_precision(dense, 8, 7)
     rest = jnp.zeros((LANES - 2 * experts, count), jnp.float32)
     table = jnp.concatenate([high, dense - high, rest]).astype(jnp.bfloat16)
@@ -34,21 +41,28 @@
         (((1,), (1,)), ((), ())),
         preferred_element_type=jnp.float32,
     )
-    width = rows_ref.shape[1]
-    out_ref[:, :width] = rows_ref[...]
+    width = rows.shape[1]
     out_ref[:, width:] = columns.astype(jnp.bfloat16)
+    copies[0].wait()
+    out_ref[:, :width] = rows[...]
 
 
 def with_routing(rows, expert_ids, gate_scores, experts):
     count, width = rows.shape
+    arrays = [
+        pltpu.with_memory_space_constraint(array, pltpu.HBM)
+        for array in (rows, expert_ids.T, gate_scores.T)
+    ]
     return pl.pallas_call(
         functools.partial(send_kernel, experts),
-        in_specs=[VMEM] * 3,
+        in_specs=[HBM] * 3,
         out_specs=VMEM,
         out_shape=jax.ShapeDtypeStruct((count, width + LANES), jnp.bfloat16),
+        scratch_shapes=[pltpu.VMEM(array.shape, array.dtype) for array in arrays]
+        + [pltpu.SemaphoreType.DMA((3,))],
         compiler_params=pltpu.CompilerParams(vmem_limit_bytes=4 * MIB),
         name="with_routing",
-    )(rows, expert_ids.T, gate_scores.T)
+    )(*arrays)
 
 
 def weight_of(columns, expert, experts):
@@ -146,10 +160,18 @@
     for copy in copies:
         copy.start()
     columns = assemble(rows, x)
+    ahead = local_experts // 2
+
+    def gate_of(l):
+        gates[:, l * width : (l + 1) * width] = jnp.dot(
+            x[...], gate_w[l], preferred_element_type=jnp.float32
+        )
+
+    for l in range(ahead):
+        gate_of(l)
     for l in range(local_experts):
-        part = slice(l * width, (l + 1) * width)
-        gates[:, part] = jnp.dot(x[...], gate_w[l], preferred_element_type=jnp.float32)
-    for l in range(local_experts):
+        if l + ahead < local_experts:
+            gate_of(l + ahead)
         part = slice(l * width, (l + 1) * width)
         weight = weight_of(columns, index_ref[0] * local_experts + l, experts)
         copies[l].wait()
@@ -184,99 +206,81 @@
     )(inner_index, *blocks, w_gate, w_up)
 
 
-def fetch(source_ref, first, block_ref, sems):
+def tile_copies(source_ref, slots_ref, sems):
     copies = []
-    for at in range(0, block_ref.shape[2], TILE):
-        size = min(TILE, block_ref.shape[2] - at)
+    for at in range(0, source_ref.shape[2], TILE):
+        slot = at // TILE % slots_ref.shape[0]
         copy = pltpu.make_async_copy(
-            source_ref.at[:, :, pl.ds(first + at, size)],
-            block_ref.at[:, :, pl.ds(at, size)],
-            sems.at[at // TILE],
+            source_ref.at[:, :, pl.ds(at, TILE)], slots_ref.at[slot], sems.at[slot]
         )
+        copies.append((at, slot, copy))
+    return copies
+
+
+def far_kernel(experts, blocks, cut, index_ref, *refs):
+    rows, rest = refs[:blocks], refs[blocks:]
+    gate_w, up_w, near, down_w, own_a, near_a, far_a, own_b, other_b = rest[:9]
+    x, hidden, slots, sems = rest[9:]
+    local_experts, _, width = gate_w.shape
+    copies = tile_copies(down_w, slots, sems)
+    for _, _, copy in copies[:SLOTS]:
         copy.start()
-        copies.append((at, size, copy))
-    return copies
-
-
-def down_into(copies, hidden_ref, block_ref, near_out, far_out, other_out):
-    half = near_out.shape[0]
-    for at, size, copy in copies:
-        copy.wait()
-        block = block_ref[:, :, at : at + size].reshape(-1, size)
-        value = jnp.dot(hidden_ref[...], block, preferred_element_type=jnp.float32)
-        value = value.astype(jnp.bfloat16)
-        near_out[:, at : at + size] = value[:half]
-        other_out[:half, at : at + size] = value[half : 2 * half]
-        far_out[:, at : at + size] = value[2 * half : 3 * half]
-        other_out[half:, at : at + size] = value[3 * half :]
-
-
-def far_kernel(experts, blocks, index_ref, *refs):
-    rows, rest = refs[:blocks], refs[blocks:]
-    gate_w, up_w, near, down_w, hidden, near_out, far_out, other_out, x, block, sems = rest
-    local_experts, _, width = gate_w.shape
-    copies = fetch(down_w, 0, block, sems)
     columns = assemble(rows, x)
     count = near.shape[0]
+    half = count // 2
     hidden[:count] = near[...]
     for l in range(local_experts):
         weight = weight_of(columns, index_ref[0] * local_experts + l, experts)
         hidden[count:, l * width : (l + 1) * width] = hidden_of(
             x[...], gate_w[l], up_w[l], weight
         )
-    down_into(copies, hidden, block, near_out, far_out, other_out)
-
-
-def down_kernel(first, hidden, down_w, near_out, far_out, other_out, block, sems):
-    down_into(
-        fetch(down_w, first, block, sems), hidden, block, near_out, far_out, other_out
-    )
-
-
-def sums(half, columns):
-    return [
-        jax.ShapeDtypeStruct((rows, columns), jnp.bfloat16) for rows in (half, half, 2 * half)
-    ]
-
-
-def tiles(local_experts, width, columns):
-    return [
-        pltpu.VMEM((local_experts, width, columns), jnp.bfloat16),
-        pltpu.SemaphoreType.DMA((pl.cdiv(columns, TILE),)),
-    ]
+    for i, (at, slot, copy) in enumerate(copies):
+        copy.wait()
+        value = jnp.dot(
+            hidden[...],
+            slots[slot].reshape(-1, TILE),
+            preferred_element_type=jnp.float32,
+        ).astype(jnp.bfloat16)
+        if i + SLOTS < len(copies):
+            copies[i + SLOTS][2].start()
+        own, start = (own_a, 0) if at < cut else (own_b, cut)
+        to = slice(at - start, at - start + TILE)
+        own[:half, to] = value[:half]
+        own[half:, to] = value[count : count + half]
+        if at < cut:
+            near_a[:, to] = value[half:count]
+            far_a[:, to] = value[count + half :]
+        else:
+            other_b[:half, to] = value[half:count]
+            other_b[half:, to] = value[count + half :]
 
 
 def far_rows(blocks, w_gate, w_up, near, w_down, inner_index, experts, cut):
     count, depth = near.shape
     local_experts, width, model_width = w_down.shape
     return pl.pallas_call(
-        functools.partial(far_kernel, experts, len(blocks)),
+        functools.partial(far_kernel, experts, len(blocks), cut),
         in_specs=[SMEM] + [VMEM] * (len(blocks) + 3) + [HBM],
-        out_specs=[VMEM] * 4,
-        out_shape=[jax.ShapeDtypeStruct((2 * count, depth), near.dtype)]
-        + sums(count // 2, cut),
-        scratch_shapes=[pltpu.VMEM((count, model_width), jnp.bfloat16)]
-        + tiles(local_experts, width, cut),
-        compiler_params=pltpu.CompilerParams(vmem_limit_bytes=15 * MIB),
+        out_specs=[VMEM] * 5,
+        out_shape=[
+            jax.ShapeDtypeStruct(shape, jnp.bfloat16)
+            for shape in (
+                (count, cut),
+                (count // 2, cut),
+                (count // 2, cut),
+                (count, model_width - cut),
+                (count, model_width - cut),
+            )
+        ],
+        scratch_shapes=[
+            pltpu.VMEM((count, model_width), jnp.bfloat16),
+            pltpu.VMEM((2 * count, depth), jnp.bfloat16),
+            pltpu.VMEM((SLOTS, local_experts, width, TILE), w_down.dtype),
+            pltpu.SemaphoreType.DMA((SLOTS,)),
+        ],
+        compiler_params=pltpu.CompilerParams(vmem_limit_bytes=14 * MIB),
         name="far_rows",
     )(inner_index, *blocks, w_gate, w_up, near, w_down)
-
-
-def down(hidden, w_down, first):
-    local_experts, width, model_width = w_down.shape
-    columns = model_width - first
-    return pl.pallas_call(
-        functools.partial(down_kernel, first),
-        in_specs=[VMEM, HBM],
-        out_specs=[VMEM] * 3,
-        out_shape=sums(hidden.shape[0] // 4, columns),
-        scratch_shapes=tiles(local_experts, width, columns),
-        compiler_params=pltpu.CompilerParams(vmem_limit_bytes=15 * MIB),
-        cost_estimate=pl.CostEstimate(
-            flops=2 * hidden.size * columns, bytes_accessed=0, transcendentals=0
-        ),
-        name="down",
-    )(hidden, w_down)
 
 
 def swap_core(value):
@@ -319,38 +323,29 @@
     near = [own, z1, z2, z3]
     near += [swap_core(block) for block in near]
     hidden, w_up = near_rows(near, w_gate, w_up, inner_index, experts)
-    hidden, y3 = tie(hidden, y3)
+    hidden, y2, y3 = tie(hidden, y2, y3)
     far = [y0, y1, y2, y3]
     far += [swap_core(block) for block in far]
 
     cut = (model_width // LANES * 5 // 7) * LANES
-    group = 4 * count
-
-    def rows(step):
-        return slice(step * count, (step + 1) * count)
-
-    hidden, near_a, far_a, other_a = far_rows(
+    own_a, near_a, far_a, own_b, other_b = far_rows(
         far, w_gate, w_up, hidden, w_down, inner_index, experts, cut
     )
-    other_a = swap_core(other_a)
-    far_a = (wide(far_a) + wide(other_a[group:])).astype(jnp.bfloat16)
-    far_a, hidden = tie(far_a, hidden)
+    group = 4 * count
+    far_a = (wide(own_a[group:]) + wide(swap_core(far_a))).astype(jnp.bfloat16)
+    near_a = wide(own_a[:group]) + wide(swap_core(near_a))
     across = swap_inner(far_a, 1)
-    near_b, far_b, other_b = down(hidden, w_down, cut)
-    other_b = swap_core(other_b)
-
-    both = jnp.stack([near_b, far_b]).reshape(2, 4, count, -1)
-    both = wide(both) + wide(other_b.reshape(2, 4, count, -1))
+    both = (wide(own_b) + wide(swap_core(other_b))).reshape(2, 4, count, -1)
     sent_b = [swap_inner(both[:, step].astype(jnp.bfloat16), 2 * step) for step in (3, 2, 1)]
     across, *sent_b = tie(across, *sent_b)
-
-    total_a = wide(near_a) + wide(other_a[:group]) + wide(across)
+    sums_a = near_a + wide(across)
     sent_a = [
-        swap_inner(total_a[rows(step)].astype(jnp.bfloat16), 2 * step) for step in (3, 2, 1)
+        swap_inner(sums_a[at * count : (at + 1) * count].astype(jnp.bfloat16), 2 * at)
+        for at in (3, 2, 1)
     ]
     sum_b = sum((wide(block) for block in sent_b), both[:, 0])
     sum_b = sum_b[0] + wide(swap_inner(sum_b[1].astype(jnp.bfloat16), 1))
-    sum_a = sum((wide(block) for block in sent_a), total_a[rows(0)])
+    sum_a = sum((wide(block) for block in sent_a), sums_a[:count])
     return jnp.concatenate([sum_a, sum_b], axis=1).astype(jnp.bfloat16)
 
 

time: 87.6 us -> 82 us (0.936)
  waiting for transfers between devices: 29.9 us -> 27 us
  local copies, waits for them, and re-layouts: 2.35 us -> 0.07 us
  Pallas kernels: 29.6 us -> 28 us
  starting transfers between devices: 24.1 us -> 25.4 us
    ppermute x10 -> x11, waiting for transfers between devices: 4.86 us -> 2.53 us  [swap_core(): return lax.ppermute(value, 'outer', [(0, 1), (1, 0)])]
    unnamed x6 -> x0, local copies, waits for them, and re-layouts: 2.29 us -> none
    pallas_call x3 -> x2, Pallas kernels: 16.3 us -> 15.5 us  [the longest x1 14.5 us: far_rows(): pl.pallas_call(functools.partial(far_kernel, experts, len(blocks), cut),...]
    ppermute x10 -> x11, starting transfers between devices: 1.24 us -> 1.83 us  [swap_core(): return lax.ppermute(value, 'outer', [(0, 1), (1, 0)])]
  transfers between devices with their start and end apart: 25 -> 26, of which waited for: 12 -> 13; matrix products, arithmetic and copies ran while one was open for 0% -> 1% of each run, Pallas kernels for 15% -> 15%
where the time goes in v3:
time: 82 us; the launch traced here: 81.8 us
  Pallas kernels  28 us (34%)
  waiting for transfers between devices  27 us (33%)
  starting transfers between devices  25.4 us (31%)
  other arithmetic  1.2 us (1%)
    ppermute x15, waiting for transfers between devices, swap_inner(): return lax.ppermute(value, 'inner', [(i, i ^ bit) for i in range(8)])  24.5 us
    ppermute x15, starting transfers between devices, swap_inner(): return lax.ppermute(value, 'inner', [(i, i ^ bit) for i in range(8)])  23.5 us
    pallas_call x1, Pallas kernels, far_rows(): pl.pallas_call(functools.partial(far_kernel, experts, len(blocks), cut),...  14.5 us
    pallas_call x1, Pallas kernels, near_rows(): pl.pallas_call(functools.partial(near_kernel, experts, len(blocks)), in_s...  7.35 us
    pallas_call x1, Pallas kernels, load(): pl.pallas_call(load_kernel, in_specs=[pl.BlockSpec(memory_space=pltpu.HBM...  5.18 us
    ppermute x11, waiting for transfers between devices, swap_core(): return lax.ppermute(value, 'outer', [(0, 1), (1, 0)])  2.53 us
    ppermute x11, starting transfers between devices, swap_core(): return lax.ppermute(value, 'outer', [(0, 1), (1, 0)])  1.83 us
  transfers between devices with their start and end apart: 26, of which 13 were waited for; matrix products, arithmetic and copies ran while one was open for 1% of the time, Pallas kernels for 15%

profile of v3, /device:TPU:0, one launch (start us, length us, event | category | flops | bytes accessed | tf_op | source)
XLA Modules:
  0.0 81.8 jit_solution(12787497417306700521)
XLA Ops:
  0.0 1.0 %with_routing.1.refs_0_ = bf16[24,3712]{1,0:T(8,128)(2,1)S(1)} custom-call(bf16[24,3584]{1,0:T(8,128)(2,1)} %rows_hbm.1, s32[8,24]{1,0:T(8,128)} %bitcast.28, f32[8,24]{1,0:T(8,128)} %bitcast.29), custom_call_target="tpu_custom_call" | custom-call | tf_op jit(solution)/shard_map/with_routing/pallas_call | solution.py:56
  1.0 3.0 %collective-permute-start.2 = (bf16[24,3712]{1,0:T(8,128)(2,1)S(1)}, bf16[24,3712]{1,0:T(8,128)(2,1)S(1)}, u32[]{:S(2)}, u32[]{:S(2)}) collective-permute-start(bf16[24,3712]{1,0:T(8,128)(2,1)S(1)} %with_routing.1.refs_0_), channel_id=1, source_target_pairs={{0,1},{1,0},{2,3},{3,2},{4,5},{5,4},{6,7},{7,6},{8,9},{9,8},{10,11... | collective-permute-start | bytes 534536 | tf_op jit(solution)/shard_map/ppermute | solution.py:291
  4.0 2.6 %collective-permute-start.1 = (bf16[24,3712]{1,0:T(8,128)(2,1)S(1)}, bf16[24,3712]{1,0:T(8,128)(2,1)S(1)}, u32[]{:S(2)}, u32[]{:S(2)}) collective-permute-start(bf16[24,3712]{1,0:T(8,128)(2,1)S(1)} %with_routing.1.refs_0_), channel_id=1, source_target_pairs={{0,4},{1,5},{2,6},{3,7},{4,0},{5,1},{6,2},{7,3},{8,12},{9,13},{10,... | collective-permute-start | bytes 534536 | tf_op jit(solution)/shard_map/ppermute | solution.py:291
  6.6 1.6 %collective-permute-start = (bf16[24,3712]{1,0:T(8,128)(2,1)S(1)}, bf16[24,3712]{1,0:T(8,128)(2,1)S(1)}, u32[]{:S(2)}, u32[]{:S(2)}) collective-permute-start(bf16[24,3712]{1,0:T(8,128)(2,1)S(1)} %with_routing.1.refs_0_), channel_id=1, source_target_pairs={{0,2},{1,3},{2,0},{3,1},{4,6},{5,7},{6,4},{7,5},{8,10},{9,11},{10,... | collective-permute-start | bytes 534536 | tf_op jit(solution)/shard_map/ppermute | solution.py:291
  8.2 5.2 %load.1.refs_8_ = bf16[4,3584,512]{2,1,0:T(8,128)(2,1)S(1)} custom-call(bf16[4,3584,512]{2,1,0:T(8,128)(2,1)} %source_ref.1), custom_call_target="tpu_custom_call" | custom-call | bytes 29360128 | tf_op jit(solution)/shard_map/load/pallas_call | solution.py:134
  13.4 1.4 %collective-permute-done.1.refs_2_ = bf16[24,3712]{1,0:T(8,128)(2,1)S(1)} collective-permute-done((bf16[24,3712]{1,0:T(8,128)(2,1)S(1)}, bf16[24,3712]{1,0:T(8,128)(2,1)S(1)}, u32[]{:S(2)}, u32[]{:S(2)}) %collective-permute-start.1) | collective-permute-done | bytes 178208 | tf_op jit(solution)/shard_map/ppermute | solution.py:291
  14.8 0.2 collective-permute-done.refs_1_
  15.0 3.2 %collective-permute-start.4 = (bf16[24,3712]{1,0:T(8,128)(2,1)S(1)}, bf16[24,3712]{1,0:T(8,128)(2,1)S(1)}, u32[]{:S(2)}, u32[]{:S(2)}) collective-permute-start(bf16[24,3712]{1,0:T(8,128)(2,1)S(1)} %with_routing.1.refs_0_), channel_id=1, source_target_pairs={{0,6},{1,7},{2,4},{3,5},{4,2},{5,3},{6,0},{7,1},{8,14},{9,15},{10,... | collective-permute-start | bytes 534536 | tf_op jit(solution)/shard_map/ppermute | solution.py:291
  18.2 0.0 collective-permute-start.6
  18.2 0.5 collective-permute-start.3
  18.7 0.2 collective-permute-start.5
  18.9 0.3 collective-permute-start.7
  19.2 3.8 %collective-permute-done.4.refs_3_ = bf16[24,3712]{1,0:T(8,128)(2,1)S(1)} collective-permute-done((bf16[24,3712]{1,0:T(8,128)(2,1)S(1)}, bf16[24,3712]{1,0:T(8,128)(2,1)S(1)}, u32[]{:S(2)}, u32[]{:S(2)}) %collective-permute-start.4) | collective-permute-done | bytes 178208 | tf_op jit(solution)/shard_map/ppermute | solution.py:291
  23.0 0.0 collective-permute-start.8
  23.0 0.0 collective-permute-done.6.refs_5_
  23.0 0.5 collective-permute-start.9
  23.5 1.6 %collective-permute-done.3.refs_1_ = bf16[24,3712]{1,0:T(8,128)(2,1)S(1)} collective-permute-done((bf16[24,3712]{1,0:T(8,128)(2,1)S(1)}, bf16[24,3712]{1,0:T(8,128)(2,1)S(1)}, u32[]{:S(2)}, u32[]{:S(2)}) %collective-permute-start.3) | collective-permute-done | bytes 178208 | tf_op jit(solution)/shard_map/ppermute | solution.py:291
  25.1 0.5 collective-permute-start.10
  25.7 0.2 collective-permute-start.12
  25.9 7.3 %near_rows.1 = (bf16[192,2048]{1,0:T(8,128)(2,1)S(1)}, bf16[4,3584,512]{2,1,0:T(8,128)(2,1)S(1)}) custom-call(s32[1]{0:T(128)} %bitcast.2.index_ref, bf16[24,3712]{1,0:T(8,128)(2,1)S(1)} %with_routing.1.refs_0_, bf16[24,3712]{1,0:T(8,128)(2,1)S(1)} %collective-permute-done.refs_1_, bf16[24,3712]{1,0:T(8,128)(2,1)S(1)} %collective-permute-done.1.refs_2_, ...), custom_call_target="tpu_custom_call" | custom-call | flops 5637144576 | tf_op jit(solution)/shard_map/near_rows/pallas_call | solution.py:186
  33.2 0.0 collective-permute-done.9.refs_2_
  33.2 0.5 collective-permute-done.10.refs_3_
  33.8 0.5 collective-permute-start.14
  34.3 0.0 collective-permute-done.12.refs_5_
  34.3 0.9 %collective-permute-done.13.refs_6_ = bf16[24,3712]{1,0:T(8,128)(2,1)S(1)} collective-permute-done((bf16[24,3712]{1,0:T(8,128)(2,1)S(1)}, bf16[24,3712]{1,0:T(8,128)(2,1)S(1)}, u32[]{:S(2)}, u32[]{:S(2)}) %collective-permute-start.13) | collective-permute-done | bytes 178208 | tf_op jit(solution)/shard_map/ppermute | solution.py:287
  35.2 0.3 collective-permute-done.14.refs_7_
  35.4 14.5 %far_rows.1 = (bf16[192,2560]{1,0:T(8,128)(2,1)S(1)}, bf16[96,2560]{1,0:T(8,128)(2,1)S(1)}, bf16[96,2560]{1,0:T(8,128)(2,1)S(1)}, bf16[192,1024]{1,0:T(8,128)(2,1)S(1)}, bf16[192,1024]{1,0:T(8,128)(2,1)S(1)}) custom-call(s32[1]{0:T(128)} %bitcast.2.index_ref, bf16[24,3712]{1,0:T(8,128)(2,1)S(1)} %collective-permute-done.2.refs_0_, ...), custom_call_target="tpu_custom_call" | custom-call | tf_op jit(solution)/shard_map/far_rows/pallas_call | solution.py:261
  50.0 0.3 collective-permute-start.16
  50.3 0.3 collective-permute-start.18
  50.5 1.4 %collective-permute-done.16 = bf16[96,2560]{1,0:T(8,128)(2,1)S(1)} collective-permute-done((bf16[96,2560]{1,0:T(8,128)(2,1)S(1)}, bf16[96,2560]{1,0:T(8,128)(2,1)S(1)}, u32[]{:S(2)}, u32[]{:S(2)}) %collective-permute-start.16) | collective-permute-done | bytes 491552 | tf_op jit(solution)/shard_map/ppermute | solution.py:287
  51.9 0.1 add_convert_fusion
  52.0 1.2 %collective-permute-start.17 = (bf16[96,2560]{1,0:T(8,128)(2,1)S(1)}, bf16[96,2560]{1,0:T(8,128)(2,1)S(1)}, u32[]{:S(2)}, u32[]{:S(2)}) collective-permute-start(bf16[96,2560]{1,0:T(8,128)(2,1)S(1)} %add_convert_fusion), channel_id=1, source_target_pairs={{0,1},{1,0},{2,3},{3,2},{4,5},{5,4},{6,7},{7,6},{8,9},{9,8},{10,11... | collective-permute-start | bytes 1474568 | tf_op jit(solution)/shard_map/ppermute | solution.py:291
  53.2 0.1 convert_add_fusion.1
  53.4 2.1 %collective-permute-start.21 = (bf16[2,24,1024]{2,1,0:T(8,128)(2,1)S(1)}, bf16[2,24,1024]{2,1,0:T(8,128)(2,1)S(1)}, u32[]{:S(2)}, u32[]{:S(2)}) collective-permute-start(bf16[2,24,1024]{2,1,0:T(8,128)(2,1)S(1)} %get-tuple-element.52), channel_id=1, source_target_pairs={{0,2},{1,3},{2,0},{3,1},{4,6},{5,7},{6,4},{7,5},{8,10},{9,11},{10,... | collective-permute-start | bytes 294920 | tf_op jit(solution)/shard_map/ppermute | solution.py:291
  55.4 1.5 %collective-permute-start.20 = (bf16[2,24,1024]{2,1,0:T(8,128)(2,1)S(1)}, bf16[2,24,1024]{2,1,0:T(8,128)(2,1)S(1)}, u32[]{:S(2)}, u32[]{:S(2)}) collective-permute-start(bf16[2,24,1024]{2,1,0:T(8,128)(2,1)S(1)} %get-tuple-element.53), channel_id=1, source_target_pairs={{0,4},{1,5},{2,6},{3,7},{4,0},{5,1},{6,2},{7,3},{8,12},{9,13},{10,... | collective-permute-start | bytes 294920 | tf_op jit(solution)/shard_map/ppermute | solution.py:291
  56.9 1.0 %collective-permute-start.19 = (bf16[2,24,1024]{2,1,0:T(8,128)(2,1)S(1)}, bf16[2,24,1024]{2,1,0:T(8,128)(2,1)S(1)}, u32[]{:S(2)}, u32[]{:S(2)}) collective-permute-start(bf16[2,24,1024]{2,1,0:T(8,128)(2,1)S(1)} %get-tuple-element.54), channel_id=1, source_target_pairs={{0,6},{1,7},{2,4},{3,5},{4,2},{5,3},{6,0},{7,1},{8,14},{9,15},{10,... | collective-permute-start | bytes 294920 | tf_op jit(solution)/shard_map/ppermute | solution.py:291
  57.9 0.7 collective-permute-done.21
  58.6 7.1 %collective-permute-done.20 = bf16[2,24,1024]{2,1,0:T(8,128)(2,1)S(1)} collective-permute-done((bf16[2,24,1024]{2,1,0:T(8,128)(2,1)S(1)}, bf16[2,24,1024]{2,1,0:T(8,128)(2,1)S(1)}, u32[]{:S(2)}, u32[]{:S(2)}) %collective-permute-start.20) | collective-permute-done | bytes 98336 | tf_op jit(solution)/shard_map/ppermute | solution.py:291
  65.8 1.4 %collective-permute-start.25 = (bf16[24,1024]{1,0:T(8,128)(2,1)S(1)}, bf16[24,1024]{1,0:T(8,128)(2,1)S(1)}, u32[]{:S(2)}, u32[]{:S(2)}) collective-permute-start(bf16[24,1024]{1,0:T(8,128)(2,1)S(1)} %fusion.8), channel_id=1, source_target_pairs={{0,1},{1,0},{2,3},{3,2},{4,5},{5,4},{6,7},{7,6},{8,9},{9,8},{10,11... | collective-permute-start | bytes 147464 | tf_op jit(solution)/shard_map/ppermute | solution.py:291
  67.3 0.2 fusion.9
  67.5 2.4 %collective-permute-start.22 = (bf16[24,2560]{1,0:T(8,128)(2,1)S(1)}, bf16[24,2560]{1,0:T(8,128)(2,1)S(1)}, u32[]{:S(2)}, u32[]{:S(2)}) collective-permute-start(bf16[24,2560]{1,0:T(8,128)(2,1)S(1)} %get-tuple-element.49), channel_id=1, source_target_pairs={{0,6},{1,7},{2,4},{3,5},{4,2},{5,3},{6,0},{7,1},{8,14},{9,15},{10,... | collective-permute-start | bytes 368648 | tf_op jit(solution)/shard_map/ppermute | solution.py:291
  69.9 0.0 collective-permute-start.24
  70.0 2.0 %collective-permute-start.23 = (bf16[24,2560]{1,0:T(8,128)(2,1)S(1)}, bf16[24,2560]{1,0:T(8,128)(2,1)S(1)}, u32[]{:S(2)}, u32[]{:S(2)}) collective-permute-start(bf16[24,2560]{1,0:T(8,128)(2,1)S(1)} %get-tuple-element.51), channel_id=1, source_target_pairs={{0,4},{1,5},{2,6},{3,7},{4,0},{5,1},{6,2},{7,3},{8,12},{9,13},{10,... | collective-permute-start | bytes 368648 | tf_op jit(solution)/shard_map/ppermute | solution.py:291
  72.0 3.6 %collective-permute-done.22 = bf16[24,2560]{1,0:T(8,128)(2,1)S(1)} collective-permute-done((bf16[24,2560]{1,0:T(8,128)(2,1)S(1)}, bf16[24,2560]{1,0:T(8,128)(2,1)S(1)}, u32[]{:S(2)}, u32[]{:S(2)}) %collective-permute-start.22) | collective-permute-done | bytes 122912 | tf_op jit(solution)/shard_map/ppermute | solution.py:291
  75.6 0.3 collective-permute-done.24
  75.9 5.2 %collective-permute-done.23 = bf16[24,2560]{1,0:T(8,128)(2,1)S(1)} collective-permute-done((bf16[24,2560]{1,0:T(8,128)(2,1)S(1)}, bf16[24,2560]{1,0:T(8,128)(2,1)S(1)}, u32[]{:S(2)}, u32[]{:S(2)}) %collective-permute-start.23) | collective-permute-done | bytes 122912 | tf_op jit(solution)/shard_map/ppermute | solution.py:291
  81.1 0.1 fusion.2
  81.2 0.7 pad_maximum_fusion
  (18 shorter events, 0.2 us)
Async XLA Ops:
  1.0 12.4 %collective-permute-start.2 = (bf16[24,3712]{1,0:T(8,128)(2,1)S(1)}, bf16[24,3712]{1,0:T(8,128)(2,1)S(1)}, u32[]{:S(2)}, u32[]{:S(2)}) collective-permute-start(bf16[24,3712]{1,0:T(8,128)(2,1)S(1)} %with_routing.1.refs_0_), channel_id=1, source_target_pairs={{0,1},{1,0},{2,3},{3,2},{4,5},{5,4},{6,7},{7,6},{8,9},{9,8},{10,11... | collective-permute-start | bytes 534536 | tf_op jit(solution)/shard_map/ppermute | solution.py:291
  4.0 10.8 %collective-permute-start.1 = (bf16[24,3712]{1,0:T(8,128)(2,1)S(1)}, bf16[24,3712]{1,0:T(8,128)(2,1)S(1)}, u32[]{:S(2)}, u32[]{:S(2)}) collective-permute-start(bf16[24,3712]{1,0:T(8,128)(2,1)S(1)} %with_routing.1.refs_0_), channel_id=1, source_target_pairs={{0,4},{1,5},{2,6},{3,7},{4,0},{5,1},{6,2},{7,3},{8,12},{9,13},{10,... | collective-permute-start | bytes 534536 | tf_op jit(solution)/shard_map/ppermute | solution.py:291
  6.6 8.4 %collective-permute-start = (bf16[24,3712]{1,0:T(8,128)(2,1)S(1)}, bf16[24,3712]{1,0:T(8,128)(2,1)S(1)}, u32[]{:S(2)}, u32[]{:S(2)}) collective-permute-start(bf16[24,3712]{1,0:T(8,128)(2,1)S(1)} %with_routing.1.refs_0_), channel_id=1, source_target_pairs={{0,2},{1,3},{2,0},{3,1},{4,6},{5,7},{6,4},{7,5},{8,10},{9,11},{10,... | collective-permute-start | bytes 534536 | tf_op jit(solution)/shard_map/ppermute | solution.py:291
  15.0 8.0 %collective-permute-start.4 = (bf16[24,3712]{1,0:T(8,128)(2,1)S(1)}, bf16[24,3712]{1,0:T(8,128)(2,1)S(1)}, u32[]{:S(2)}, u32[]{:S(2)}) collective-permute-start(bf16[24,3712]{1,0:T(8,128)(2,1)S(1)} %with_routing.1.refs_0_), channel_id=1, source_target_pairs={{0,6},{1,7},{2,4},{3,5},{4,2},{5,3},{6,0},{7,1},{8,14},{9,15},{10,... | collective-permute-start | bytes 534536 | tf_op jit(solution)/shard_map/ppermute | solution.py:291
  18.2 4.8 %collective-permute-start.6 = (bf16[24,3712]{1,0:T(8,128)(2,1)S(1)}, bf16[24,3712]{1,0:T(8,128)(2,1)S(1)}, u32[]{:S(2)}, u32[]{:S(2)}) collective-permute-start(bf16[24,3712]{1,0:T(8,128)(2,1)S(1)} %collective-permute-done.refs_1_), channel_id=1, source_target_pairs={{0,8},{8,0},{1,9},{9,1},{2,10},{10,2},{3,11},{11,3},{4,12},{12,4},... | collective-permute-start | bytes 534536 | tf_op jit(solution)/shard_map/ppermute | solution.py:287
  18.2 6.9 %collective-permute-start.3 = (bf16[24,3712]{1,0:T(8,128)(2,1)S(1)}, bf16[24,3712]{1,0:T(8,128)(2,1)S(1)}, u32[]{:S(2)}, u32[]{:S(2)}) collective-permute-start(bf16[24,3712]{1,0:T(8,128)(2,1)S(1)} %collective-permute-done.refs_1_), channel_id=1, source_target_pairs={{0,1},{1,0},{2,3},{3,2},{4,5},{5,4},{6,7},{7,6},{8,9},{9,8},{10,11... | collective-permute-start | bytes 534536 | tf_op jit(solution)/shard_map/ppermute | solution.py:291
  18.7 6.4 %collective-permute-start.5 = (bf16[24,3712]{1,0:T(8,128)(2,1)S(1)}, bf16[24,3712]{1,0:T(8,128)(2,1)S(1)}, u32[]{:S(2)}, u32[]{:S(2)}) collective-permute-start(bf16[24,3712]{1,0:T(8,128)(2,1)S(1)} %with_routing.1.refs_0_), channel_id=1, source_target_pairs={{0,8},{8,0},{1,9},{9,1},{2,10},{10,2},{3,11},{11,3},{4,12},{12,4},... | collective-permute-start | bytes 534536 | tf_op jit(solution)/shard_map/ppermute | solution.py:287
  18.9 6.7 %collective-permute-start.7 = (bf16[24,3712]{1,0:T(8,128)(2,1)S(1)}, bf16[24,3712]{1,0:T(8,128)(2,1)S(1)}, u32[]{:S(2)}, u32[]{:S(2)}) collective-permute-start(bf16[24,3712]{1,0:T(8,128)(2,1)S(1)} %collective-permute-done.1.refs_2_), channel_id=1, source_target_pairs={{0,8},{8,0},{1,9},{9,1},{2,10},{10,2},{3,11},{11,3},{4,12},{12,4},... | collective-permute-start | bytes 534536 | tf_op jit(solution)/shard_map/ppermute | solution.py:287
  23.0 2.9 %collective-permute-start.8 = (bf16[24,3712]{1,0:T(8,128)(2,1)S(1)}, bf16[24,3712]{1,0:T(8,128)(2,1)S(1)}, u32[]{:S(2)}, u32[]{:S(2)}) collective-permute-start(bf16[24,3712]{1,0:T(8,128)(2,1)S(1)} %collective-permute-done.4.refs_3_), channel_id=1, source_target_pairs={{0,8},{8,0},{1,9},{9,1},{2,10},{10,2},{3,11},{11,3},{4,12},{12,4},... | collective-permute-start | bytes 534536 | tf_op jit(solution)/shard_map/ppermute | solution.py:287
  23.0 10.2 %collective-permute-start.9 = (bf16[24,3712]{1,0:T(8,128)(2,1)S(1)}, bf16[24,3712]{1,0:T(8,128)(2,1)S(1)}, u32[]{:S(2)}, u32[]{:S(2)}) collective-permute-start(bf16[24,3712]{1,0:T(8,128)(2,1)S(1)} %collective-permute-done.1.refs_2_), channel_id=1, source_target_pairs={{0,1},{1,0},{2,3},{3,2},{4,5},{5,4},{6,7},{7,6},{8,9},{9,8},{10,11... | collective-permute-start | bytes 534536 | tf_op jit(solution)/shard_map/ppermute | solution.py:291
  25.1 9.1 %collective-permute-start.11 = (bf16[24,3712]{1,0:T(8,128)(2,1)S(1)}, bf16[24,3712]{1,0:T(8,128)(2,1)S(1)}, u32[]{:S(2)}, u32[]{:S(2)}) collective-permute-start(bf16[24,3712]{1,0:T(8,128)(2,1)S(1)} %collective-permute-done.2.refs_0_), channel_id=1, source_target_pairs={{0,8},{8,0},{1,9},{9,1},{2,10},{10,2},{3,11},{11,3},{4,12},{12,4},... | collective-permute-start | bytes 534536 | tf_op jit(solution)/shard_map/ppermute | solution.py:287
  25.1 8.6 %collective-permute-start.10 = (bf16[24,3712]{1,0:T(8,128)(2,1)S(1)}, bf16[24,3712]{1,0:T(8,128)(2,1)S(1)}, u32[]{:S(2)}, u32[]{:S(2)}) collective-permute-start(bf16[24,3712]{1,0:T(8,128)(2,1)S(1)} %collective-permute-done.4.refs_3_), channel_id=1, source_target_pairs={{0,1},{1,0},{2,3},{3,2},{4,5},{5,4},{6,7},{7,6},{8,9},{9,8},{10,11... | collective-permute-start | bytes 534536 | tf_op jit(solution)/shard_map/ppermute | solution.py:291
  25.7 8.6 %collective-permute-start.12 = (bf16[24,3712]{1,0:T(8,128)(2,1)S(1)}, bf16[24,3712]{1,0:T(8,128)(2,1)S(1)}, u32[]{:S(2)}, u32[]{:S(2)}) collective-permute-start(bf16[24,3712]{1,0:T(8,128)(2,1)S(1)} %collective-permute-done.3.refs_1_), channel_id=1, source_target_pairs={{0,8},{8,0},{1,9},{9,1},{2,10},{10,2},{3,11},{11,3},{4,12},{12,4},... | collective-permute-start | bytes 534536 | tf_op jit(solution)/shard_map/ppermute | solution.py:287
  33.7 1.4 %collective-permute-start.13 = (bf16[24,3712]{1,0:T(8,128)(2,1)S(1)}, bf16[24,3712]{1,0:T(8,128)(2,1)S(1)}, u32[]{:S(2)}, u32[]{:S(2)}) collective-permute-start(bf16[24,3712]{1,0:T(8,128)(2,1)S(1)} %collective-permute-done.9.refs_2_), channel_id=1, source_target_pairs={{0,8},{8,0},{1,9},{9,1},{2,10},{10,2},{3,11},{11,3},{4,12},{12,4},... | collective-permute-start | bytes 534536 | tf_op jit(solution)/shard_map/ppermute | solution.py:287
  33.8 1.7 %collective-permute-start.14 = (bf16[24,3712]{1,0:T(8,128)(2,1)S(1)}, bf16[24,3712]{1,0:T(8,128)(2,1)S(1)}, u32[]{:S(2)}, u32[]{:S(2)}) collective-permute-start(bf16[24,3712]{1,0:T(8,128)(2,1)S(1)} %collective-permute-done.10.refs_3_), channel_id=1, source_target_pairs={{0,8},{8,0},{1,9},{9,1},{2,10},{10,2},{3,11},{11,3},{4,12},{12,4},... | collective-permute-start | bytes 534536 | tf_op jit(solution)/shard_map/ppermute | solution.py:287
  50.0 1.9 %collective-permute-start.16 = (bf16[96,2560]{1,0:T(8,128)(2,1)S(1)}, bf16[96,2560]{1,0:T(8,128)(2,1)S(1)}, u32[]{:S(2)}, u32[]{:S(2)}) collective-permute-start(bf16[96,2560]{1,0:T(8,128)(2,1)S(1)} %get-tuple-element.40), channel_id=1, source_target_pairs={{0,8},{8,0},{1,9},{9,1},{2,10},{10,2},{3,11},{11,3},{4,12},{12,4},... | collective-permute-start | bytes 1474568 | tf_op jit(solution)/shard_map/ppermute | solution.py:287
  50.3 2.9 %collective-permute-start.18 = (bf16[192,1024]{1,0:T(8,128)(2,1)S(1)}, bf16[192,1024]{1,0:T(8,128)(2,1)S(1)}, u32[]{:S(2)}, u32[]{:S(2)}) collective-permute-start(bf16[192,1024]{1,0:T(8,128)(2,1)S(1)} %get-tuple-element.42), channel_id=1, source_target_pairs={{0,8},{8,0},{1,9},{9,1},{2,10},{10,2},{3,11},{11,3},{4,12},{12,4},... | collective-permute-start | bytes 1179656 | tf_op jit(solution)/shard_map/ppermute | solution.py:287
  52.0 13.7 %collective-permute-start.17 = (bf16[96,2560]{1,0:T(8,128)(2,1)S(1)}, bf16[96,2560]{1,0:T(8,128)(2,1)S(1)}, u32[]{:S(2)}, u32[]{:S(2)}) collective-permute-start(bf16[96,2560]{1,0:T(8,128)(2,1)S(1)} %add_convert_fusion), channel_id=1, source_target_pairs={{0,1},{1,0},{2,3},{3,2},{4,5},{5,4},{6,7},{7,6},{8,9},{9,8},{10,11... | collective-permute-start | bytes 1474568 | tf_op jit(solution)/shard_map/ppermute | solution.py:291
  53.4 5.2 %collective-permute-start.21 = (bf16[2,24,1024]{2,1,0:T(8,128)(2,1)S(1)}, bf16[2,24,1024]{2,1,0:T(8,128)(2,1)S(1)}, u32[]{:S(2)}, u32[]{:S(2)}) collective-permute-start(bf16[2,24,1024]{2,1,0:T(8,128)(2,1)S(1)} %get-tuple-element.52), channel_id=1, source_target_pairs={{0,2},{1,3},{2,0},{3,1},{4,6},{5,7},{6,4},{7,5},{8,10},{9,11},{10,... | collective-permute-start | bytes 294920 | tf_op jit(solution)/shard_map/ppermute | solution.py:291
  55.4 10.3 %collective-permute-start.20 = (bf16[2,24,1024]{2,1,0:T(8,128)(2,1)S(1)}, bf16[2,24,1024]{2,1,0:T(8,128)(2,1)S(1)}, u32[]{:S(2)}, u32[]{:S(2)}) collective-permute-start(bf16[2,24,1024]{2,1,0:T(8,128)(2,1)S(1)} %get-tuple-element.53), channel_id=1, source_target_pairs={{0,4},{1,5},{2,6},{3,7},{4,0},{5,1},{6,2},{7,3},{8,12},{9,13},{10,... | collective-permute-start | bytes 294920 | tf_op jit(solution)/shard_map/ppermute | solution.py:291
  56.9 8.9 %collective-permute-start.19 = (bf16[2,24,1024]{2,1,0:T(8,128)(2,1)S(1)}, bf16[2,24,1024]{2,1,0:T(8,128)(2,1)S(1)}, u32[]{:S(2)}, u32[]{:S(2)}) collective-permute-start(bf16[2,24,1024]{2,1,0:T(8,128)(2,1)S(1)} %get-tuple-element.54), channel_id=1, source_target_pairs={{0,6},{1,7},{2,4},{3,5},{4,2},{5,3},{6,0},{7,1},{8,14},{9,15},{10,... | collective-permute-start | bytes 294920 | tf_op jit(solution)/shard_map/ppermute | solution.py:291
  57.9 9.4 %collective-permute-start.15 = (bf16[96,2560]{1,0:T(8,128)(2,1)S(1)}, bf16[96,2560]{1,0:T(8,128)(2,1)S(1)}, u32[]{:S(2)}, u32[]{:S(2)}) collective-permute-start(bf16[96,2560]{1,0:T(8,128)(2,1)S(1)} %get-tuple-element.39), channel_id=1, source_target_pairs={{0,8},{8,0},{1,9},{9,1},{2,10},{10,2},{3,11},{11,3},{4,12},{12,4},... | collective-permute-start | bytes 1474568 | tf_op jit(solution)/shard_map/ppermute | solution.py:287
  65.8 6.1 %collective-permute-start.25 = (bf16[24,1024]{1,0:T(8,128)(2,1)S(1)}, bf16[24,1024]{1,0:T(8,128)(2,1)S(1)}, u32[]{:S(2)}, u32[]{:S(2)}) collective-permute-start(bf16[24,1024]{1,0:T(8,128)(2,1)S(1)} %fusion.8), channel_id=1, source_target_pairs={{0,1},{1,0},{2,3},{3,2},{4,5},{5,4},{6,7},{7,6},{8,9},{9,8},{10,11... | collective-permute-start | bytes 147464 | tf_op jit(solution)/shard_map/ppermute | solution.py:291
  67.5 8.1 %collective-permute-start.22 = (bf16[24,2560]{1,0:T(8,128)(2,1)S(1)}, bf16[24,2560]{1,0:T(8,128)(2,1)S(1)}, u32[]{:S(2)}, u32[]{:S(2)}) collective-permute-start(bf16[24,2560]{1,0:T(8,128)(2,1)S(1)} %get-tuple-element.49), channel_id=1, source_target_pairs={{0,6},{1,7},{2,4},{3,5},{4,2},{5,3},{6,0},{7,1},{8,14},{9,15},{10,... | collective-permute-start | bytes 368648 | tf_op jit(solution)/shard_map/ppermute | solution.py:291
  69.9 6.0 %collective-permute-start.24 = (bf16[24,2560]{1,0:T(8,128)(2,1)S(1)}, bf16[24,2560]{1,0:T(8,128)(2,1)S(1)}, u32[]{:S(2)}, u32[]{:S(2)}) collective-permute-start(bf16[24,2560]{1,0:T(8,128)(2,1)S(1)} %get-tuple-element.50), channel_id=1, source_target_pairs={{0,2},{1,3},{2,0},{3,1},{4,6},{5,7},{6,4},{7,5},{8,10},{9,11},{10,... | collective-permute-start | bytes 368648 | tf_op jit(solution)/shard_map/ppermute | solution.py:291
  70.0 11.1 %collective-permute-start.23 = (bf16[24,2560]{1,0:T(8,128)(2,1)S(1)}, bf16[24,2560]{1,0:T(8,128)(2,1)S(1)}, u32[]{:S(2)}, u32[]{:S(2)}) collective-permute-start(bf16[24,2560]{1,0:T(8,128)(2,1)S(1)} %get-tuple-element.51), channel_id=1, source_target_pairs={{0,4},{1,5},{2,6},{3,7},{4,0},{5,1},{6,2},{7,3},{8,12},{9,13},{10,... | collective-permute-start | bytes 368648 | tf_op jit(solution)/shard_map/ppermute | solution.py:291

commit v4 on v3

--- a/solution.py
+++ b/solution.py
@@ -219,8 +219,8 @@
 
 def far_kernel(experts, blocks, cut, index_ref, *refs):
     rows, rest = refs[:blocks], refs[blocks:]
-    gate_w, up_w, near, down_w, own_a, near_a, far_a, own_b, other_b = rest[:9]
-    x, hidden, slots, sems = rest[9:]
+    gate_w, up_w, near, down_w, own, other, high_a, high_b = rest[:8]
+    x, hidden, slots, sems = rest[8:]
     local_experts, _, width = gate_w.shape
     copies = tile_copies(down_w, slots, sems)
     for _, _, copy in copies[:SLOTS]:
@@ -243,16 +243,16 @@
         ).astype(jnp.bfloat16)
         if i + SLOTS < len(copies):
             copies[i + SLOTS][2].start()
-        own, start = (own_a, 0) if at < cut else (own_b, cut)
-        to = slice(at - start, at - start + TILE)
+        to = slice(at, at + TILE)
         own[:half, to] = value[:half]
         own[half:, to] = value[count : count + half]
+        other[:half, to] = value[half:count]
+        value = value[count + half :]
+        other[half:, to] = value[: half // 2]
         if at < cut:
-            near_a[:, to] = value[half:count]
-            far_a[:, to] = value[count + half :]
+            high_a[:, to] = value[half // 2 :]
         else:
-            other_b[:half, to] = value[half:count]
-            other_b[half:, to] = value[count + half :]
+            high_b[:, at - cut : at - cut + TILE] = value[half // 2 :]
 
 
 def far_rows(blocks, w_gate, w_up, near, w_down, inner_index, experts, cut):
@@ -261,15 +261,14 @@
     return pl.pallas_call(
         functools.partial(far_kernel, experts, len(blocks), cut),
         in_specs=[SMEM] + [VMEM] * (len(blocks) + 3) + [HBM],
-        out_specs=[VMEM] * 5,
+        out_specs=[VMEM] * 4,
         out_shape=[
             jax.ShapeDtypeStruct(shape, jnp.bfloat16)
             for shape in (
-                (count, cut),
-                (count // 2, cut),
-                (count // 2, cut),
-                (count, model_width - cut),
-                (count, model_width - cut),
+                (count, model_width),
+                (count * 3 // 4, model_width),
+                (count // 4, cut),
+                (count // 4, model_width - cut),
             )
         ],
         scratch_shapes=[
@@ -327,26 +326,44 @@
     far = [y0, y1, y2, y3]
     far += [swap_core(block) for block in far]
 
-    cut = (model_width // LANES * 5 // 7) * LANES
-    own_a, near_a, far_a, own_b, other_b = far_rows(
+    cut = (model_width // LANES * 6 // 7) * LANES
+    own, other, high_a, high_b = far_rows(
         far, w_gate, w_up, hidden, w_down, inner_index, experts, cut
     )
-    group = 4 * count
-    far_a = (wide(own_a[group:]) + wide(swap_core(far_a))).astype(jnp.bfloat16)
-    near_a = wide(own_a[:group]) + wide(swap_core(near_a))
-    across = swap_inner(far_a, 1)
-    both = (wide(own_b) + wide(swap_core(other_b))).reshape(2, 4, count, -1)
-    sent_b = [swap_inner(both[:, step].astype(jnp.bfloat16), 2 * step) for step in (3, 2, 1)]
-    across, *sent_b = tie(across, *sent_b)
-    sums_a = near_a + wide(across)
-    sent_a = [
-        swap_inner(sums_a[at * count : (at + 1) * count].astype(jnp.bfloat16), 2 * at)
-        for at in (3, 2, 1)
+    half = 4 * count
+    middle = half + 2 * count
+    high_a = (wide(own[middle:, :cut]) + wide(swap_core(high_a))).astype(jnp.bfloat16)
+    high_a, other = tie(high_a, other)
+    across = swap_inner(high_a, 1)
+    other = wide(own[:middle]) + wide(swap_core(other))
+    near, low = other[:half].reshape(4, count, model_width), other[half:]
+
+    def together(near_rows, far_rows):
+        return jnp.concatenate([near_rows, far_rows]).astype(jnp.bfloat16)
+
+    first, high_b = tie(together(near[1], low[count:]), high_b)
+    one = swap_inner(first, 2)
+    high_b = wide(own[middle:, cut:]) + wide(swap_core(high_b))
+    high_b = high_b.reshape(2, count, -1)
+    two, three = (
+        swap_inner(together(near[2 + i][:, cut:], high_b[i]), 4 + 2 * i) for i in (0, 1)
+    )
+    sent = [
+        swap_inner(
+            (near[2 + i][:, :cut] + wide(across[i * count : (i + 1) * count])).astype(
+                jnp.bfloat16
+            ),
+            4 + 2 * i,
+        )
+        for i in (0, 1)
     ]
-    sum_b = sum((wide(block) for block in sent_b), both[:, 0])
-    sum_b = sum_b[0] + wide(swap_inner(sum_b[1].astype(jnp.bfloat16), 1))
-    sum_a = sum((wide(block) for block in sent_a), sums_a[:count])
-    return jnp.concatenate([sum_a, sum_b], axis=1).astype(jnp.bfloat16)
+    rest = wide(two) + wide(three)
+    back = low[:count] + wide(one[count:])
+    back = jnp.concatenate([back[:, :cut], back[:, cut:] + rest[count:]], axis=1)
+    back = swap_inner(back.astype(jnp.bfloat16), 1)
+    total = near[0] + wide(one[:count]) + wide(back)
+    along = jnp.concatenate([wide(sent[0]) + wide(sent[1]), rest[:count]], axis=1)
+    return (total + along).astype(jnp.bfloat16)
 
 
 def solution(mesh):

time: 82 us -> 78.6 us (0.959)
  waiting for transfers between devices: 27 us -> 22.8 us
    ppermute x15 -> x14, waiting for transfers between devices: 24.5 us -> 19.1 us  [swap_inner(): return lax.ppermute(value, 'inner', [(i, i ^ bit) for i in range(8)])]
    ppermute x11, waiting for transfers between devices: 2.53 us -> 3.76 us  [swap_core(): return lax.ppermute(value, 'outer', [(0, 1), (1, 0)])]
    ppermute x15 -> x14, starting transfers between devices: 23.5 us -> 23.6 us  [swap_inner(): return lax.ppermute(value, 'inner', [(i, i ^ bit) for i in range(8)])]
  transfers between devices with their start and end apart: 26 -> 25, of which waited for: 13 -> 13; matrix products, arithmetic and copies ran while one was open for 1% -> 1% of each run, Pallas kernels for 15% -> 16%
where the time goes in v4:
time: 78.6 us; the launch traced here: 78.2 us
  Pallas kernels  28.1 us (36%)
  starting transfers between devices  25.8 us (33%)
  waiting for transfers between devices  22.8 us (29%)
  other arithmetic  1.35 us (2%)
    ppermute x14, starting transfers between devices, swap_inner(): return lax.ppermute(value, 'inner', [(i, i ^ bit) for i in range(8)])  23.6 us
    ppermute x14, waiting for transfers between devices, swap_inner(): return lax.ppermute(value, 'inner', [(i, i ^ bit) for i in range(8)])  19.1 us
    pallas_call x1, Pallas kernels, far_rows(): pl.pallas_call(functools.partial(far_kernel, experts, len(blocks), cut),...  14.5 us
    pallas_call x1, Pallas kernels, near_rows(): pl.pallas_call(functools.partial(near_kernel, experts, len(blocks)), in_s...  7.35 us
    pallas_call x1, Pallas kernels, load(): pl.pallas_call(load_kernel, in_specs=[pl.BlockSpec(memory_space=pltpu.HBM...  5.18 us
    ppermute x11, waiting for transfers between devices, swap_core(): return lax.ppermute(value, 'outer', [(0, 1), (1, 0)])  3.76 us
    ppermute x11, starting transfers between devices, swap_core(): return lax.ppermute(value, 'outer', [(0, 1), (1, 0)])  2.18 us
  transfers between devices with their start and end apart: 25, of which 13 were waited for; matrix products, arithmetic and copies ran while one was open for 1% of the time, Pallas kernels for 16%

profile of v4, /device:TPU:0, one launch (start us, length us, event | category | flops | bytes accessed | tf_op | source)
XLA Modules:
  0.0 78.2 jit_solution(5997232085718017956)
XLA Ops:
  0.0 1.0 %with_routing.1.refs_0_ = bf16[24,3712]{1,0:T(8,128)(2,1)S(1)} custom-call(bf16[24,3584]{1,0:T(8,128)(2,1)} %rows_hbm.1, s32[8,24]{1,0:T(8,128)} %bitcast.3, f32[8,24]{1,0:T(8,128)} %bitcast.4), custom_call_target="tpu_custom_call" | custom-call | tf_op jit(solution)/shard_map/with_routing/pallas_call | solution.py:56
  1.0 3.0 %collective-permute-start.2 = (bf16[24,3712]{1,0:T(8,128)(2,1)S(1)}, bf16[24,3712]{1,0:T(8,128)(2,1)S(1)}, u32[]{:S(2)}, u32[]{:S(2)}) collective-permute-start(bf16[24,3712]{1,0:T(8,128)(2,1)S(1)} %with_routing.1.refs_0_), channel_id=1, source_target_pairs={{0,1},{1,0},{2,3},{3,2},{4,5},{5,4},{6,7},{7,6},{8,9},{9,8},{10,11... | collective-permute-start | bytes 534536 | tf_op jit(solution)/shard_map/ppermute | solution.py:290
  4.0 2.6 %collective-permute-start.1 = (bf16[24,3712]{1,0:T(8,128)(2,1)S(1)}, bf16[24,3712]{1,0:T(8,128)(2,1)S(1)}, u32[]{:S(2)}, u32[]{:S(2)}) collective-permute-start(bf16[24,3712]{1,0:T(8,128)(2,1)S(1)} %with_routing.1.refs_0_), channel_id=1, source_target_pairs={{0,4},{1,5},{2,6},{3,7},{4,0},{5,1},{6,2},{7,3},{8,12},{9,13},{10,... | collective-permute-start | bytes 534536 | tf_op jit(solution)/shard_map/ppermute | solution.py:290
  6.6 1.6 %collective-permute-start = (bf16[24,3712]{1,0:T(8,128)(2,1)S(1)}, bf16[24,3712]{1,0:T(8,128)(2,1)S(1)}, u32[]{:S(2)}, u32[]{:S(2)}) collective-permute-start(bf16[24,3712]{1,0:T(8,128)(2,1)S(1)} %with_routing.1.refs_0_), channel_id=1, source_target_pairs={{0,2},{1,3},{2,0},{3,1},{4,6},{5,7},{6,4},{7,5},{8,10},{9,11},{10,... | collective-permute-start | bytes 534536 | tf_op jit(solution)/shard_map/ppermute | solution.py:290
  8.2 5.2 %load.1.refs_8_ = bf16[4,3584,512]{2,1,0:T(8,128)(2,1)S(1)} custom-call(bf16[4,3584,512]{2,1,0:T(8,128)(2,1)} %source_ref.1), custom_call_target="tpu_custom_call" | custom-call | bytes 29360128 | tf_op jit(solution)/shard_map/load/pallas_call | solution.py:134
  13.4 0.0 collective-permute-done.2.refs_0_
  13.4 1.4 %collective-permute-done.1.refs_2_ = bf16[24,3712]{1,0:T(8,128)(2,1)S(1)} collective-permute-done((bf16[24,3712]{1,0:T(8,128)(2,1)S(1)}, bf16[24,3712]{1,0:T(8,128)(2,1)S(1)}, u32[]{:S(2)}, u32[]{:S(2)}) %collective-permute-start.1) | collective-permute-done | bytes 178208 | tf_op jit(solution)/shard_map/ppermute | solution.py:290
  14.8 0.2 collective-permute-done.refs_1_
  15.0 3.2 %collective-permute-start.4 = (bf16[24,3712]{1,0:T(8,128)(2,1)S(1)}, bf16[24,3712]{1,0:T(8,128)(2,1)S(1)}, u32[]{:S(2)}, u32[]{:S(2)}) collective-permute-start(bf16[24,3712]{1,0:T(8,128)(2,1)S(1)} %with_routing.1.refs_0_), channel_id=1, source_target_pairs={{0,6},{1,7},{2,4},{3,5},{4,2},{5,3},{6,0},{7,1},{8,14},{9,15},{10,... | collective-permute-start | bytes 534536 | tf_op jit(solution)/shard_map/ppermute | solution.py:290
  18.2 0.5 collective-permute-start.3
  18.7 0.2 collective-permute-start.5
  18.9 0.3 collective-permute-start.7
  19.2 3.8 %collective-permute-done.4.refs_3_ = bf16[24,3712]{1,0:T(8,128)(2,1)S(1)} collective-permute-done((bf16[24,3712]{1,0:T(8,128)(2,1)S(1)}, bf16[24,3712]{1,0:T(8,128)(2,1)S(1)}, u32[]{:S(2)}, u32[]{:S(2)}) %collective-permute-start.4) | collective-permute-done | bytes 178208 | tf_op jit(solution)/shard_map/ppermute | solution.py:290
  23.0 0.5 collective-permute-start.9
  23.5 1.6 %collective-permute-done.3.refs_1_ = bf16[24,3712]{1,0:T(8,128)(2,1)S(1)} collective-permute-done((bf16[24,3712]{1,0:T(8,128)(2,1)S(1)}, bf16[24,3712]{1,0:T(8,128)(2,1)S(1)}, u32[]{:S(2)}, u32[]{:S(2)}) %collective-permute-start.3) | collective-permute-done | bytes 178208 | tf_op jit(solution)/shard_map/ppermute | solution.py:290
  25.1 0.0 collective-permute-start.11
  25.1 0.0 collective-permute-done.5.refs_4_
  25.1 0.5 collective-permute-start.10
  25.6 0.0 collective-permute-done.7.refs_6_
  25.7 0.2 collective-permute-start.12
  25.9 7.3 %near_rows.1 = (bf16[192,2048]{1,0:T(8,128)(2,1)S(1)}, bf16[4,3584,512]{2,1,0:T(8,128)(2,1)S(1)}) custom-call(s32[1]{0:T(128)} %bitcast.2.index_ref, bf16[24,3712]{1,0:T(8,128)(2,1)S(1)} %with_routing.1.refs_0_, bf16[24,3712]{1,0:T(8,128)(2,1)S(1)} %collective-permute-done.refs_1_, bf16[24,3712]{1,0:T(8,128)(2,1)S(1)} %collective-permute-done.1.refs_2_, ...), custom_call_target="tpu_custom_call" | custom-call | flops 5637144576 | tf_op jit(solution)/shard_map/near_rows/pallas_call | solution.py:186
  33.2 0.0 collective-permute-done.9.refs_2_
  33.2 0.5 collective-permute-done.10.refs_3_
  33.8 0.5 collective-permute-start.14
  34.3 0.0 collective-permute-done.11.refs_4_
  34.3 0.9 %collective-permute-done.13.refs_6_ = bf16[24,3712]{1,0:T(8,128)(2,1)S(1)} collective-permute-done((bf16[24,3712]{1,0:T(8,128)(2,1)S(1)}, bf16[24,3712]{1,0:T(8,128)(2,1)S(1)}, u32[]{:S(2)}, u32[]{:S(2)}) %collective-permute-start.13) | collective-permute-done | bytes 178208 | tf_op jit(solution)/shard_map/ppermute | solution.py:286
  35.2 0.3 collective-permute-done.14.refs_7_
  35.4 14.5 %far_rows.1 = (bf16[192,3584]{1,0:T(8,128)(2,1)S(1)}, bf16[144,3584]{1,0:T(8,128)(2,1)S(1)}, bf16[48,3072]{1,0:T(8,128)(2,1)S(1)}, bf16[48,512]{1,0:T(8,128)(2,1)S(1)}) custom-call(s32[1]{0:T(128)} %bitcast.2.index_ref, bf16[24,3712]{1,0:T(8,128)(2,1)S(1)} %collective-permute-done.2.refs_0_, bf16[24,3712]{1,0:T(8,128)(2,1)S(1)} %collective-permute-done.3.refs_1_, ...), custom_call_target="tpu_custom_call" | custom-call | tf_op jit(solution)/shard_map/far_rows/pallas_call | solution.py:261
  50.0 0.3 collective-permute-start.15
  50.3 1.3 %collective-permute-done.15 = bf16[48,3072]{1,0:T(8,128)(2,1)S(1)} collective-permute-done((bf16[48,3072]{1,0:T(8,128)(2,1)S(1)}, bf16[48,3072]{1,0:T(8,128)(2,1)S(1)}, u32[]{:S(2)}, u32[]{:S(2)}) %collective-permute-start.15) | collective-permute-done | bytes 294944 | tf_op jit(solution)/shard_map/ppermute | solution.py:286
  51.6 0.1 add_convert_fusion
  51.7 0.3 collective-permute-start.16
  52.0 1.1 %collective-permute-start.22 = (bf16[48,3072]{1,0:T(8,128)(2,1)S(1)}, bf16[48,3072]{1,0:T(8,128)(2,1)S(1)}, u32[]{:S(2)}, u32[]{:S(2)}) collective-permute-start(bf16[48,3072]{1,0:T(8,128)(2,1)S(1)} %add_convert_fusion), channel_id=1, source_target_pairs={{0,1},{1,0},{2,3},{3,2},{4,5},{5,4},{6,7},{7,6},{8,9},{9,8},{10,11... | collective-permute-start | bytes 884744 | tf_op jit(solution)/shard_map/ppermute | solution.py:290
  53.1 1.3 %collective-permute-done.16 = bf16[144,3584]{1,0:T(8,128)(2,1)S(1)} collective-permute-done((bf16[144,3584]{1,0:T(8,128)(2,1)S(1)}, bf16[144,3584]{1,0:T(8,128)(2,1)S(1)}, u32[]{:S(2)}, u32[]{:S(2)}) %collective-permute-start.16) | collective-permute-done | bytes 1032224 | tf_op jit(solution)/shard_map/ppermute | solution.py:286
  54.4 0.3 fusion.6
  54.8 0.3 collective-permute-start.18
  55.1 2.6 %collective-permute-start.17 = (bf16[48,3584]{1,0:T(8,128)(2,1)S(1)}, bf16[48,3584]{1,0:T(8,128)(2,1)S(1)}, u32[]{:S(2)}, u32[]{:S(2)}) collective-permute-start(bf16[48,3584]{1,0:T(8,128)(2,1)S(1)} %pad_maximum_fusion), channel_id=1, source_target_pairs={{0,2},{1,3},{2,0},{3,1},{4,6},{5,7},{6,4},{7,5},{8,10},{9,11},{10,... | collective-permute-start | bytes 1032200 | tf_op jit(solution)/shard_map/ppermute | solution.py:290
  57.8 1.9 %collective-permute-start.20 = (bf16[48,512]{1,0:T(8,128)(2,1)S(1)}, bf16[48,512]{1,0:T(8,128)(2,1)S(1)}, u32[]{:S(2)}, u32[]{:S(2)}) collective-permute-start(bf16[48,512]{1,0:T(8,128)(2,1)S(1)} %pad_maximum_fusion.3), channel_id=1, source_target_pairs={{0,6},{1,7},{2,4},{3,5},{4,2},{5,3},{6,0},{7,1},{8,14},{9,15},{10,... | collective-permute-start | bytes 147464 | tf_op jit(solution)/shard_map/ppermute | solution.py:290
  59.7 0.6 collective-permute-start.19
  60.3 0.9 %collective-permute-done.22 = bf16[48,3072]{1,0:T(8,128)(2,1)S(1)} collective-permute-done((bf16[48,3072]{1,0:T(8,128)(2,1)S(1)}, bf16[48,3072]{1,0:T(8,128)(2,1)S(1)}, u32[]{:S(2)}, u32[]{:S(2)}) %collective-permute-start.22) | collective-permute-done | bytes 294944 | tf_op jit(solution)/shard_map/ppermute | solution.py:290
  61.2 0.1 fusion.4
  61.2 1.7 %collective-permute-start.23 = (bf16[24,3072]{1,0:T(8,128)(2,1)S(1)}, bf16[24,3072]{1,0:T(8,128)(2,1)S(1)}, u32[]{:S(2)}, u32[]{:S(2)}) collective-permute-start(bf16[24,3072]{1,0:T(8,128)(2,1)S(1)} %get-tuple-element.47), channel_id=1, source_target_pairs={{0,4},{1,5},{2,6},{3,7},{4,0},{5,1},{6,2},{7,3},{8,12},{9,13},{10,... | collective-permute-start | bytes 442376 | tf_op jit(solution)/shard_map/ppermute | solution.py:290
  62.9 3.4 %collective-permute-start.24 = (bf16[24,3072]{1,0:T(8,128)(2,1)S(1)}, bf16[24,3072]{1,0:T(8,128)(2,1)S(1)}, u32[]{:S(2)}, u32[]{:S(2)}) collective-permute-start(bf16[24,3072]{1,0:T(8,128)(2,1)S(1)} %get-tuple-element.48), channel_id=1, source_target_pairs={{0,6},{1,7},{2,4},{3,5},{4,2},{5,3},{6,0},{7,1},{8,14},{9,15},{10,... | collective-permute-start | bytes 442376 | tf_op jit(solution)/shard_map/ppermute | solution.py:290
  66.3 2.3 %collective-permute-done.20 = bf16[48,512]{1,0:T(8,128)(2,1)S(1)} collective-permute-done((bf16[48,512]{1,0:T(8,128)(2,1)S(1)}, bf16[48,512]{1,0:T(8,128)(2,1)S(1)}, u32[]{:S(2)}, u32[]{:S(2)}) %collective-permute-start.20) | collective-permute-done | bytes 49184 | tf_op jit(solution)/shard_map/ppermute | solution.py:290
  68.6 2.0 %collective-permute-done.17 = bf16[48,3584]{1,0:T(8,128)(2,1)S(1)} collective-permute-done((bf16[48,3584]{1,0:T(8,128)(2,1)S(1)}, bf16[48,3584]{1,0:T(8,128)(2,1)S(1)}, u32[]{:S(2)}, u32[]{:S(2)}) %collective-permute-start.17) | collective-permute-done | bytes 344096 | tf_op jit(solution)/shard_map/ppermute | solution.py:290
  70.7 0.3 collective-permute-start.21
  71.0 6.4 %collective-permute-done.23 = bf16[24,3072]{1,0:T(8,128)(2,1)S(1)} collective-permute-done((bf16[24,3072]{1,0:T(8,128)(2,1)S(1)}, bf16[24,3072]{1,0:T(8,128)(2,1)S(1)}, u32[]{:S(2)}, u32[]{:S(2)}) %collective-permute-start.23) | collective-permute-done | bytes 147488 | tf_op jit(solution)/shard_map/ppermute | solution.py:290
  77.5 0.8 fusion.2
  (23 shorter events, 0.2 us)
Async XLA Ops:
  1.0 12.4 %collective-permute-start.2 = (bf16[24,3712]{1,0:T(8,128)(2,1)S(1)}, bf16[24,3712]{1,0:T(8,128)(2,1)S(1)}, u32[]{:S(2)}, u32[]{:S(2)}) collective-permute-start(bf16[24,3712]{1,0:T(8,128)(2,1)S(1)} %with_routing.1.refs_0_), channel_id=1, source_target_pairs={{0,1},{1,0},{2,3},{3,2},{4,5},{5,4},{6,7},{7,6},{8,9},{9,8},{10,11... | collective-permute-start | bytes 534536 | tf_op jit(solution)/shard_map/ppermute | solution.py:290
  4.0 10.8 %collective-permute-start.1 = (bf16[24,3712]{1,0:T(8,128)(2,1)S(1)}, bf16[24,3712]{1,0:T(8,128)(2,1)S(1)}, u32[]{:S(2)}, u32[]{:S(2)}) collective-permute-start(bf16[24,3712]{1,0:T(8,128)(2,1)S(1)} %with_routing.1.refs_0_), channel_id=1, source_target_pairs={{0,4},{1,5},{2,6},{3,7},{4,0},{5,1},{6,2},{7,3},{8,12},{9,13},{10,... | collective-permute-start | bytes 534536 | tf_op jit(solution)/shard_map/ppermute | solution.py:290
  6.6 8.4 %collective-permute-start = (bf16[24,3712]{1,0:T(8,128)(2,1)S(1)}, bf16[24,3712]{1,0:T(8,128)(2,1)S(1)}, u32[]{:S(2)}, u32[]{:S(2)}) collective-permute-start(bf16[24,3712]{1,0:T(8,128)(2,1)S(1)} %with_routing.1.refs_0_), channel_id=1, source_target_pairs={{0,2},{1,3},{2,0},{3,1},{4,6},{5,7},{6,4},{7,5},{8,10},{9,11},{10,... | collective-permute-start | bytes 534536 | tf_op jit(solution)/shard_map/ppermute | solution.py:290
  15.0 8.0 %collective-permute-start.4 = (bf16[24,3712]{1,0:T(8,128)(2,1)S(1)}, bf16[24,3712]{1,0:T(8,128)(2,1)S(1)}, u32[]{:S(2)}, u32[]{:S(2)}) collective-permute-start(bf16[24,3712]{1,0:T(8,128)(2,1)S(1)} %with_routing.1.refs_0_), channel_id=1, source_target_pairs={{0,6},{1,7},{2,4},{3,5},{4,2},{5,3},{6,0},{7,1},{8,14},{9,15},{10,... | collective-permute-start | bytes 534536 | tf_op jit(solution)/shard_map/ppermute | solution.py:290
  18.2 4.8 %collective-permute-start.6 = (bf16[24,3712]{1,0:T(8,128)(2,1)S(1)}, bf16[24,3712]{1,0:T(8,128)(2,1)S(1)}, u32[]{:S(2)}, u32[]{:S(2)}) collective-permute-start(bf16[24,3712]{1,0:T(8,128)(2,1)S(1)} %collective-permute-done.refs_1_), channel_id=1, source_target_pairs={{0,8},{8,0},{1,9},{9,1},{2,10},{10,2},{3,11},{11,3},{4,12},{12,4},... | collective-permute-start | bytes 534536 | tf_op jit(solution)/shard_map/ppermute | solution.py:286
  18.2 6.9 %collective-permute-start.3 = (bf16[24,3712]{1,0:T(8,128)(2,1)S(1)}, bf16[24,3712]{1,0:T(8,128)(2,1)S(1)}, u32[]{:S(2)}, u32[]{:S(2)}) collective-permute-start(bf16[24,3712]{1,0:T(8,128)(2,1)S(1)} %collective-permute-done.refs_1_), channel_id=1, source_target_pairs={{0,1},{1,0},{2,3},{3,2},{4,5},{5,4},{6,7},{7,6},{8,9},{9,8},{10,11... | collective-permute-start | bytes 534536 | tf_op jit(solution)/shard_map/ppermute | solution.py:290
  18.7 6.4 %collective-permute-start.5 = (bf16[24,3712]{1,0:T(8,128)(2,1)S(1)}, bf16[24,3712]{1,0:T(8,128)(2,1)S(1)}, u32[]{:S(2)}, u32[]{:S(2)}) collective-permute-start(bf16[24,3712]{1,0:T(8,128)(2,1)S(1)} %with_routing.1.refs_0_), channel_id=1, source_target_pairs={{0,8},{8,0},{1,9},{9,1},{2,10},{10,2},{3,11},{11,3},{4,12},{12,4},... | collective-permute-start | bytes 534536 | tf_op jit(solution)/shard_map/ppermute | solution.py:286
  18.9 6.7 %collective-permute-start.7 = (bf16[24,3712]{1,0:T(8,128)(2,1)S(1)}, bf16[24,3712]{1,0:T(8,128)(2,1)S(1)}, u32[]{:S(2)}, u32[]{:S(2)}) collective-permute-start(bf16[24,3712]{1,0:T(8,128)(2,1)S(1)} %collective-permute-done.1.refs_2_), channel_id=1, source_target_pairs={{0,8},{8,0},{1,9},{9,1},{2,10},{10,2},{3,11},{11,3},{4,12},{12,4},... | collective-permute-start | bytes 534536 | tf_op jit(solution)/shard_map/ppermute | solution.py:286
  23.0 2.9 %collective-permute-start.8 = (bf16[24,3712]{1,0:T(8,128)(2,1)S(1)}, bf16[24,3712]{1,0:T(8,128)(2,1)S(1)}, u32[]{:S(2)}, u32[]{:S(2)}) collective-permute-start(bf16[24,3712]{1,0:T(8,128)(2,1)S(1)} %collective-permute-done.4.refs_3_), channel_id=1, source_target_pairs={{0,8},{8,0},{1,9},{9,1},{2,10},{10,2},{3,11},{11,3},{4,12},{12,4},... | collective-permute-start | bytes 534536 | tf_op jit(solution)/shard_map/ppermute | solution.py:286
  23.0 10.2 %collective-permute-start.9 = (bf16[24,3712]{1,0:T(8,128)(2,1)S(1)}, bf16[24,3712]{1,0:T(8,128)(2,1)S(1)}, u32[]{:S(2)}, u32[]{:S(2)}) collective-permute-start(bf16[24,3712]{1,0:T(8,128)(2,1)S(1)} %collective-permute-done.1.refs_2_), channel_id=1, source_target_pairs={{0,1},{1,0},{2,3},{3,2},{4,5},{5,4},{6,7},{7,6},{8,9},{9,8},{10,11... | collective-permute-start | bytes 534536 | tf_op jit(solution)/shard_map/ppermute | solution.py:290
  25.1 9.1 %collective-permute-start.11 = (bf16[24,3712]{1,0:T(8,128)(2,1)S(1)}, bf16[24,3712]{1,0:T(8,128)(2,1)S(1)}, u32[]{:S(2)}, u32[]{:S(2)}) collective-permute-start(bf16[24,3712]{1,0:T(8,128)(2,1)S(1)} %collective-permute-done.2.refs_0_), channel_id=1, source_target_pairs={{0,8},{8,0},{1,9},{9,1},{2,10},{10,2},{3,11},{11,3},{4,12},{12,4},... | collective-permute-start | bytes 534536 | tf_op jit(solution)/shard_map/ppermute | solution.py:286
  25.1 8.6 %collective-permute-start.10 = (bf16[24,3712]{1,0:T(8,128)(2,1)S(1)}, bf16[24,3712]{1,0:T(8,128)(2,1)S(1)}, u32[]{:S(2)}, u32[]{:S(2)}) collective-permute-start(bf16[24,3712]{1,0:T(8,128)(2,1)S(1)} %collective-permute-done.4.refs_3_), channel_id=1, source_target_pairs={{0,1},{1,0},{2,3},{3,2},{4,5},{5,4},{6,7},{7,6},{8,9},{9,8},{10,11... | collective-permute-start | bytes 534536 | tf_op jit(solution)/shard_map/ppermute | solution.py:290
  25.7 8.6 %collective-permute-start.12 = (bf16[24,3712]{1,0:T(8,128)(2,1)S(1)}, bf16[24,3712]{1,0:T(8,128)(2,1)S(1)}, u32[]{:S(2)}, u32[]{:S(2)}) collective-permute-start(bf16[24,3712]{1,0:T(8,128)(2,1)S(1)} %collective-permute-done.3.refs_1_), channel_id=1, source_target_pairs={{0,8},{8,0},{1,9},{9,1},{2,10},{10,2},{3,11},{11,3},{4,12},{12,4},... | collective-permute-start | bytes 534536 | tf_op jit(solution)/shard_map/ppermute | solution.py:286
  33.7 1.4 %collective-permute-start.13 = (bf16[24,3712]{1,0:T(8,128)(2,1)S(1)}, bf16[24,3712]{1,0:T(8,128)(2,1)S(1)}, u32[]{:S(2)}, u32[]{:S(2)}) collective-permute-start(bf16[24,3712]{1,0:T(8,128)(2,1)S(1)} %collective-permute-done.9.refs_2_), channel_id=1, source_target_pairs={{0,8},{8,0},{1,9},{9,1},{2,10},{10,2},{3,11},{11,3},{4,12},{12,4},... | collective-permute-start | bytes 534536 | tf_op jit(solution)/shard_map/ppermute | solution.py:286
  33.8 1.7 %collective-permute-start.14 = (bf16[24,3712]{1,0:T(8,128)(2,1)S(1)}, bf16[24,3712]{1,0:T(8,128)(2,1)S(1)}, u32[]{:S(2)}, u32[]{:S(2)}) collective-permute-start(bf16[24,3712]{1,0:T(8,128)(2,1)S(1)} %collective-permute-done.10.refs_3_), channel_id=1, source_target_pairs={{0,8},{8,0},{1,9},{9,1},{2,10},{10,2},{3,11},{11,3},{4,12},{12,4},... | collective-permute-start | bytes 534536 | tf_op jit(solution)/shard_map/ppermute | solution.py:286
  50.0 1.6 %collective-permute-start.15 = (bf16[48,3072]{1,0:T(8,128)(2,1)S(1)}, bf16[48,3072]{1,0:T(8,128)(2,1)S(1)}, u32[]{:S(2)}, u32[]{:S(2)}) collective-permute-start(bf16[48,3072]{1,0:T(8,128)(2,1)S(1)} %get-tuple-element.38), channel_id=1, source_target_pairs={{0,8},{8,0},{1,9},{9,1},{2,10},{10,2},{3,11},{11,3},{4,12},{12,4},... | collective-permute-start | bytes 884744 | tf_op jit(solution)/shard_map/ppermute | solution.py:286
  51.7 2.7 %collective-permute-start.16 = (bf16[144,3584]{1,0:T(8,128)(2,1)S(1)}, bf16[144,3584]{1,0:T(8,128)(2,1)S(1)}, u32[]{:S(2)}, u32[]{:S(2)}) collective-permute-start(bf16[144,3584]{1,0:T(8,128)(2,1)S(1)} %get-tuple-element.40), channel_id=1, source_target_pairs={{0,8},{8,0},{1,9},{9,1},{2,10},{10,2},{3,11},{11,3},{4,12},{12,4},... | collective-permute-start | bytes 3096584 | tf_op jit(solution)/shard_map/ppermute | solution.py:286
  52.0 9.2 %collective-permute-start.22 = (bf16[48,3072]{1,0:T(8,128)(2,1)S(1)}, bf16[48,3072]{1,0:T(8,128)(2,1)S(1)}, u32[]{:S(2)}, u32[]{:S(2)}) collective-permute-start(bf16[48,3072]{1,0:T(8,128)(2,1)S(1)} %add_convert_fusion), channel_id=1, source_target_pairs={{0,1},{1,0},{2,3},{3,2},{4,5},{5,4},{6,7},{7,6},{8,9},{9,8},{10,11... | collective-permute-start | bytes 884744 | tf_op jit(solution)/shard_map/ppermute | solution.py:290
  54.8 3.0 %collective-permute-start.18 = (bf16[48,512]{1,0:T(8,128)(2,1)S(1)}, bf16[48,512]{1,0:T(8,128)(2,1)S(1)}, u32[]{:S(2)}, u32[]{:S(2)}) collective-permute-start(bf16[48,512]{1,0:T(8,128)(2,1)S(1)} %get-tuple-element.43), channel_id=1, source_target_pairs={{0,8},{8,0},{1,9},{9,1},{2,10},{10,2},{3,11},{11,3},{4,12},{12,4},... | collective-permute-start | bytes 147464 | tf_op jit(solution)/shard_map/ppermute | solution.py:286
  55.1 15.5 %collective-permute-start.17 = (bf16[48,3584]{1,0:T(8,128)(2,1)S(1)}, bf16[48,3584]{1,0:T(8,128)(2,1)S(1)}, u32[]{:S(2)}, u32[]{:S(2)}) collective-permute-start(bf16[48,3584]{1,0:T(8,128)(2,1)S(1)} %pad_maximum_fusion), channel_id=1, source_target_pairs={{0,2},{1,3},{2,0},{3,1},{4,6},{5,7},{6,4},{7,5},{8,10},{9,11},{10,... | collective-permute-start | bytes 1032200 | tf_op jit(solution)/shard_map/ppermute | solution.py:290
  57.8 10.8 %collective-permute-start.20 = (bf16[48,512]{1,0:T(8,128)(2,1)S(1)}, bf16[48,512]{1,0:T(8,128)(2,1)S(1)}, u32[]{:S(2)}, u32[]{:S(2)}) collective-permute-start(bf16[48,512]{1,0:T(8,128)(2,1)S(1)} %pad_maximum_fusion.3), channel_id=1, source_target_pairs={{0,6},{1,7},{2,4},{3,5},{4,2},{5,3},{6,0},{7,1},{8,14},{9,15},{10,... | collective-permute-start | bytes 147464 | tf_op jit(solution)/shard_map/ppermute | solution.py:290
  59.7 8.9 %collective-permute-start.19 = (bf16[48,512]{1,0:T(8,128)(2,1)S(1)}, bf16[48,512]{1,0:T(8,128)(2,1)S(1)}, u32[]{:S(2)}, u32[]{:S(2)}) collective-permute-start(bf16[48,512]{1,0:T(8,128)(2,1)S(1)} %pad_maximum_fusion.2), channel_id=1, source_target_pairs={{0,4},{1,5},{2,6},{3,7},{4,0},{5,1},{6,2},{7,3},{8,12},{9,13},{10,... | collective-permute-start | bytes 147464 | tf_op jit(solution)/shard_map/ppermute | solution.py:290
  61.2 16.2 %collective-permute-start.23 = (bf16[24,3072]{1,0:T(8,128)(2,1)S(1)}, bf16[24,3072]{1,0:T(8,128)(2,1)S(1)}, u32[]{:S(2)}, u32[]{:S(2)}) collective-permute-start(bf16[24,3072]{1,0:T(8,128)(2,1)S(1)} %get-tuple-element.47), channel_id=1, source_target_pairs={{0,4},{1,5},{2,6},{3,7},{4,0},{5,1},{6,2},{7,3},{8,12},{9,13},{10,... | collective-permute-start | bytes 442376 | tf_op jit(solution)/shard_map/ppermute | solution.py:290
  62.9 14.5 %collective-permute-start.24 = (bf16[24,3072]{1,0:T(8,128)(2,1)S(1)}, bf16[24,3072]{1,0:T(8,128)(2,1)S(1)}, u32[]{:S(2)}, u32[]{:S(2)}) collective-permute-start(bf16[24,3072]{1,0:T(8,128)(2,1)S(1)} %get-tuple-element.48), channel_id=1, source_target_pairs={{0,6},{1,7},{2,4},{3,5},{4,2},{5,3},{6,0},{7,1},{8,14},{9,15},{10,... | collective-permute-start | bytes 442376 | tf_op jit(solution)/shard_map/ppermute | solution.py:290
  70.7 6.8 %collective-permute-start.21 = (bf16[24,3584]{1,0:T(8,128)(2,1)S(1)}, bf16[24,3584]{1,0:T(8,128)(2,1)S(1)}, u32[]{:S(2)}, u32[]{:S(2)}) collective-permute-start(bf16[24,3584]{1,0:T(8,128)(2,1)S(1)} %pad_maximum_fusion.1), channel_id=1, source_target_pairs={{0,1},{1,0},{2,3},{3,2},{4,5},{5,4},{6,7},{7,6},{8,9},{9,8},{10,11... | collective-permute-start | bytes 516104 | tf_op jit(solution)/shard_map/ppermute | solution.py:290

commit v5 on v4

--- a/solution.py
+++ b/solution.py
@@ -315,10 +315,11 @@
     )
     own, inner_index = tie(own, inner_index)
     z1, y0, z2 = swap_inner(own, 2), swap_inner(own, 1), swap_inner(own, 4)
-    w_gate = load(w_gate)
-    own, z1, z2, y0, w_gate = tie(own, z1, z2, y0, w_gate)
-    z3, y1, y2 = swap_inner(own, 6), swap_inner(z1, 1), swap_inner(z2, 1)
-    y3 = swap_inner(z3, 1)
+    again, z1, y0, source = tie(own, z1, y0, w_gate)
+    z3, y1 = swap_inner(again, 6), swap_inner(z1, 1)
+    w_gate = load(source)
+    z2, w_gate = tie(z2, w_gate)
+    y2, y3 = swap_inner(z2, 1), swap_inner(z3, 1)
     near = [own, z1, z2, z3]
     near += [swap_core(block) for block in near]
     hidden, w_up = near_rows(near, w_gate, w_up, inner_index, experts)
@@ -333,18 +334,16 @@
     half = 4 * count
     middle = half + 2 * count
     high_a = (wide(own[middle:, :cut]) + wide(swap_core(high_a))).astype(jnp.bfloat16)
-    high_a, other = tie(high_a, other)
     across = swap_inner(high_a, 1)
     other = wide(own[:middle]) + wide(swap_core(other))
+    high_b = wide(own[middle:, cut:]) + wide(swap_core(high_b))
     near, low = other[:half].reshape(4, count, model_width), other[half:]
+    high_b = high_b.reshape(2, count, -1)
 
     def together(near_rows, far_rows):
         return jnp.concatenate([near_rows, far_rows]).astype(jnp.bfloat16)
 
-    first, high_b = tie(together(near[1], low[count:]), high_b)
-    one = swap_inner(first, 2)
-    high_b = wide(own[middle:, cut:]) + wide(swap_core(high_b))
-    high_b = high_b.reshape(2, count, -1)
+    one = swap_inner(together(near[1], low[count:]), 2)
     two, three = (
         swap_inner(together(near[2 + i][:, cut:], high_b[i]), 4 + 2 * i) for i in (0, 1)
     )

time: 78.6 us -> 77.4 us (0.985)
  waiting for transfers between devices: 22.8 us -> 21.5 us
    ppermute x11, waiting for transfers between devices: 3.76 us -> 2.21 us  [swap_core(): return lax.ppermute(value, 'outer', [(0, 1), (1, 0)])]
  transfers between devices with their start and end apart: 25 -> 25, of which waited for: 13 -> 11; matrix products, arithmetic and copies ran while one was open for 1% -> 1% of each run, Pallas kernels for 16% -> 16%
where the time goes in v5:
time: 77.4 us; the launch traced here: 77.2 us
  Pallas kernels  28.1 us (36%)
  starting transfers between devices  26.1 us (34%)
  waiting for transfers between devices  21.5 us (28%)
  other arithmetic  1.34 us (2%)
    ppermute x14, starting transfers between devices, swap_inner(): return lax.ppermute(value, 'inner', [(i, i ^ bit) for i in range(8)])  23.5 us
    ppermute x14, waiting for transfers between devices, swap_inner(): return lax.ppermute(value, 'inner', [(i, i ^ bit) for i in range(8)])  19.3 us
    pallas_call x1, Pallas kernels, far_rows(): pl.pallas_call(functools.partial(far_kernel, experts, len(blocks), cut),...  14.5 us
    pallas_call x1, Pallas kernels, near_rows(): pl.pallas_call(functools.partial(near_kernel, experts, len(blocks)), in_s...  7.36 us
    pallas_call x1, Pallas kernels, load(): pl.pallas_call(load_kernel, in_specs=[pl.BlockSpec(memory_space=pltpu.HBM...  5.18 us
    ppermute x11, starting transfers between devices, swap_core(): return lax.ppermute(value, 'outer', [(0, 1), (1, 0)])  2.57 us
    ppermute x11, waiting for transfers between devices, swap_core(): return lax.ppermute(value, 'outer', [(0, 1), (1, 0)])  2.21 us
  transfers between devices with their start and end apart: 25, of which 11 were waited for; matrix products, arithmetic and copies ran while one was open for 1% of the time, Pallas kernels for 16%

profile of v5, /device:TPU:0, one launch (start us, length us, event | category | flops | bytes accessed | tf_op | source)
XLA Modules:
  0.0 77.2 jit_solution(13867840756573432511)
XLA Ops:
  0.0 1.0 %with_routing.1.refs_0_ = bf16[24,3712]{1,0:T(8,128)(2,1)S(1)} custom-call(bf16[24,3584]{1,0:T(8,128)(2,1)} %rows_hbm.1, s32[8,24]{1,0:T(8,128)} %bitcast.3, f32[8,24]{1,0:T(8,128)} %bitcast.4), custom_call_target="tpu_custom_call" | custom-call | tf_op jit(solution)/shard_map/with_routing/pallas_call | solution.py:56
  1.0 3.0 %collective-permute-start.1 = (bf16[24,3712]{1,0:T(8,128)(2,1)S(1)}, bf16[24,3712]{1,0:T(8,128)(2,1)S(1)}, u32[]{:S(2)}, u32[]{:S(2)}) collective-permute-start(bf16[24,3712]{1,0:T(8,128)(2,1)S(1)} %with_routing.1.refs_0_), channel_id=1, source_target_pairs={{0,1},{1,0},{2,3},{3,2},{4,5},{5,4},{6,7},{7,6},{8,9},{9,8},{10,11... | collective-permute-start | bytes 534536 | tf_op jit(solution)/shard_map/ppermute | solution.py:290
  4.0 1.6 %collective-permute-start = (bf16[24,3712]{1,0:T(8,128)(2,1)S(1)}, bf16[24,3712]{1,0:T(8,128)(2,1)S(1)}, u32[]{:S(2)}, u32[]{:S(2)}) collective-permute-start(bf16[24,3712]{1,0:T(8,128)(2,1)S(1)} %with_routing.1.refs_0_), channel_id=1, source_target_pairs={{0,2},{1,3},{2,0},{3,1},{4,6},{5,7},{6,4},{7,5},{8,10},{9,11},{10,... | collective-permute-start | bytes 534536 | tf_op jit(solution)/shard_map/ppermute | solution.py:290
  5.6 2.6 %collective-permute-start.3 = (bf16[24,3712]{1,0:T(8,128)(2,1)S(1)}, bf16[24,3712]{1,0:T(8,128)(2,1)S(1)}, u32[]{:S(2)}, u32[]{:S(2)}) collective-permute-start(bf16[24,3712]{1,0:T(8,128)(2,1)S(1)} %with_routing.1.refs_0_), channel_id=1, source_target_pairs={{0,4},{1,5},{2,6},{3,7},{4,0},{5,1},{6,2},{7,3},{8,12},{9,13},{10,... | collective-permute-start | bytes 534536 | tf_op jit(solution)/shard_map/ppermute | solution.py:290
  8.2 0.3 collective-permute-done.1.refs_0_
  8.5 5.1 %collective-permute-done.refs_1_ = bf16[24,3712]{1,0:T(8,128)(2,1)S(1)} collective-permute-done((bf16[24,3712]{1,0:T(8,128)(2,1)S(1)}, bf16[24,3712]{1,0:T(8,128)(2,1)S(1)}, u32[]{:S(2)}, u32[]{:S(2)}) %collective-permute-start) | collective-permute-done | bytes 178208 | tf_op jit(solution)/shard_map/ppermute | solution.py:290
  13.7 2.5 %collective-permute-start.4 = (bf16[24,3712]{1,0:T(8,128)(2,1)S(1)}, bf16[24,3712]{1,0:T(8,128)(2,1)S(1)}, u32[]{:S(2)}, u32[]{:S(2)}) collective-permute-start(bf16[24,3712]{1,0:T(8,128)(2,1)S(1)} %with_routing.1.refs_0_), channel_id=1, source_target_pairs={{0,6},{1,7},{2,4},{3,5},{4,2},{5,3},{6,0},{7,1},{8,14},{9,15},{10,... | collective-permute-start | bytes 534536 | tf_op jit(solution)/shard_map/ppermute | solution.py:290
  16.2 0.0 collective-permute-start.5
  16.2 0.5 collective-permute-start.6
  16.7 0.5 collective-permute-start.2
  17.2 5.2 %load.1.refs_8_ = bf16[4,3584,512]{2,1,0:T(8,128)(2,1)S(1)} custom-call(bf16[4,3584,512]{2,1,0:T(8,128)(2,1)} %source_ref), custom_call_target="tpu_custom_call" | custom-call | bytes 29360128 | tf_op jit(solution)/shard_map/load/pallas_call | solution.py:134
  22.4 0.1 collective-permute-start.7
  22.5 0.0 collective-permute-done.4.refs_3_
  22.5 0.5 collective-permute-start.8
  23.0 1.5 %collective-permute-start.9 = (bf16[24,3712]{1,0:T(8,128)(2,1)S(1)}, bf16[24,3712]{1,0:T(8,128)(2,1)S(1)}, u32[]{:S(2)}, u32[]{:S(2)}) collective-permute-start(bf16[24,3712]{1,0:T(8,128)(2,1)S(1)} %collective-permute-done.3.refs_2_), channel_id=1, source_target_pairs={{0,1},{1,0},{2,3},{3,2},{4,5},{5,4},{6,7},{7,6},{8,9},{9,8},{10,11... | collective-permute-start | bytes 534536 | tf_op jit(solution)/shard_map/ppermute | solution.py:290
  24.5 0.0 collective-permute-done.6.refs_5_
  24.5 0.0 collective-permute-start.11
  24.5 0.6 collective-permute-start.10
  25.1 0.2 collective-permute-start.12
  25.3 0.0 collective-permute-done.8.refs_7_
  25.3 7.4 %near_rows.1 = (bf16[192,2048]{1,0:T(8,128)(2,1)S(1)}, bf16[4,3584,512]{2,1,0:T(8,128)(2,1)S(1)}) custom-call(s32[1]{0:T(128)} %bitcast.2.index_ref, bf16[24,3712]{1,0:T(8,128)(2,1)S(1)} %with_routing.1.refs_0_, bf16[24,3712]{1,0:T(8,128)(2,1)S(1)} %collective-permute-done.refs_1_, bf16[24,3712]{1,0:T(8,128)(2,1)S(1)} %collective-permute-done.3.refs_2_, ...), custom_call_target="tpu_custom_call" | custom-call | flops 5637144576 | tf_op jit(solution)/shard_map/near_rows/pallas_call | solution.py:186
  32.6 0.0 collective-permute-done.9.refs_2_
  32.6 0.7 collective-permute-done.10.refs_3_
  33.3 0.5 collective-permute-start.14
  33.8 0.0 collective-permute-done.11.refs_4_
  33.8 0.9 %collective-permute-done.13.refs_6_ = bf16[24,3712]{1,0:T(8,128)(2,1)S(1)} collective-permute-done((bf16[24,3712]{1,0:T(8,128)(2,1)S(1)}, bf16[24,3712]{1,0:T(8,128)(2,1)S(1)}, u32[]{:S(2)}, u32[]{:S(2)}) %collective-permute-start.13) | collective-permute-done | bytes 178208 | tf_op jit(solution)/shard_map/ppermute | solution.py:286
  34.7 0.3 collective-permute-done.14.refs_7_
  35.0 14.5 %far_rows.1 = (bf16[192,3584]{1,0:T(8,128)(2,1)S(1)}, bf16[144,3584]{1,0:T(8,128)(2,1)S(1)}, bf16[48,3072]{1,0:T(8,128)(2,1)S(1)}, bf16[48,512]{1,0:T(8,128)(2,1)S(1)}) custom-call(s32[1]{0:T(128)} %bitcast.2.index_ref, bf16[24,3712]{1,0:T(8,128)(2,1)S(1)} %collective-permute-done.1.refs_0_, bf16[24,3712]{1,0:T(8,128)(2,1)S(1)} %collective-permute-done.2.refs_1_, ...), custom_call_target="tpu_custom_call" | custom-call | tf_op jit(solution)/shard_map/far_rows/pallas_call | solution.py:261
  49.5 0.3 collective-permute-start.17
  49.8 0.3 collective-permute-start.21
  50.1 0.3 collective-permute-start.15
  50.3 0.5 collective-permute-done.17
  50.8 0.6 collective-permute-done.21
  51.4 0.1 add_convert_fusion
  51.5 1.6 %collective-permute-start.22 = (bf16[48,3072]{1,0:T(8,128)(2,1)S(1)}, bf16[48,3072]{1,0:T(8,128)(2,1)S(1)}, u32[]{:S(2)}, u32[]{:S(2)}) collective-permute-start(bf16[48,3072]{1,0:T(8,128)(2,1)S(1)} %add_convert_fusion), channel_id=1, source_target_pairs={{0,1},{1,0},{2,3},{3,2},{4,5},{5,4},{6,7},{7,6},{8,9},{9,8},{10,11... | collective-permute-start | bytes 884744 | tf_op jit(solution)/shard_map/ppermute | solution.py:290
  53.1 0.3 fusion.6
  53.5 1.4 %collective-permute-start.19 = (bf16[48,512]{1,0:T(8,128)(2,1)S(1)}, bf16[48,512]{1,0:T(8,128)(2,1)S(1)}, u32[]{:S(2)}, u32[]{:S(2)}) collective-permute-start(bf16[48,512]{1,0:T(8,128)(2,1)S(1)} %pad_maximum_fusion.3), channel_id=1, source_target_pairs={{0,6},{1,7},{2,4},{3,5},{4,2},{5,3},{6,0},{7,1},{8,14},{9,15},{10,... | collective-permute-start | bytes 147464 | tf_op jit(solution)/shard_map/ppermute | solution.py:290
  54.8 1.7 %collective-permute-start.18 = (bf16[48,512]{1,0:T(8,128)(2,1)S(1)}, bf16[48,512]{1,0:T(8,128)(2,1)S(1)}, u32[]{:S(2)}, u32[]{:S(2)}) collective-permute-start(bf16[48,512]{1,0:T(8,128)(2,1)S(1)} %pad_maximum_fusion.2), channel_id=1, source_target_pairs={{0,4},{1,5},{2,6},{3,7},{4,0},{5,1},{6,2},{7,3},{8,12},{9,13},{10,... | collective-permute-start | bytes 147464 | tf_op jit(solution)/shard_map/ppermute | solution.py:290
  56.5 1.5 %collective-permute-start.16 = (bf16[48,3584]{1,0:T(8,128)(2,1)S(1)}, bf16[48,3584]{1,0:T(8,128)(2,1)S(1)}, u32[]{:S(2)}, u32[]{:S(2)}) collective-permute-start(bf16[48,3584]{1,0:T(8,128)(2,1)S(1)} %pad_maximum_fusion), channel_id=1, source_target_pairs={{0,2},{1,3},{2,0},{3,1},{4,6},{5,7},{6,4},{7,5},{8,10},{9,11},{10,... | collective-permute-start | bytes 1032200 | tf_op jit(solution)/shard_map/ppermute | solution.py:290
  58.0 2.7 %collective-permute-done.22 = bf16[48,3072]{1,0:T(8,128)(2,1)S(1)} collective-permute-done((bf16[48,3072]{1,0:T(8,128)(2,1)S(1)}, bf16[48,3072]{1,0:T(8,128)(2,1)S(1)}, u32[]{:S(2)}, u32[]{:S(2)}) %collective-permute-start.22) | collective-permute-done | bytes 294944 | tf_op jit(solution)/shard_map/ppermute | solution.py:290
  60.7 0.1 fusion.4
  60.8 2.8 %collective-permute-start.23 = (bf16[24,3072]{1,0:T(8,128)(2,1)S(1)}, bf16[24,3072]{1,0:T(8,128)(2,1)S(1)}, u32[]{:S(2)}, u32[]{:S(2)}) collective-permute-start(bf16[24,3072]{1,0:T(8,128)(2,1)S(1)} %get-tuple-element.41), channel_id=1, source_target_pairs={{0,4},{1,5},{2,6},{3,7},{4,0},{5,1},{6,2},{7,3},{8,12},{9,13},{10,... | collective-permute-start | bytes 442376 | tf_op jit(solution)/shard_map/ppermute | solution.py:290
  63.6 1.4 %collective-permute-start.24 = (bf16[24,3072]{1,0:T(8,128)(2,1)S(1)}, bf16[24,3072]{1,0:T(8,128)(2,1)S(1)}, u32[]{:S(2)}, u32[]{:S(2)}) collective-permute-start(bf16[24,3072]{1,0:T(8,128)(2,1)S(1)} %get-tuple-element.42), channel_id=1, source_target_pairs={{0,6},{1,7},{2,4},{3,5},{4,2},{5,3},{6,0},{7,1},{8,14},{9,15},{10,... | collective-permute-start | bytes 442376 | tf_op jit(solution)/shard_map/ppermute | solution.py:290
  64.9 6.0 %collective-permute-done.16 = bf16[48,3584]{1,0:T(8,128)(2,1)S(1)} collective-permute-done((bf16[48,3584]{1,0:T(8,128)(2,1)S(1)}, bf16[48,3584]{1,0:T(8,128)(2,1)S(1)}, u32[]{:S(2)}, u32[]{:S(2)}) %collective-permute-start.16) | collective-permute-done | bytes 344096 | tf_op jit(solution)/shard_map/ppermute | solution.py:290
  71.0 0.9 %collective-permute-start.20 = (bf16[24,3584]{1,0:T(8,128)(2,1)S(1)}, bf16[24,3584]{1,0:T(8,128)(2,1)S(1)}, u32[]{:S(2)}, u32[]{:S(2)}) collective-permute-start(bf16[24,3584]{1,0:T(8,128)(2,1)S(1)} %pad_maximum_fusion.1), channel_id=1, source_target_pairs={{0,1},{1,0},{2,3},{3,2},{4,5},{5,4},{6,7},{7,6},{8,9},{9,8},{10,11... | collective-permute-start | bytes 516104 | tf_op jit(solution)/shard_map/ppermute | solution.py:290
  72.0 2.9 %collective-permute-done.23 = bf16[24,3072]{1,0:T(8,128)(2,1)S(1)} collective-permute-done((bf16[24,3072]{1,0:T(8,128)(2,1)S(1)}, bf16[24,3072]{1,0:T(8,128)(2,1)S(1)}, u32[]{:S(2)}, u32[]{:S(2)}) %collective-permute-start.23) | collective-permute-done | bytes 147488 | tf_op jit(solution)/shard_map/ppermute | solution.py:290
  74.9 1.6 %collective-permute-done.20 = bf16[24,3584]{1,0:T(8,128)(2,1)S(1)} collective-permute-done((bf16[24,3584]{1,0:T(8,128)(2,1)S(1)}, bf16[24,3584]{1,0:T(8,128)(2,1)S(1)}, u32[]{:S(2)}, u32[]{:S(2)}) %collective-permute-start.20) | collective-permute-done | bytes 172064 | tf_op jit(solution)/shard_map/ppermute | solution.py:290
  76.5 0.7 fusion.2
  (23 shorter events, 0.2 us)
Async XLA Ops:
  1.0 7.5 %collective-permute-start.1 = (bf16[24,3712]{1,0:T(8,128)(2,1)S(1)}, bf16[24,3712]{1,0:T(8,128)(2,1)S(1)}, u32[]{:S(2)}, u32[]{:S(2)}) collective-permute-start(bf16[24,3712]{1,0:T(8,128)(2,1)S(1)} %with_routing.1.refs_0_), channel_id=1, source_target_pairs={{0,1},{1,0},{2,3},{3,2},{4,5},{5,4},{6,7},{7,6},{8,9},{9,8},{10,11... | collective-permute-start | bytes 534536 | tf_op jit(solution)/shard_map/ppermute | solution.py:290
  4.0 9.6 %collective-permute-start = (bf16[24,3712]{1,0:T(8,128)(2,1)S(1)}, bf16[24,3712]{1,0:T(8,128)(2,1)S(1)}, u32[]{:S(2)}, u32[]{:S(2)}) collective-permute-start(bf16[24,3712]{1,0:T(8,128)(2,1)S(1)} %with_routing.1.refs_0_), channel_id=1, source_target_pairs={{0,2},{1,3},{2,0},{3,1},{4,6},{5,7},{6,4},{7,5},{8,10},{9,11},{10,... | collective-permute-start | bytes 534536 | tf_op jit(solution)/shard_map/ppermute | solution.py:290
  5.6 16.8 %collective-permute-start.3 = (bf16[24,3712]{1,0:T(8,128)(2,1)S(1)}, bf16[24,3712]{1,0:T(8,128)(2,1)S(1)}, u32[]{:S(2)}, u32[]{:S(2)}) collective-permute-start(bf16[24,3712]{1,0:T(8,128)(2,1)S(1)} %with_routing.1.refs_0_), channel_id=1, source_target_pairs={{0,4},{1,5},{2,6},{3,7},{4,0},{5,1},{6,2},{7,3},{8,12},{9,13},{10,... | collective-permute-start | bytes 534536 | tf_op jit(solution)/shard_map/ppermute | solution.py:290
  13.7 8.8 %collective-permute-start.4 = (bf16[24,3712]{1,0:T(8,128)(2,1)S(1)}, bf16[24,3712]{1,0:T(8,128)(2,1)S(1)}, u32[]{:S(2)}, u32[]{:S(2)}) collective-permute-start(bf16[24,3712]{1,0:T(8,128)(2,1)S(1)} %with_routing.1.refs_0_), channel_id=1, source_target_pairs={{0,6},{1,7},{2,4},{3,5},{4,2},{5,3},{6,0},{7,1},{8,14},{9,15},{10,... | collective-permute-start | bytes 534536 | tf_op jit(solution)/shard_map/ppermute | solution.py:290
  16.2 6.8 %collective-permute-start.5 = (bf16[24,3712]{1,0:T(8,128)(2,1)S(1)}, bf16[24,3712]{1,0:T(8,128)(2,1)S(1)}, u32[]{:S(2)}, u32[]{:S(2)}) collective-permute-start(bf16[24,3712]{1,0:T(8,128)(2,1)S(1)} %with_routing.1.refs_0_), channel_id=1, source_target_pairs={{0,8},{8,0},{1,9},{9,1},{2,10},{10,2},{3,11},{11,3},{4,12},{12,4},... | collective-permute-start | bytes 534536 | tf_op jit(solution)/shard_map/ppermute | solution.py:286
  16.2 8.3 %collective-permute-start.6 = (bf16[24,3712]{1,0:T(8,128)(2,1)S(1)}, bf16[24,3712]{1,0:T(8,128)(2,1)S(1)}, u32[]{:S(2)}, u32[]{:S(2)}) collective-permute-start(bf16[24,3712]{1,0:T(8,128)(2,1)S(1)} %collective-permute-done.refs_1_), channel_id=1, source_target_pairs={{0,8},{8,0},{1,9},{9,1},{2,10},{10,2},{3,11},{11,3},{4,12},{12,4},... | collective-permute-start | bytes 534536 | tf_op jit(solution)/shard_map/ppermute | solution.py:286
  16.7 7.8 %collective-permute-start.2 = (bf16[24,3712]{1,0:T(8,128)(2,1)S(1)}, bf16[24,3712]{1,0:T(8,128)(2,1)S(1)}, u32[]{:S(2)}, u32[]{:S(2)}) collective-permute-start(bf16[24,3712]{1,0:T(8,128)(2,1)S(1)} %collective-permute-done.refs_1_), channel_id=1, source_target_pairs={{0,1},{1,0},{2,3},{3,2},{4,5},{5,4},{6,7},{7,6},{8,9},{9,8},{10,11... | collective-permute-start | bytes 534536 | tf_op jit(solution)/shard_map/ppermute | solution.py:290
  22.4 2.7 %collective-permute-start.7 = (bf16[24,3712]{1,0:T(8,128)(2,1)S(1)}, bf16[24,3712]{1,0:T(8,128)(2,1)S(1)}, u32[]{:S(2)}, u32[]{:S(2)}) collective-permute-start(bf16[24,3712]{1,0:T(8,128)(2,1)S(1)} %collective-permute-done.3.refs_2_), channel_id=1, source_target_pairs={{0,8},{8,0},{1,9},{9,1},{2,10},{10,2},{3,11},{11,3},{4,12},{12,4},... | collective-permute-start | bytes 534536 | tf_op jit(solution)/shard_map/ppermute | solution.py:286
  22.5 2.8 %collective-permute-start.8 = (bf16[24,3712]{1,0:T(8,128)(2,1)S(1)}, bf16[24,3712]{1,0:T(8,128)(2,1)S(1)}, u32[]{:S(2)}, u32[]{:S(2)}) collective-permute-start(bf16[24,3712]{1,0:T(8,128)(2,1)S(1)} %collective-permute-done.4.refs_3_), channel_id=1, source_target_pairs={{0,8},{8,0},{1,9},{9,1},{2,10},{10,2},{3,11},{11,3},{4,12},{12,4},... | collective-permute-start | bytes 534536 | tf_op jit(solution)/shard_map/ppermute | solution.py:286
  23.0 9.6 %collective-permute-start.9 = (bf16[24,3712]{1,0:T(8,128)(2,1)S(1)}, bf16[24,3712]{1,0:T(8,128)(2,1)S(1)}, u32[]{:S(2)}, u32[]{:S(2)}) collective-permute-start(bf16[24,3712]{1,0:T(8,128)(2,1)S(1)} %collective-permute-done.3.refs_2_), channel_id=1, source_target_pairs={{0,1},{1,0},{2,3},{3,2},{4,5},{5,4},{6,7},{7,6},{8,9},{9,8},{10,11... | collective-permute-start | bytes 534536 | tf_op jit(solution)/shard_map/ppermute | solution.py:290
  24.5 9.3 %collective-permute-start.11 = (bf16[24,3712]{1,0:T(8,128)(2,1)S(1)}, bf16[24,3712]{1,0:T(8,128)(2,1)S(1)}, u32[]{:S(2)}, u32[]{:S(2)}) collective-permute-start(bf16[24,3712]{1,0:T(8,128)(2,1)S(1)} %collective-permute-done.1.refs_0_), channel_id=1, source_target_pairs={{0,8},{8,0},{1,9},{9,1},{2,10},{10,2},{3,11},{11,3},{4,12},{12,4},... | collective-permute-start | bytes 534536 | tf_op jit(solution)/shard_map/ppermute | solution.py:286
  24.5 8.8 %collective-permute-start.10 = (bf16[24,3712]{1,0:T(8,128)(2,1)S(1)}, bf16[24,3712]{1,0:T(8,128)(2,1)S(1)}, u32[]{:S(2)}, u32[]{:S(2)}) collective-permute-start(bf16[24,3712]{1,0:T(8,128)(2,1)S(1)} %collective-permute-done.4.refs_3_), channel_id=1, source_target_pairs={{0,1},{1,0},{2,3},{3,2},{4,5},{5,4},{6,7},{7,6},{8,9},{9,8},{10,11... | collective-permute-start | bytes 534536 | tf_op jit(solution)/shard_map/ppermute | solution.py:290
  25.1 8.7 %collective-permute-start.12 = (bf16[24,3712]{1,0:T(8,128)(2,1)S(1)}, bf16[24,3712]{1,0:T(8,128)(2,1)S(1)}, u32[]{:S(2)}, u32[]{:S(2)}) collective-permute-start(bf16[24,3712]{1,0:T(8,128)(2,1)S(1)} %collective-permute-done.2.refs_1_), channel_id=1, source_target_pairs={{0,8},{8,0},{1,9},{9,1},{2,10},{10,2},{3,11},{11,3},{4,12},{12,4},... | collective-permute-start | bytes 534536 | tf_op jit(solution)/shard_map/ppermute | solution.py:286
  33.3 1.4 %collective-permute-start.13 = (bf16[24,3712]{1,0:T(8,128)(2,1)S(1)}, bf16[24,3712]{1,0:T(8,128)(2,1)S(1)}, u32[]{:S(2)}, u32[]{:S(2)}) collective-permute-start(bf16[24,3712]{1,0:T(8,128)(2,1)S(1)} %collective-permute-done.9.refs_2_), channel_id=1, source_target_pairs={{0,8},{8,0},{1,9},{9,1},{2,10},{10,2},{3,11},{11,3},{4,12},{12,4},... | collective-permute-start | bytes 534536 | tf_op jit(solution)/shard_map/ppermute | solution.py:286
  33.3 1.7 %collective-permute-start.14 = (bf16[24,3712]{1,0:T(8,128)(2,1)S(1)}, bf16[24,3712]{1,0:T(8,128)(2,1)S(1)}, u32[]{:S(2)}, u32[]{:S(2)}) collective-permute-start(bf16[24,3712]{1,0:T(8,128)(2,1)S(1)} %collective-permute-done.10.refs_3_), channel_id=1, source_target_pairs={{0,8},{8,0},{1,9},{9,1},{2,10},{10,2},{3,11},{11,3},{4,12},{12,4},... | collective-permute-start | bytes 534536 | tf_op jit(solution)/shard_map/ppermute | solution.py:286
  49.5 1.3 %collective-permute-start.17 = (bf16[48,512]{1,0:T(8,128)(2,1)S(1)}, bf16[48,512]{1,0:T(8,128)(2,1)S(1)}, u32[]{:S(2)}, u32[]{:S(2)}) collective-permute-start(bf16[48,512]{1,0:T(8,128)(2,1)S(1)} %get-tuple-element.37), channel_id=1, source_target_pairs={{0,8},{8,0},{1,9},{9,1},{2,10},{10,2},{3,11},{11,3},{4,12},{12,4},... | collective-permute-start | bytes 147464 | tf_op jit(solution)/shard_map/ppermute | solution.py:286
  49.8 1.6 %collective-permute-start.21 = (bf16[48,3072]{1,0:T(8,128)(2,1)S(1)}, bf16[48,3072]{1,0:T(8,128)(2,1)S(1)}, u32[]{:S(2)}, u32[]{:S(2)}) collective-permute-start(bf16[48,3072]{1,0:T(8,128)(2,1)S(1)} %get-tuple-element.38), channel_id=1, source_target_pairs={{0,8},{8,0},{1,9},{9,1},{2,10},{10,2},{3,11},{11,3},{4,12},{12,4},... | collective-permute-start | bytes 884744 | tf_op jit(solution)/shard_map/ppermute | solution.py:286
  50.1 3.0 %collective-permute-start.15 = (bf16[144,3584]{1,0:T(8,128)(2,1)S(1)}, bf16[144,3584]{1,0:T(8,128)(2,1)S(1)}, u32[]{:S(2)}, u32[]{:S(2)}) collective-permute-start(bf16[144,3584]{1,0:T(8,128)(2,1)S(1)} %get-tuple-element.36), channel_id=1, source_target_pairs={{0,8},{8,0},{1,9},{9,1},{2,10},{10,2},{3,11},{11,3},{4,12},{12,4},... | collective-permute-start | bytes 3096584 | tf_op jit(solution)/shard_map/ppermute | solution.py:286
  51.5 9.2 %collective-permute-start.22 = (bf16[48,3072]{1,0:T(8,128)(2,1)S(1)}, bf16[48,3072]{1,0:T(8,128)(2,1)S(1)}, u32[]{:S(2)}, u32[]{:S(2)}) collective-permute-start(bf16[48,3072]{1,0:T(8,128)(2,1)S(1)} %add_convert_fusion), channel_id=1, source_target_pairs={{0,1},{1,0},{2,3},{3,2},{4,5},{5,4},{6,7},{7,6},{8,9},{9,8},{10,11... | collective-permute-start | bytes 884744 | tf_op jit(solution)/shard_map/ppermute | solution.py:290
  53.5 11.5 %collective-permute-start.19 = (bf16[48,512]{1,0:T(8,128)(2,1)S(1)}, bf16[48,512]{1,0:T(8,128)(2,1)S(1)}, u32[]{:S(2)}, u32[]{:S(2)}) collective-permute-start(bf16[48,512]{1,0:T(8,128)(2,1)S(1)} %pad_maximum_fusion.3), channel_id=1, source_target_pairs={{0,6},{1,7},{2,4},{3,5},{4,2},{5,3},{6,0},{7,1},{8,14},{9,15},{10,... | collective-permute-start | bytes 147464 | tf_op jit(solution)/shard_map/ppermute | solution.py:290
  54.8 10.1 %collective-permute-start.18 = (bf16[48,512]{1,0:T(8,128)(2,1)S(1)}, bf16[48,512]{1,0:T(8,128)(2,1)S(1)}, u32[]{:S(2)}, u32[]{:S(2)}) collective-permute-start(bf16[48,512]{1,0:T(8,128)(2,1)S(1)} %pad_maximum_fusion.2), channel_id=1, source_target_pairs={{0,4},{1,5},{2,6},{3,7},{4,0},{5,1},{6,2},{7,3},{8,12},{9,13},{10,... | collective-permute-start | bytes 147464 | tf_op jit(solution)/shard_map/ppermute | solution.py:290
  56.5 14.4 %collective-permute-start.16 = (bf16[48,3584]{1,0:T(8,128)(2,1)S(1)}, bf16[48,3584]{1,0:T(8,128)(2,1)S(1)}, u32[]{:S(2)}, u32[]{:S(2)}) collective-permute-start(bf16[48,3584]{1,0:T(8,128)(2,1)S(1)} %pad_maximum_fusion), channel_id=1, source_target_pairs={{0,2},{1,3},{2,0},{3,1},{4,6},{5,7},{6,4},{7,5},{8,10},{9,11},{10,... | collective-permute-start | bytes 1032200 | tf_op jit(solution)/shard_map/ppermute | solution.py:290
  60.8 14.1 %collective-permute-start.23 = (bf16[24,3072]{1,0:T(8,128)(2,1)S(1)}, bf16[24,3072]{1,0:T(8,128)(2,1)S(1)}, u32[]{:S(2)}, u32[]{:S(2)}) collective-permute-start(bf16[24,3072]{1,0:T(8,128)(2,1)S(1)} %get-tuple-element.41), channel_id=1, source_target_pairs={{0,4},{1,5},{2,6},{3,7},{4,0},{5,1},{6,2},{7,3},{8,12},{9,13},{10,... | collective-permute-start | bytes 442376 | tf_op jit(solution)/shard_map/ppermute | solution.py:290
  63.6 11.3 %collective-permute-start.24 = (bf16[24,3072]{1,0:T(8,128)(2,1)S(1)}, bf16[24,3072]{1,0:T(8,128)(2,1)S(1)}, u32[]{:S(2)}, u32[]{:S(2)}) collective-permute-start(bf16[24,3072]{1,0:T(8,128)(2,1)S(1)} %get-tuple-element.42), channel_id=1, source_target_pairs={{0,6},{1,7},{2,4},{3,5},{4,2},{5,3},{6,0},{7,1},{8,14},{9,15},{10,... | collective-permute-start | bytes 442376 | tf_op jit(solution)/shard_map/ppermute | solution.py:290
  71.0 5.5 %collective-permute-start.20 = (bf16[24,3584]{1,0:T(8,128)(2,1)S(1)}, bf16[24,3584]{1,0:T(8,128)(2,1)S(1)}, u32[]{:S(2)}, u32[]{:S(2)}) collective-permute-start(bf16[24,3584]{1,0:T(8,128)(2,1)S(1)} %pad_maximum_fusion.1), channel_id=1, source_target_pairs={{0,1},{1,0},{2,3},{3,2},{4,5},{5,4},{6,7},{7,6},{8,9},{9,8},{10,11... | collective-permute-start | bytes 516104 | tf_op jit(solution)/shard_map/ppermute | solution.py:290
